TPU v7x, 512 devices: a whole 4x8x8 slice. The times are simulated.
512 devices in a mesh: pts: 256 (over x, z, y), rhs: 2 (over core).
Axes of the slice: x: 4, y: 8, z: 8, core: 2. Of those that a mesh axis runs over, the one named last changes fastest.
Arguments:
- points: bfloat16 [524288, 64], P('pts'), may hold values from -6 to 6
- inputs: bfloat16 [524288, 128], P('pts', 'rhs'), may hold values from -6 to 6
- cotangent: bfloat16 [524288, 128], P('pts', 'rhs'), may hold values from -6 to 6
- order: int32 [524288], P('pts'), may hold values from 0 to 524287, as said below
- near_ids: int32 [2048, 12], P('pts'), may hold values from 0 to 2047, as said below
- near_valid: int32 [2048, 12], P('pts'), may hold values from 0 to 1, as said below
- leaf_basis: bfloat16 [2048, 256, 128], P('pts'), may hold values from -0.375 to 0.375
- local_transfer: bfloat16 [1792, 256, 128], P('pts'), may hold values from -0.375 to 0.375
- chain_transfer: bfloat16 [256, 4, 256, 128], P('pts'), as said below
- leaf_skel: bfloat16 [2048, 128, 64], P('pts'), may hold values from -4 to 4
- local_skel: bfloat16 [1792, 128, 64], P('pts'), may hold values from -4 to 4
- chain_skel: bfloat16 [256, 4, 2, 128, 64], P('pts'), may hold values from -4 to 4, as said below
- top_skel: bfloat16 [16, 128, 64], replicated, may hold values from -4 to 4
Outputs:
- output: bfloat16 [524288, 128], P('pts', 'rhs')
- basis_grad: bfloat16 [2048, 256, 128], P('pts', 'rhs')
Inputs may be any that keep to these rules, and one draw needn't show every extreme that they name: `order`: within each aligned block of 2048 rows, a permutation of that block's row indices. `near_ids`: each entry names a leaf of the same aligned block of 8 leaves or of one of the two blocks beside it; slot 0 is the leaf itself; the other slots of a row are distinct and name neither the leaf itself nor its tree sibling. `near_valid`: slot 0 is 1 for every leaf. `chain_transfer`: for each b, the same matrix in every row d with equal d >> (b + 1). chain_skel[d, b, m] equals the skeleton of the same node wherever that node appears, in local_skel and top_skel too.
All inputs are finite; a program needn't handle non-finite values.
Results may differ from a plain program's by a relative error of at most 0.0049.
Values may be sent and summed in bfloat16 or wider, within the bound.
No kernel may reach another device: no remote copies, remote signals or barrier semaphores. Data moves between devices by JAX's collectives and lax.ppermute only.
A program may use at most 64 MiB of HBM per device.

v0:
```python
import jax
import jax.numpy as jnp
from jax import lax
from jax.sharding import PartitionSpec as P

UP = 4


HIGHEST = lax.Precision.HIGHEST


def partner_2(value, axis, bit):
    mask = 2**bit
    pairs = [(source, source ^ mask) for source in range(lax.axis_size(axis))]
    return lax.ppermute(value, axis, pairs)


def with_halo(block, sides, width):
    for axis, dim in sides:
        count = lax.axis_size(axis)
        forward = [(i, i + 1) for i in range(count - 1)]
        backward = [(target, source) for source, target in forward]
        low = lax.ppermute(
            lax.slice_in_dim(block, block.shape[dim] - width, None, axis=dim), axis, forward
        )
        high = lax.ppermute(lax.slice_in_dim(block, 0, width, axis=dim), axis, backward)
        block = jnp.concatenate([low, block, high], axis=dim)
    return block


def kernel_block(left_pts, right_pts):
    left_wide = left_pts.astype(jnp.float32)
    right_wide = right_pts.astype(jnp.float32)
    inner_sum = jnp.einsum("nid,njd->nij", left_pts, right_pts, preferred_element_type=jnp.float32)
    distance = (
        jnp.sum(left_wide * left_wide, -1)[:, :, None]
        + jnp.sum(right_wide * right_wide, -1)[:, None, :]
        - 2.0 * inner_sum
    )
    return jnp.exp(distance * (-2.0 / left_pts.shape[-1]))


def sibling_terms(kernel, coeffs):
    even_term = jnp.einsum("nij,njc->nic", kernel, coeffs[1::2], precision=HIGHEST)
    odd_term = jnp.einsum("nji,njc->nic", kernel, coeffs[0::2], precision=HIGHEST)
    return jnp.stack([even_term, odd_term], 1).reshape(coeffs.shape)


def near_terms(own_leaves, blocks, leaf_ids, leaf_valid, dimension):

    def single(item_tuple):
        own_pts, slot_ids, slot_valid = item_tuple
        others = jnp.take(blocks, slot_ids, axis=0)
        other_pts = others[:, :, :dimension]
        other_vals = others[:, :, dimension:]
        inner_sum = jnp.einsum(
            "ad,kbd->kab", own_pts, other_pts, preferred_element_type=jnp.float32
        )
        own_wide = own_pts.astype(jnp.float32)
        other_wide = other_pts.astype(jnp.float32)
        distance = (
            jnp.sum(own_wide * own_wide, -1)[None, :, None]
            + jnp.sum(other_wide * other_wide, -1)[:, None, :]
            - 2.0 * inner_sum
        )
        tile_block = (
            jnp.exp(distance * (-2.0 / dimension)) * slot_valid.astype(jnp.float32)[:, None, None]
        )
        tile_block = tile_block.astype(jnp.bfloat16)
        return jnp.einsum("kab,kbc->ac", tile_block, other_vals, preferred_element_type=jnp.float32)

    return lax.map(single, (own_leaves, leaf_ids, leaf_valid))


def climb(values_leaf, tree_data):
    (
        leaf_basis,
        level_mats,
        level_kernels,
        chain_mats,
        chain_kernels,
        bit_values,
        group_index,
        group_points,
        flat_points,
        share_rows,
        slot_start,
    ) = tree_data
    rank_size = leaf_basis.shape[2]
    columns = values_leaf.shape[2]
    coeffs = jnp.einsum("lpr,lpc->lrc", leaf_basis, values_leaf, preferred_element_type=jnp.float32)
    couplings = []
    for matrix, kernel in zip(level_mats, level_kernels):
        couplings.append(sibling_terms(kernel, coeffs))
        coeffs = jnp.einsum(
            "nkr,nkc->nrc", matrix, coeffs.reshape(-1, 2 * rank_size, columns), precision=HIGHEST
        )
    current = coeffs[0]
    for bit_index in range(len(bit_values)):
        sibling = partner_2(current, "pts", bit_index)
        couplings.append(jnp.dot(chain_kernels[bit_index], sibling, precision=HIGHEST))
        stacked = jnp.where(
            bit_values[bit_index] == 0,
            jnp.concatenate([current, sibling], 0),
            jnp.concatenate([sibling, current], 0),
        )
        current = jnp.dot(chain_mats[bit_index].T, stacked, precision=HIGHEST)
    portion = lax.dynamic_slice_in_dim(current, slot_start, share_rows, 0)
    piece_data = lax.all_gather(portion, "pts", axis=0, tiled=True)
    piece_rows = piece_data.shape[0]
    kernel = kernel_block(group_points[None], flat_points[None])[0]
    owners = jnp.arange(piece_rows, dtype=jnp.int32) // rank_size
    kernel = jnp.where(owners[None, :] == group_index, jnp.float32(0.0), kernel)
    field_now = jnp.dot(kernel, piece_data, precision=HIGHEST)
    local_levels = len(level_mats)
    for bit_index in reversed(range(len(bit_values))):
        spread = jnp.dot(chain_mats[bit_index], field_now, precision=HIGHEST)
        field_now = couplings[local_levels + bit_index] + lax.dynamic_slice_in_dim(
            spread, bit_values[bit_index] * rank_size, rank_size, 0
        )
    field_now = field_now[None]
    for level_index in reversed(range(local_levels)):
        spread = jnp.einsum("nkr,nrc->nkc", level_mats[level_index], field_now, precision=HIGHEST)
        field_now = couplings[level_index] + spread.reshape(-1, rank_size, columns)
    return field_now


def local(
    points,
    inputs,
    cotangent,
    order,
    near_ids,
    near_valid,
    leaf_basis,
    local_transfer,
    chain_transfer,
    leaf_skel,
    local_skel,
    chain_skel,
    top_skel,
):
    leaf_count = leaf_basis.shape[0]
    leaf_size = leaf_basis.shape[1]
    rank_size = leaf_basis.shape[2]
    dimension = points.shape[1]
    row_count = points.shape[0]
    columns = inputs.shape[1]
    device = lax.axis_index("pts")
    local_order = order - device * row_count
    own_points = jnp.take(points, local_order, axis=0)
    own_inputs = jnp.take(inputs, local_order, axis=0)
    relative = near_ids - (device - 1) * leaf_count
    points_leaf = own_points.reshape(leaf_count, leaf_size, dimension)
    joined = jnp.concatenate([own_points, own_inputs], 1)
    widened = with_halo(joined, (("pts", 0),), row_count)
    blocks = widened.reshape(3 * leaf_count, leaf_size, dimension + columns)
    near_sum = near_terms(points_leaf, blocks, relative, near_valid, dimension)
    local_count = leaf_count.bit_length() - 1
    local_mats = local_transfer.astype(jnp.float32)
    level_mats = []
    level_kernels = []
    skeletons = leaf_skel
    offset = 0
    node_count = leaf_count
    for level_index in range(local_count):
        level_kernels.append(kernel_block(skeletons[0::2], skeletons[1::2]))
        node_count = node_count // 2
        level_mats.append(local_mats[offset : offset + node_count])
        skeletons = local_skel[offset : offset + node_count]
        offset = offset + node_count
    chain_mats = chain_transfer[0].astype(jnp.float32)
    bit_values = []
    chain_kernels = []
    for bit_index in range(UP):
        own_bit = jnp.bitwise_and(jnp.right_shift(device, bit_index), 1)
        pair_points = chain_skel[0, bit_index]
        mine_points = jnp.take(pair_points, own_bit, axis=0)
        theirs = jnp.take(pair_points, 1 - own_bit, axis=0)
        chain_kernels.append(kernel_block(mine_points[None], theirs[None])[0])
        bit_values.append(own_bit)
    group_index = jnp.right_shift(device, UP)
    group_points = jnp.take(top_skel, group_index, axis=0)
    flat_points = top_skel.reshape(-1, dimension)
    share_rows = rank_size // 2**UP
    slot_start = jnp.bitwise_and(device, 2**UP - 1) * share_rows
    tree_data = (
        leaf_basis,
        level_mats,
        level_kernels,
        chain_mats,
        chain_kernels,
        bit_values,
        group_index,
        group_points,
        flat_points,
        share_rows,
        slot_start,
    )
    inputs_leaf = own_inputs.reshape(leaf_count, leaf_size, columns)
    cot_leaf = cotangent.reshape(leaf_count, leaf_size, columns)
    field_in = climb(inputs_leaf, tree_data)
    field_cot = climb(cot_leaf, tree_data)
    basis_wide = leaf_basis.astype(jnp.float32)
    output = near_sum + jnp.einsum("lpr,lrc->lpc", basis_wide, field_in, precision=HIGHEST)
    partial_grad = jnp.einsum(
        "lpc,lrc->lpr", cot_leaf.astype(jnp.float32), field_in, precision=HIGHEST
    )
    partial_grad = partial_grad + jnp.einsum(
        "lpc,lrc->lpr", inputs_leaf.astype(jnp.float32), field_cot, precision=HIGHEST
    )
    basis_grad = lax.psum_scatter(partial_grad, "rhs", scatter_dimension=1, tiled=True)
    return (
        output.reshape(row_count, columns).astype(jnp.bfloat16),
        basis_grad.astype(jnp.bfloat16),
    )


def solution(mesh):
    placed = (
        P("pts", None),
        P("pts", "rhs"),
        P("pts", "rhs"),
        P("pts"),
        P("pts", None),
        P("pts", None),
        P("pts", None, None),
        P("pts", None, None),
        P("pts", None, None, None),
        P("pts", None, None),
        P("pts", None, None),
        P("pts", None, None, None, None),
        P(),
    )
    return jax.shard_map(
        local,
        mesh=mesh,
        in_specs=placed,
        out_specs=(P("pts", "rhs"), P("pts", "rhs", None)),
        check_vma=False,
    )
```

profile of v0, /device:TPU:8, one launch (start us, length us, event | category | flops | bytes accessed | tf_op | source)
XLA Modules:
  0.0 1566.4 jit_solution(10213241947142160839)
XLA Ops:
  11.1 6.2 gather_fusion.1
  17.3 6.2 gather_fusion.2
  25.1 3.5 collective-permute-start
  28.6 6.3 collective-permute-start.1
  37.0 1.9 collective-permute-start.6
  41.0 3.9 collective-permute-start.2
  76.8 1.9 collective-permute-start.7
  79.8 4.8 collective-permute-start.3
  84.8 3.4 collective-permute-start.8
  88.4 6.4 collective-permute-start.4
  94.9 1.9 collective-permute-start.9
  98.9 4.3 collective-permute-start.5
  103.5 684.7 %all_gather.7 = f32[2048,64]{1,0:T(8,128)S(1)} all-gather(f32[8,64]{1,0:T(8,128)S(1)} %fusion.209), channel_id=1, replica_groups=mesh['pts'=256,'rhs'=2] {'pts'}, dimensions={0}, use_global_device_ids=true | all-gather | bytes 526336 | tf_op jit(solution)/shard_map/all_gather | solution.py:109
  800.9 686.9 %all_gather.6 = f32[2048,64]{1,0:T(8,128)S(1)} all-gather(f32[8,64]{1,0:T(8,128)S(1)} %fusion.208), channel_id=1, replica_groups=mesh['pts'=256,'rhs'=2] {'pts'}, dimensions={0}, use_global_device_ids=true | all-gather | bytes 526336 | tf_op jit(solution)/shard_map/all_gather | solution.py:109
  1487.8 1.8 fusion.225
  1501.0 54.8 %while.12 = (s32[]{:T(128)}, f32[8,256,64]{1,2,0:T(8,128)}, bf16[8,256,64]{1,2,0:T(8,128)(2,1)}, s32[8,12]{1,0:T(8,128)S(1)}, bf16[24,256,128]{2,1,0:T(8,128)(2,1)S(1)}, /*index=5*/s32[8,12]{1,0:T(8,128)}, s32[]{:T(128)}) while((s32[]{:T(128)}, f32[8,256,64]{1,2,0:T(8,128)}, bf16[8,256,64]{1,2,0:T(8,128)(2,1)}, s32[8,12]{1,0:T(8,128)S(1)}, ...), condition=%wide.region_3.5_spmd, body=%wide.region_0.4_spmd.sunk | while | flops 207075200 | bytes 18644524 | solution.py:72
  1504.9 2.9 fusion.297
  1511.8 2.9 fusion.297
  1518.6 2.9 fusion.297
  1525.5 3.0 fusion.297
  1532.3 2.9 fusion.297
  1539.2 2.9 fusion.297
  1546.0 2.9 fusion.297
  1552.9 2.9 fusion.297
  (288 shorter events, 103.2 us)
Async XLA Ops:
  7.2 27.8 %copy-start = (bf16[8,256,128]{2,1,0:T(8,128)(2,1)S(1)}, bf16[8,256,128]{2,1,0:T(8,128)(2,1)}, u32[]{:S(2)}) copy-start(bf16[8,256,128]{2,1,0:T(8,128)(2,1)} %param.25) | copy-start | bytes 1572868
  7.2 1550.5 %reduce-scatter.2.cloned.1.call-start = ((), (), s32[]{:S(2)}) async-start(), calls=%async_computation.1 | async-start | bytes 1572864 | tf_op jit(solution)/shard_map/reduce_scatter | solution.py:212
  23.5 11.4 copy-start.9
  24.0 11.5 copy-start.3
  25.1 1474.4 %collective-permute-start = (bf16[2048,128]{1,0:T(8,128)(2,1)}, bf16[2048,128]{1,0:T(8,128)(2,1)}, u32[]{:S(2)}, u32[]{:S(2)}) collective-permute-start(bf16[2048,128]{1,0:T(8,128)(2,1)} %pad_maximum_fusion.1), channel_id=1, source_target_pairs={{0,2},{2,4},{4,6},{6,8},{8,10},{10,12},{12,14},{14,16},{16,18},{18... | collective-permute-start | bytes 1572872 | tf_op jit(solution)/shard_map/ppermute | solution.py:23
  28.6 1470.9 %collective-permute-start.1 = (bf16[2048,128]{1,0:T(8,128)(2,1)}, bf16[2048,128]{1,0:T(8,128)(2,1)}, u32[]{:S(2)}, u32[]{:S(2)}) collective-permute-start(bf16[2048,128]{1,0:T(8,128)(2,1)} %pad_maximum_fusion.1), channel_id=1, source_target_pairs={{2,0},{4,2},{6,4},{8,6},{10,8},{12,10},{14,12},{16,14},{18,16},{20... | collective-permute-start | bytes 1572872 | tf_op jit(solution)/shard_map/ppermute | solution.py:26
  37.0 38.8 %collective-permute-start.6 = (f32[128,64]{0,1:T(8,128)}, f32[128,64]{0,1:T(8,128)}, u32[]{:S(2)}, u32[]{:S(2)}) collective-permute-start(f32[128,64]{0,1:T(8,128)} %convolution_bitcast_fusion.22), channel_id=1, source_target_pairs={{0,2},{2,0},{4,6},{6,4},{8,10},{10,8},{12,14},{14,12},{16,18},{18,... | collective-permute-start | bytes 98312 | tf_op jit(solution)/shard_map/ppermute | solution.py:15
  39.5 11.8 copy-start.18
  41.0 37.7 %collective-permute-start.2 = (f32[128,64]{0,1:T(8,128)}, f32[128,64]{0,1:T(8,128)}, u32[]{:S(2)}, u32[]{:S(2)}) collective-permute-start(f32[128,64]{0,1:T(8,128)} %convolution_bitcast_fusion.28), channel_id=1, source_target_pairs={{0,2},{2,0},{4,6},{6,4},{8,10},{10,8},{12,14},{14,12},{16,18},{18,... | collective-permute-start | bytes 98312 | tf_op jit(solution)/shard_map/ppermute | solution.py:15
  56.6 8.8 copy-start.27
  59.8 730.5 %copy-start.11 = (f32[128,128]{1,0:T(8,128)}, f32[128,128]{1,0:T(8,128)S(1)}, u32[]{:S(2)}) copy-start(f32[128,128]{1,0:T(8,128)S(1)} %fusion.35) | copy-start | bytes 196612
  66.9 8.9 copy-start.5
  76.8 7.8 collective-permute-start.7
  79.8 8.4 collective-permute-start.3
  84.8 10.0 collective-permute-start.8
  88.2 15.3 copy-start.23
  88.4 9.7 collective-permute-start.4
  94.9 8.3 collective-permute-start.9
  98.1 5.4 copy-start.25
  98.9 700.9 %collective-permute-start.5 = (f32[128,64]{0,1:T(8,128)}, f32[128,64]{0,1:T(8,128)}, u32[]{:S(2)}, u32[]{:S(2)}) collective-permute-start(f32[128,64]{0,1:T(8,128)} %convolution_bitcast_fusion.25), channel_id=1, source_target_pairs={{0,16},{2,18},{4,20},{6,22},{8,24},{10,26},{12,28},{14,30},{16,0},... | collective-permute-start | bytes 98312 | tf_op jit(solution)/shard_map/ppermute | solution.py:15
  800.9 689.0 %copy-start.12 = (f32[128,128]{1,0:T(8,128)S(1)}, f32[128,128]{1,0:T(8,128)}, u32[]{:S(2)}) copy-start(f32[128,128]{1,0:T(8,128)} %copy-done.11) | copy-start | bytes 196612
  1487.8 5.3 copy-start.19
  1487.8 5.3 copy-start.20
  1501.0 54.8 %copy-start.4 = (f32[8,256,64]{1,2,0:T(8,128)S(1)}, f32[8,256,64]{1,2,0:T(8,128)}, u32[]{:S(2)}) copy-start(f32[8,256,64]{1,2,0:T(8,128)} %convolution_bitcast_fusion.1) | copy-start | bytes 1572868
  (29 other events, 75.2 us)
Sparse Core Ops, SparseCore 0:
  1498.1 6.0 reduce-scatter.1
where the time goes:
time: 1570 us
  blocking collectives  1370 us (87%)
  matrix products  61.5 us (4%)
  local copies, waits for them, and re-layouts  49 us (3%)
  starting transfers between devices  38.4 us (2%)
  other arithmetic  29.1 us (2%)
    all_gather x2, blocking collectives, climb(): piece_data = lax.all_gather(portion, 'pts', axis=0, tiled=True)  1370 us
  transfers between devices with their start and end apart: 11, of which 1 were waited for; matrix products, arithmetic and copies ran while one was open for 7% of the time, Pallas kernels for 0%

commit v1 on v0

v1 whole, which is shorter than its diff:
```python
import functools
import math

import jax
import jax.numpy as jnp
from jax import lax
from jax.experimental import pallas as pl
from jax.experimental.pallas import tpu as pltpu
from jax.sharding import PartitionSpec as P

F32 = jnp.float32
BF16 = jnp.bfloat16

LEVELS = 4
MEMBERS = 16
GROUPS = 16
SLAB = 48
SHARE = 8
LEAVES = 8
ROWS = 256
RANK = 128
DIM = 64
SLOTS = 12

VMEM = pl.BlockSpec(memory_space=pltpu.VMEM)
SMEM = pl.BlockSpec(memory_space=pltpu.SMEM)
NN = (((1,), (0,)), ((), ()))
NT = (((1,), (1,)), ((), ()))


def mm(a, b, dims=NN):
    return lax.dot_general(a, b, dims, preferred_element_type=F32)


def split(a):
    high = a.astype(BF16)
    return high, (a - high.astype(F32)).astype(BF16)


def mm2(a, b, dims=NN):
    high, low = split(a)
    return mm(high, b, dims) + mm(low, b, dims)


def lanes(rows, width=128):
    return lax.broadcasted_iota(jnp.int32, (rows, width), 1)


def norm_terms(wide):
    half = -0.5 * jnp.sum(wide * wide, axis=1, keepdims=True)
    first = half.astype(BF16).astype(F32)
    rest = half - first
    second = rest.astype(BF16).astype(F32)
    third = (rest - second).astype(BF16).astype(F32)
    return first, second, third


def extended(pts, base, left, right):
    first, second, third = norm_terms(pts)
    lane = lanes(pts.shape[0], pts.shape[1])
    out = []
    for want, lo, hi in ((left, 0, 3), (right, 3, 0)):
        if not want:
            continue
        value = pts
        for offset, term in ((lo, first), (lo + 1, second), (lo + 2, third)):
            value = jnp.where(lane == base + offset, term, value)
        ones = (lane >= base + hi) & (lane < base + hi + 3)
        out.append(jnp.where(ones, 1.0, value).astype(BF16))
    return out


EXPO = 4.0 / (DIM * math.log(2.0))


def skel_rows(pts):
    wide = pts.astype(F32)
    return jnp.concatenate([wide, jnp.zeros_like(wide)], axis=1)


def kappa(left_pts, right_pts):
    (left,) = extended(skel_rows(left_pts), DIM, True, False)
    (right,) = extended(skel_rows(right_pts), DIM, False, True)
    return jnp.exp2(mm(left, right, NT) * EXPO)


def call(kernel, outs, specs, scratch=(), cost=(0, 0, 0)):
    return pl.pallas_call(
        kernel,
        out_shape=outs,
        in_specs=specs,
        out_specs=jax.tree.map(lambda _: VMEM, outs),
        scratch_shapes=list(scratch),
        compiler_params=pltpu.CompilerParams(vmem_limit_bytes=40 * 2**20),
        cost_estimate=pl.CostEstimate(
            flops=cost[0], bytes_accessed=cost[1], transcendentals=cost[2]
        ),
    )


def sds(shape, dtype):
    return jax.ShapeDtypeStruct(shape, dtype)


def order_kernel(pos, points, inputs, order, joined, source):
    base = pos[0] * (LEAVES * ROWS)
    source[...] = jnp.concatenate([inputs[...], points[...]], axis=1)
    lane = lanes(ROWS).astype(F32).astype(BF16)
    for leaf in range(LEAVES):
        row = order[pl.ds(leaf, 1), :] - base
        low = jnp.bitwise_and(row, 127).astype(F32)
        high = jnp.right_shift(row, 7).astype(F32)
        low = jnp.broadcast_to(low, (128, ROWS)).T.astype(BF16)
        high = jnp.broadcast_to(high, (128, ROWS)).T.astype(BF16)
        one, zero = jnp.ones((), BF16), jnp.zeros((), BF16)
        hit = jnp.where(low == lane, one, zero)
        pick = jnp.concatenate(
            [jnp.where(high == jnp.full((), c, BF16), hit, zero) for c in range(16)], axis=1
        )
        joined[leaf] = mm(pick, source[...]).astype(BF16)


def up_kernel(pos, joined, cot, basis, transfer, chain, both, coeffs, send):
    device = pos[0]
    now = []
    for leaf in range(LEAVES):
        pair = jnp.concatenate(
            [joined[leaf][:, :DIM], cot[leaf]], axis=1
        )
        both[leaf] = pair
        now.append(mm(pair.T, basis[leaf]))
    offset, done = 0, 0
    while len(now) > 1:
        for node, value in enumerate(now):
            coeffs[done + node] = value
        done += len(now)
        now = [
            mm2(jnp.concatenate([now[2 * n], now[2 * n + 1]], axis=1), transfer[offset + n])
            for n in range(len(now) // 2)
        ]
        offset += len(now)
    value = now[0]
    parts = [value]
    for level in range(LEVELS):
        bit = jnp.bitwise_and(jnp.right_shift(device, level), 1)
        half = chain[0, level, pl.ds(pl.multiple_of(bit * RANK, RANK), RANK), :]
        value = mm2(value, half)
        parts.append(value)
    parts = [part.reshape(MEMBERS, SHARE, RANK) for part in parts]
    parts.append(jnp.zeros((MEMBERS, SLAB - 5 * SHARE, RANK), F32))
    send[...] = jnp.concatenate(parts, axis=1).astype(BF16)


def couple_kernel(
    pos, coeffs, leaf_skel, local_skel, chain_skel, top_skel, couplings, chain_k, top_k
):
    device = pos[0]
    group = jnp.right_shift(device, LEVELS)
    for node in range(0, 14, 2):
        if node < 8:
            even, odd = leaf_skel[node], leaf_skel[node + 1]
        else:
            even, odd = local_skel[node - 8], local_skel[node - 7]
        high, low = split(kappa(even, odd))
        for target, other, dims in ((node, node + 1, NT), (node + 1, node, NN)):
            value = coeffs[other]
            couplings[target] = mm2(value, high, dims) + mm(value.astype(BF16), low, dims)
    for level in range(LEVELS):
        bit = jnp.bitwise_and(jnp.right_shift(device, level), 1)
        chain_k[level] = kappa(chain_skel[0, level, 1 - bit], chain_skel[0, level, bit]).astype(BF16)
    mine = top_skel[group]
    for other in range(GROUPS):
        value = kappa(top_skel[other], mine)
        top_k[other] = jnp.where(group == other, 0.0, value).astype(BF16)


def part(received, member, index):
    return received[member].astype(F32)[index * SHARE : (index + 1) * SHARE]


def level_sums(received, index):
    sums = [part(received, member, index) for member in range(MEMBERS)]
    for _ in range(index):
        sums = [sums[2 * n] + sums[2 * n + 1] for n in range(len(sums) // 2)]
    return sums


def total_kernel(received, send):
    total = level_sums(received, LEVELS)[0]
    total = jnp.concatenate([total, jnp.zeros_like(total)], axis=0).astype(BF16)
    for group in range(GROUPS):
        send[group] = total


def reply_kernel(received, totals, top_k, reply):
    flat = jnp.concatenate([totals[group] for group in range(GROUPS)], axis=1)
    field = mm(flat, top_k[...].reshape(GROUPS * RANK, RANK))[:SHARE]
    levels = [level_sums(received, level) for level in range(LEVELS)]
    blank = jnp.zeros((SHARE, RANK), F32)
    for member in range(MEMBERS):
        rows = [levels[level][(member >> level) ^ 1] for level in range(LEVELS)]
        reply[member] = jnp.concatenate(rows + [field, blank], axis=0).astype(BF16)


def down_kernel(pos, replies, chain_k, chain, couplings, transfer, both, fields, give):
    device, core = pos[0], pos[1]
    table = replies[...].astype(F32)
    got = [
        table[:, index * SHARE : (index + 1) * SHARE].reshape(RANK, RANK)
        for index in range(LEVELS + 1)
    ]
    field = got[LEVELS]
    for level in reversed(range(LEVELS)):
        bit = jnp.bitwise_and(jnp.right_shift(device, level), 1)
        half = chain[0, level, pl.ds(pl.multiple_of(bit * RANK, RANK), RANK), :]
        field = mm(got[level].astype(BF16), chain_k[level]) + mm2(field, half, NT)
    now = [field]
    for start, count, offset in ((6, 1, 12), (4, 2, 8), (0, 4, 0)):
        below = []
        for node in range(count):
            spread = mm2(now[node], transfer[start + node], NT)
            for child in range(2):
                rows = spread[:, child * RANK : (child + 1) * RANK]
                below.append(couplings[offset + 2 * node + child] + rows)
        now = below
    away = pl.multiple_of((1 - core) * RANK, RANK)
    for leaf in range(LEAVES):
        fields[leaf] = now[leaf]
        swapped = jnp.concatenate([now[leaf][DIM:], now[leaf][:DIM]], axis=0)
        high, low = split(swapped)
        rows = both[leaf, pl.ds(away, RANK), :]
        give[leaf] = (mm(rows, high) + mm(rows, low)).astype(BF16)


def finish_kernel(pos, fields, both, basis, near, output, keep):
    core = pos[1]
    stay = pl.multiple_of(core * RANK, RANK)
    for leaf in range(LEAVES):
        field = fields[leaf]
        high, low = split(field)
        far = mm(basis[leaf], high, NT) + mm(basis[leaf], low, NT)
        output[pl.ds(leaf * ROWS, ROWS), :] = (near[leaf] + far)[:, :DIM].astype(BF16)
        swapped = jnp.concatenate([field[DIM:], field[:DIM]], axis=0)
        high, low = split(swapped)
        rows = both[leaf, pl.ds(stay, RANK), :]
        keep[leaf] = mm(rows, high) + mm(rows, low)


def prepare_kernel(below, own, above, left, right):
    lane = lanes(ROWS)
    for index, block in enumerate((below, own, above)):
        for leaf in range(LEAVES):
            pts = jnp.where(lane >= DIM, block[leaf].astype(F32), 0.0)
            made = extended(pts, 0, index == 1, True)
            right[index * LEAVES + leaf] = made[-1]
            if index == 1:
                left[leaf] = made[0]


def near_kernel(first, pos, ids, valid, left, right, below, own, above, near, values):
    shift = (pos[0] - 1) * LEAVES
    for index, block in enumerate((below, own, above)):
        values[pl.ds(index * LEAVES, LEAVES)] = block[...]

    def body(step, carry):
        leaf = first + step
        mine = left[leaf]
        total = jnp.zeros((ROWS, 128), F32)
        for slot in range(SLOTS):
            where = ids[leaf, slot] - shift
            used = valid[leaf, slot].astype(F32)
            tile = jnp.exp2(mm(mine, right[where], NT) * EXPO).astype(BF16)
            other = (values[where].astype(F32) * used).astype(BF16)
            total = total + mm(tile, other)
        near[step] = total
        return carry

    lax.fori_loop(0, near.shape[0], body, 0)


def local(
    points,
    inputs,
    cotangent,
    order,
    near_ids,
    near_valid,
    leaf_basis,
    local_transfer,
    chain_transfer,
    leaf_skel,
    local_skel,
    chain_skel,
    top_skel,
):
    device = lax.axis_index("pts")
    core = lax.axis_index("rhs")
    pos = jnp.stack([device, core]).astype(jnp.int32)
    count = lax.axis_size("pts")
    block = (LEAVES, ROWS, 128)

    joined = call(
        order_kernel,
        sds(block, BF16),
        [SMEM, VMEM, VMEM, VMEM],
        [pltpu.VMEM((LEAVES * ROWS, 128), BF16)],
    )(pos, points, inputs, order.reshape(LEAVES, ROWS))

    upward = [(i, i + 1) for i in range(count - 1)]
    below = lax.ppermute(joined, "pts", upward)
    above = lax.ppermute(joined, "pts", [(b, a) for a, b in upward])

    both, coeffs, send = call(
        up_kernel,
        (
            sds(block, BF16),
            sds((14, RANK, RANK), F32),
            sds((MEMBERS, SLAB, RANK), BF16),
        ),
        [SMEM] + [VMEM] * 5,
    )(
        pos,
        joined,
        cotangent.reshape(LEAVES, ROWS, DIM),
        leaf_basis,
        local_transfer,
        chain_transfer,
    )

    groups = [[g * MEMBERS + i for i in range(MEMBERS)] for g in range(GROUPS)]
    across = [[g * MEMBERS + i for g in range(GROUPS)] for i in range(MEMBERS)]
    received = lax.all_to_all(send, "pts", 0, 0, axis_index_groups=groups, tiled=True)

    couplings, chain_k, top_k = call(
        couple_kernel,
        (
            sds((14, RANK, RANK), F32),
            sds((LEVELS, RANK, RANK), BF16),
            sds((GROUPS, RANK, RANK), BF16),
        ),
        [SMEM] + [VMEM] * 5,
        cost=(10**9, 2 * 10**6, 10**6),
    )(pos, coeffs, leaf_skel, local_skel, chain_skel, top_skel)

    left, right = call(
        prepare_kernel,
        (sds(block, BF16), sds((3 * LEAVES, ROWS, 128), BF16)),
        [VMEM] * 3,
        cost=(10**8, 4 * 10**6, 0),
    )(below, joined, above)

    near_parts = []
    per = 4
    for first in range(0, LEAVES, per):
        near_parts.append(
            call(
                functools.partial(near_kernel, first),
                sds((per, ROWS, 128), F32),
                [SMEM, SMEM, SMEM] + [VMEM] * 5,
                [pltpu.VMEM((3 * LEAVES, ROWS, 128), BF16)],
                cost=(per * 4 * 10**8, 4 * 10**6, per * 800000),
            )(pos, near_ids, near_valid, left, right, below, joined, above)
        )
    near = jnp.concatenate(near_parts, axis=0)

    totals = call(
        total_kernel, sds((GROUPS, 2 * SHARE, RANK), BF16), [VMEM]
    )(received)
    totals = lax.all_to_all(totals, "pts", 0, 0, axis_index_groups=across, tiled=True)
    reply = call(
        reply_kernel, sds((MEMBERS, SLAB, RANK), BF16), [VMEM] * 3
    )(received, totals, top_k)
    replies = lax.all_to_all(reply, "pts", 0, 0, axis_index_groups=groups, tiled=True)

    fields, give = call(
        down_kernel,
        (sds((LEAVES, RANK, RANK), F32), sds((LEAVES, RANK, RANK), BF16)),
        [SMEM] + [VMEM] * 6,
    )(pos, replies, chain_k, chain_transfer, couplings, local_transfer, both)
    got = lax.ppermute(give, "rhs", [(0, 1), (1, 0)])
    output, keep = call(
        finish_kernel,
        (sds((LEAVES * ROWS, DIM), BF16), sds((LEAVES, RANK, RANK), F32)),
        [SMEM] + [VMEM] * 4,
        cost=(2 * 10**8, 3 * 10**6, 0),
    )(pos, fields, both, leaf_basis, near)
    basis_grad = (keep + got.astype(F32)).astype(BF16)
    return output, basis_grad


def solution(mesh):
    placed = (
        P("pts", None),
        P("pts", "rhs"),
        P("pts", "rhs"),
        P("pts"),
        P("pts", None),
        P("pts", None),
        P("pts", None, None),
        P("pts", None, None),
        P("pts", None, None, None),
        P("pts", None, None),
        P("pts", None, None),
        P("pts", None, None, None, None),
        P(),
    )
    return jax.shard_map(
        local,
        mesh=mesh,
        in_specs=placed,
        out_specs=(P("pts", "rhs"), P("pts", "rhs", None)),
        check_vma=False,
    )
```

time: 1570 us -> 92.4 us (0.06)
  the two profiles are of different devices: /device:TPU:8 before, /device:TPU:1 now
where the time goes in v1:
time: 92.4 us; the launch traced here: 91.5 us
  starting transfers between devices  36.8 us (40%)
  Pallas kernels  28.8 us (31%)
  local copies, waits for them, and re-layouts  21.2 us (23%)
  waiting for transfers between devices  2.95 us (3%)
  between operations  0.95 us (1%)
    unnamed x54, local copies, waits for them, and re-layouts  21.2 us
    all_to_all x1, starting transfers between devices, local(): lax.all_to_all(totals, 'pts', 0, 0, axis_index_groups=across, tiled=True)  12.8 us
    pallas_call x2, Pallas kernels, local(): call(functools.partial(near_kernel, first), sds((per, ROWS, 128), F32), [...  11.9 us
    all_to_all x1, starting transfers between devices, local(): lax.all_to_all(send, 'pts', 0, 0, axis_index_groups=groups, tiled=True)  9.56 us
    all_to_all x1, starting transfers between devices, local(): lax.all_to_all(reply, 'pts', 0, 0, axis_index_groups=groups, tiled=True)  5.46 us
    ppermute x1, starting transfers between devices, local(): got = lax.ppermute(give, 'rhs', [(0, 1), (1, 0)])  4.38 us
    ppermute x1, starting transfers between devices, local(): below = lax.ppermute(joined, 'pts', upward)  3.29 us
    pallas_call x1, Pallas kernels, local(): call(order_kernel, sds(block, BF16), [SMEM, VMEM, VMEM, VMEM], [pltpu.VME...  3.06 us
  transfers between devices with their start and end apart: 6, of which 1 were waited for; matrix products, arithmetic and copies ran while one was open for 7% of the time, Pallas kernels for 22%

profile of v1, /device:TPU:1, one launch (start us, length us, event | category | flops | bytes accessed | tf_op | source)
XLA Modules:
  0.0 91.5 jit_solution(8803356925548504591)
XLA Ops:
  0.7 1.3 %copy.15.points = bf16[2048,64]{1,0:T(8,128)(2,1)S(1)} copy(bf16[2048,64]{0,1:T(8,128)(2,1)} %param.13) | data formatting | bytes 524288 | tf_op args[0]
  2.0 1.3 %copy.16.inputs = bf16[2048,64]{1,0:T(8,128)(2,1)S(1)} copy(bf16[2048,64]{0,1:T(8,128)(2,1)} %param.14) | data formatting | bytes 524288 | tf_op args[1]
  3.7 3.1 %shard_map.140.joined.own = bf16[8,256,128]{2,1,0:T(8,128)(2,1)S(1)} custom-call(s32[2]{0:T(128)S(1)} %pad_add_fusion.pos, bf16[2048,64]{1,0:T(8,128)(2,1)S(1)} %copy.15.points, bf16[2048,64]{1,0:T(8,128)(2,1)S(1)} %copy.16.inputs, s32[8,256]{1,0:T(8,128)S(1)} %reshape.10.order), custom_call_target="tpu_custom_call" | custom-call | tf_op jit(solution)/shard_map/pallas_call | solution.py:302
  6.8 2.7 %shard_map.141 = (bf16[8,256,128]{2,1,0:T(8,128)(2,1)S(1)}, f32[14,128,128]{2,1,0:T(8,128)S(1)}, bf16[16,48,128]{2,1,0:T(8,128)(2,1)}) custom-call(s32[2]{0:T(128)S(1)} %pad_add_fusion.pos, bf16[8,256,128]{2,1,0:T(8,128)(2,1)S(1)} %shard_map.140.joined.own, bf16[8,256,64]{2,1,0:T(8,128)(2,1)S(1)} %bitcast.3, bf16[8,256,128]{2,1,0:T(8,128)(2,1)S(1)} %copy-done, ...), custom_call_target="tpu_custom_call" | custom-call | tf_op jit(solution)/shard_map/pallas_call | solution.py:313
  10.4 9.6 %all-to-all-start = ((bf16[16,48,128]{2,1,0:T(8,128)(2,1)}), bf16[16,48,128]{2,1,0:T(8,128)(2,1)S(1)}, u32[]{:S(2)}, u32[]{:S(2)}) async-start(bf16[16,48,128]{2,1,0:T(8,128)(2,1)} %get-tuple-element.14), calls=%async_computation | async-start | bytes 393216 | tf_op jit(solution)/shard_map/all_to_all | solution.py:332
  20.0 3.3 %collective-permute-start = (bf16[8,256,128]{2,1,0:T(8,128)(2,1)S(1)}, bf16[8,256,128]{2,1,0:T(8,128)(2,1)S(1)}, u32[]{:S(2)}, u32[]{:S(2)}) collective-permute-start(bf16[8,256,128]{2,1,0:T(8,128)(2,1)S(1)} %shard_map.140.joined.own), channel_id=1, source_target_pairs={{0,2},{2,4},{4,6},{6,8},{8,10},{10,12},{12,14},{14,16},{16,18},{18... | collective-permute-start | bytes 1572872 | tf_op jit(solution)/shard_map/ppermute | solution.py:310
  23.3 1.3 %collective-permute-start.1 = (bf16[8,256,128]{2,1,0:T(8,128)(2,1)S(1)}, bf16[8,256,128]{2,1,0:T(8,128)(2,1)}, u32[]{:S(2)}, u32[]{:S(2)}) collective-permute-start(bf16[8,256,128]{2,1,0:T(8,128)(2,1)S(1)} %shard_map.140.joined.own), channel_id=1, source_target_pairs={{2,0},{4,2},{6,4},{8,6},{10,8},{12,10},{14,12},{16,14},{18,16},{20... | collective-permute-start | bytes 1572872 | tf_op jit(solution)/shard_map/ppermute | solution.py:311
  24.6 2.9 %all-to-all-done.received = bf16[16,48,128]{2,1,0:T(8,128)(2,1)S(1)} async-done(((bf16[16,48,128]{2,1,0:T(8,128)(2,1)}), bf16[16,48,128]{2,1,0:T(8,128)(2,1)S(1)}, u32[]{:S(2)}, u32[]{:S(2)}) %all-to-all-start) | async-done | bytes 196640 | tf_op jit(solution)/shard_map/all_to_all | solution.py:332
  28.1 12.8 %all-to-all-start.1 = ((bf16[16,16,128]{2,1,0:T(8,128)(2,1)}), bf16[16,16,128]{2,1,0:T(8,128)(2,1)S(1)}, u32[]{:S(2)}, u32[]{:S(2)}) async-start(bf16[16,16,128]{2,1,0:T(8,128)(2,1)} %shard_map.142), calls=%async_computation.1 | async-start | bytes 131072 | tf_op jit(solution)/shard_map/all_to_all | solution.py:369
  40.9 2.0 %copy.21.top_skel = bf16[16,128,64]{2,1,0:T(8,128)(2,1)} copy(bf16[16,128,64]{1,2,0:T(8,128)(2,1)} %param.25) | data formatting | bytes 524288 | tf_op args[12]
  43.1 1.8 %copy.20.chain_skel = bf16[1,4,2,128,64]{4,3,2,1,0:T(8,128)(2,1)} copy(bf16[1,4,2,128,64]{3,4,2,1,0:T(8,128)(2,1)} %param.24) | data formatting | bytes 262144 | tf_op args[11]
  44.8 1.7 %copy.19.local_skel = bf16[7,128,64]{2,1,0:T(8,128)(2,1)} copy(bf16[7,128,64]{1,2,0:T(8,128)(2,1)} %param.23) | data formatting | bytes 229376 | tf_op args[10]
  49.5 1.2 %copy-done.15 = f32[14,128,128]{2,1,0:T(8,128)S(1)} copy-done((f32[14,128,128]{2,1,0:T(8,128)S(1)}, f32[14,128,128]{2,1,0:T(8,128)}, u32[]{:S(2)}) %copy-start.15) | copy-done | bytes 917528
  50.6 3.0 %shard_map.143 = (f32[14,128,128]{2,1,0:T(8,128)S(1)}, bf16[4,128,128]{2,1,0:T(8,128)(2,1)S(1)}, bf16[16,128,128]{2,1,0:T(8,128)(2,1)S(1)}) custom-call(s32[2]{0:T(128)S(1)} %pad_add_fusion.pos, f32[14,128,128]{2,1,0:T(8,128)S(1)} %copy-done.15, bf16[8,128,64]{2,1,0:T(8,128)(2,1)S(1)} %copy.18.leaf_skel, bf16[7,128,64]{2,1,0:T(8,128)(2,1)S(1)} %copy-done.11, ...), custom_call_target="tpu_custom_call" | custom-call | flops 1000000000 | bytes 2000000 | tf_op jit(solution)/shard_map/pallas_call | solution.py:334
  55.4 1.0 %copy-done.7 = bf16[16,128,128]{2,1,0:T(8,128)(2,1)S(1)} copy-done((bf16[16,128,128]{2,1,0:T(8,128)(2,1)S(1)}, bf16[16,128,128]{2,1,0:T(8,128)(2,1)}, u32[]{:S(2)}) %copy-start.7) | copy-done | bytes 524312
  57.3 5.5 %all-to-all-start.2 = ((bf16[16,48,128]{2,1,0:T(8,128)(2,1)}), bf16[16,48,128]{2,1,0:T(8,128)(2,1)S(1)}, u32[]{:S(2)}, u32[]{:S(2)}) async-start(bf16[16,48,128]{2,1,0:T(8,128)(2,1)} %shard_map.144), calls=%async_computation.2 | async-start | bytes 393216 | tf_op jit(solution)/shard_map/all_to_all | solution.py:373
  62.8 2.6 %shard_map.146 = (bf16[8,256,128]{2,1,0:T(8,128)(2,1)S(1)}, bf16[24,256,128]{2,1,0:T(8,128)(2,1)S(1)}) custom-call(bf16[8,256,128]{2,1,0:T(8,128)(2,1)S(1)} %collective-permute-done.below, bf16[8,256,128]{2,1,0:T(8,128)(2,1)S(1)} %shard_map.140.joined.own, bf16[8,256,128]{2,1,0:T(8,128)(2,1)} %collective-permute-done.1.above), custom_call_target="tpu_custom_call" | custom-call | flops 100000000 | bytes 4000000 | tf_op jit(solution)/shard_map/pallas_call | solution.py:345
  65.5 5.9 %shard_map.147 = f32[4,256,128]{2,1,0:T(8,128)S(1)} custom-call(s32[2]{0:T(128)S(1)} %pad_add_fusion.pos, s32[8,12]{1,0:T(8,128)S(1)} %copy-done.18, s32[8,12]{1,0:T(8,128)S(1)} %copy-done.19, bf16[8,256,128]{2,1,0:T(8,128)(2,1)S(1)} %get-tuple-element.21.left, bf16[24,256,128]{2,1,0:T(8,128)(2,1)S(1)} %get-tuple-element.22.right, ...), custom_call_target="tpu_custom_call" | custom-call | flops 1600000000 | bytes 4000000 | tf_op jit(solution)/shard_map/pallas_call | solution.py:356
  72.2 1.2 %copy-done.12 = bf16[24,256,128]{2,1,0:T(8,128)(2,1)} copy-done((bf16[24,256,128]{2,1,0:T(8,128)(2,1)}, bf16[24,256,128]{2,1,0:T(8,128)(2,1)S(1)}, u32[]{:S(2)}) %copy-start.12) | copy-done | bytes 1572888
  74.2 1.2 %copy-done.4 = f32[14,128,128]{2,1,0:T(8,128)S(1)} copy-done((f32[14,128,128]{2,1,0:T(8,128)S(1)}, f32[14,128,128]{2,1,0:T(8,128)}, u32[]{:S(2)}) %copy-start.4) | copy-done | bytes 917528
  75.4 2.8 %shard_map.145 = (f32[8,128,128]{2,1,0:T(8,128)S(1)}, bf16[8,128,128]{2,1,0:T(8,128)(2,1)}) custom-call(s32[2]{0:T(128)S(1)} %pad_add_fusion.pos, bf16[16,48,128]{2,1,0:T(8,128)(2,1)S(1)} %all-to-all-done.2.replies, bf16[4,128,128]{2,1,0:T(8,128)(2,1)S(1)} %get-tuple-element.17.chain_k, bf16[1,4,256,128]{3,2,1,0:T(8,128)(2,1)S(1)} %copy-done.2, ...), custom_call_target="tpu_custom_call" | custom-call | tf_op jit(solution)/shard_map/pallas_call | solution.py:375
  78.2 4.4 %collective-permute-start.2 = (bf16[8,128,128]{2,1,0:T(8,128)(2,1)}, bf16[8,128,128]{2,1,0:T(8,128)(2,1)S(1)}, u32[]{:S(2)}, u32[]{:S(2)}) collective-permute-start(bf16[8,128,128]{2,1,0:T(8,128)(2,1)} %get-tuple-element.25), channel_id=1, source_target_pairs={{0,1},{1,0},{2,3},{3,2},{4,5},{5,4},{6,7},{7,6},{8,9},{9,8},{10,11... | collective-permute-start | bytes 786440 | tf_op jit(solution)/shard_map/ppermute | solution.py:380
  82.6 5.9 %shard_map.148 = f32[4,256,128]{2,1,0:T(8,128)S(1)} custom-call(s32[2]{0:T(128)S(1)} %pad_add_fusion.pos, s32[8,12]{1,0:T(8,128)S(1)} %copy-done.18, s32[8,12]{1,0:T(8,128)S(1)} %copy-done.19, bf16[8,256,128]{2,1,0:T(8,128)(2,1)S(1)} %copy-done.17, bf16[24,256,128]{2,1,0:T(8,128)(2,1)S(1)} %copy-done.13, ...), custom_call_target="tpu_custom_call" | custom-call | flops 1600000000 | bytes 4000000 | tf_op jit(solution)/shard_map/pallas_call | solution.py:356
  88.6 1.2 %shard_map.149 = (bf16[2048,64]{1,0:T(8,128)(2,1)S(1)}, f32[8,128,128]{2,1,0:T(8,128)S(1)}) custom-call(s32[2]{0:T(128)S(1)} %pad_add_fusion.pos, f32[8,128,128]{2,1,0:T(8,128)S(1)} %get-tuple-element.20.fields, bf16[8,256,128]{2,1,0:T(8,128)(2,1)S(1)} %get-tuple-element.19.both, bf16[8,256,128]{2,1,0:T(8,128)(2,1)S(1)} %copy-done, ...), custom_call_target="tpu_custom_call" | custom-call | flops 200000000 | bytes 3000000 | tf_op jit(solution)/shard_map/pallas_call | solution.py:381
  (56 shorter events, 11.0 us)
Async XLA Ops:
  0.6 2.7 %copy-start.22 = (s32[2048]{0:T(1024)S(1)}, s32[2048]{0:T(1024)}, u32[]{:S(2)}) copy-start(s32[2048]{0:T(1024)} %param.16) | copy-start | bytes 24580
  0.6 2.7 %copy-start.20 = (bf16[2048,64]{0,1:T(8,128)(2,1)S(1)}, bf16[2048,64]{0,1:T(8,128)(2,1)}, u32[]{:S(2)}) copy-start(bf16[2048,64]{0,1:T(8,128)(2,1)} %param.15) | copy-start | bytes 786436
  1.9 4.8 %copy-start = (bf16[8,256,128]{2,1,0:T(8,128)(2,1)S(1)}, bf16[8,256,128]{2,1,0:T(8,128)(2,1)}, u32[]{:S(2)}) copy-start(bf16[8,256,128]{2,1,0:T(8,128)(2,1)} %basis.3) | copy-start | bytes 1572868
  1.9 4.8 %copy-start.1 = (bf16[7,256,128]{2,1,0:T(8,128)(2,1)S(1)}, bf16[7,256,128]{2,1,0:T(8,128)(2,1)}, u32[]{:S(2)}) copy-start(bf16[7,256,128]{2,1,0:T(8,128)(2,1)} %transfer.3) | copy-start | bytes 1376260
  1.9 4.8 %copy-start.2 = (bf16[1,4,256,128]{3,2,1,0:T(8,128)(2,1)S(1)}, bf16[1,4,256,128]{3,2,1,0:T(8,128)(2,1)}, u32[]{:S(2)}) copy-start(bf16[1,4,256,128]{3,2,1,0:T(8,128)(2,1)} %chain.3) | copy-start | bytes 786436
  6.8 36.1 %copy-start.21 = (bf16[8,128,64]{1,2,0:T(8,128)(2,1)S(1)}, bf16[8,128,64]{1,2,0:T(8,128)(2,1)}, u32[]{:S(2)}) copy-start(bf16[8,128,64]{1,2,0:T(8,128)(2,1)} %param.22) | copy-start | bytes 393220
  9.5 0.9 %copy-start.14 = (f32[14,128,128]{2,1,0:T(8,128)}, f32[14,128,128]{2,1,0:T(8,128)S(1)}, u32[]{:S(2)}) copy-start(f32[14,128,128]{2,1,0:T(8,128)S(1)} %get-tuple-element.15.coeffs) | copy-start | bytes 2752516
  10.4 17.1 %all-to-all-start = ((bf16[16,48,128]{2,1,0:T(8,128)(2,1)}), bf16[16,48,128]{2,1,0:T(8,128)(2,1)S(1)}, u32[]{:S(2)}, u32[]{:S(2)}) async-start(bf16[16,48,128]{2,1,0:T(8,128)(2,1)} %get-tuple-element.14), calls=%async_computation | async-start | bytes 393216 | tf_op jit(solution)/shard_map/all_to_all | solution.py:332
  20.0 42.8 %collective-permute-start = (bf16[8,256,128]{2,1,0:T(8,128)(2,1)S(1)}, bf16[8,256,128]{2,1,0:T(8,128)(2,1)S(1)}, u32[]{:S(2)}, u32[]{:S(2)}) collective-permute-start(bf16[8,256,128]{2,1,0:T(8,128)(2,1)S(1)} %shard_map.140.joined.own), channel_id=1, source_target_pairs={{0,2},{2,4},{4,6},{6,8},{8,10},{10,12},{12,14},{14,16},{16,18},{18... | collective-permute-start | bytes 1572872 | tf_op jit(solution)/shard_map/ppermute | solution.py:310
  23.3 39.5 %collective-permute-start.1 = (bf16[8,256,128]{2,1,0:T(8,128)(2,1)S(1)}, bf16[8,256,128]{2,1,0:T(8,128)(2,1)}, u32[]{:S(2)}, u32[]{:S(2)}) collective-permute-start(bf16[8,256,128]{2,1,0:T(8,128)(2,1)S(1)} %shard_map.140.joined.own), channel_id=1, source_target_pairs={{2,0},{4,2},{6,4},{8,6},{10,8},{12,10},{14,12},{16,14},{18,16},{20... | collective-permute-start | bytes 1572872 | tf_op jit(solution)/shard_map/ppermute | solution.py:311
  28.1 27.3 %all-to-all-start.1 = ((bf16[16,16,128]{2,1,0:T(8,128)(2,1)}), bf16[16,16,128]{2,1,0:T(8,128)(2,1)S(1)}, u32[]{:S(2)}, u32[]{:S(2)}) async-start(bf16[16,16,128]{2,1,0:T(8,128)(2,1)} %shard_map.142), calls=%async_computation.1 | async-start | bytes 131072 | tf_op jit(solution)/shard_map/all_to_all | solution.py:369
  46.5 1.0 %copy-start.5 = (bf16[16,128,64]{2,1,0:T(8,128)(2,1)S(1)}, bf16[16,128,64]{2,1,0:T(8,128)(2,1)}, u32[]{:S(2)}) copy-start(bf16[16,128,64]{2,1,0:T(8,128)(2,1)} %copy.21.top_skel) | copy-start | bytes 786436
  47.6 0.9 %copy-start.10 = (bf16[1,4,2,128,64]{4,3,2,1,0:T(8,128)(2,1)S(1)}, bf16[1,4,2,128,64]{4,3,2,1,0:T(8,128)(2,1)}, u32[]{:S(2)}) copy-start(bf16[1,4,2,128,64]{4,3,2,1,0:T(8,128)(2,1)} %copy.20.chain_skel) | copy-start | bytes 393220
  49.5 1.2 %copy-start.15 = (f32[14,128,128]{2,1,0:T(8,128)S(1)}, f32[14,128,128]{2,1,0:T(8,128)}, u32[]{:S(2)}) copy-start(f32[14,128,128]{2,1,0:T(8,128)} %copy-done.14) | copy-start | bytes 2752516
  50.6 14.8 %copy-start.18 = (s32[8,12]{1,0:T(8,128)S(1)}, s32[8,12]{1,0:T(8,128)}, u32[]{:S(2)}) copy-start(s32[8,12]{1,0:T(8,128)} %ids.3) | copy-start | bytes 1156
  50.6 14.8 %copy-start.19 = (s32[8,12]{1,0:T(8,128)S(1)}, s32[8,12]{1,0:T(8,128)}, u32[]{:S(2)}) copy-start(s32[8,12]{1,0:T(8,128)} %valid.3) | copy-start | bytes 1156
  55.4 1.0 %copy-start.7 = (bf16[16,128,128]{2,1,0:T(8,128)(2,1)S(1)}, bf16[16,128,128]{2,1,0:T(8,128)(2,1)}, u32[]{:S(2)}) copy-start(bf16[16,128,128]{2,1,0:T(8,128)(2,1)} %copy-done.6) | copy-start | bytes 1572868
  57.3 16.8 %all-to-all-start.2 = ((bf16[16,48,128]{2,1,0:T(8,128)(2,1)}), bf16[16,48,128]{2,1,0:T(8,128)(2,1)S(1)}, u32[]{:S(2)}, u32[]{:S(2)}) async-start(bf16[16,48,128]{2,1,0:T(8,128)(2,1)} %shard_map.144), calls=%async_computation.2 | async-start | bytes 393216 | tf_op jit(solution)/shard_map/all_to_all | solution.py:373
  72.2 1.2 %copy-start.12 = (bf16[24,256,128]{2,1,0:T(8,128)(2,1)}, bf16[24,256,128]{2,1,0:T(8,128)(2,1)S(1)}, u32[]{:S(2)}) copy-start(bf16[24,256,128]{2,1,0:T(8,128)(2,1)S(1)} %get-tuple-element.22.right) | copy-start | bytes 4718596
  74.2 1.2 %copy-start.4 = (f32[14,128,128]{2,1,0:T(8,128)S(1)}, f32[14,128,128]{2,1,0:T(8,128)}, u32[]{:S(2)}) copy-start(f32[14,128,128]{2,1,0:T(8,128)} %copy-done.3) | copy-start | bytes 2752516
  75.4 7.2 %copy-start.13 = (bf16[24,256,128]{2,1,0:T(8,128)(2,1)S(1)}, bf16[24,256,128]{2,1,0:T(8,128)(2,1)}, u32[]{:S(2)}) copy-start(bf16[24,256,128]{2,1,0:T(8,128)(2,1)} %copy-done.12) | copy-start | bytes 4718596
  75.4 7.2 %copy-start.17 = (bf16[8,256,128]{2,1,0:T(8,128)(2,1)S(1)}, bf16[8,256,128]{2,1,0:T(8,128)(2,1)}, u32[]{:S(2)}) copy-start(bf16[8,256,128]{2,1,0:T(8,128)(2,1)} %copy-done.16) | copy-start | bytes 1572868
  78.2 10.3 %copy-start.9 = (f32[4,256,128]{2,1,0:T(8,128)S(1)}, f32[4,256,128]{2,1,0:T(8,128)}, u32[]{:S(2)}) copy-start(f32[4,256,128]{2,1,0:T(8,128)} %copy-done.8) | copy-start | bytes 1572868
  78.2 12.5 %collective-permute-start.2 = (bf16[8,128,128]{2,1,0:T(8,128)(2,1)}, bf16[8,128,128]{2,1,0:T(8,128)(2,1)S(1)}, u32[]{:S(2)}, u32[]{:S(2)}) collective-permute-start(bf16[8,128,128]{2,1,0:T(8,128)(2,1)} %get-tuple-element.25), channel_id=1, source_target_pairs={{0,1},{1,0},{2,3},{3,2},{4,5},{5,4},{6,7},{7,6},{8,9},{9,8},{10,11... | collective-permute-start | bytes 786440 | tf_op jit(solution)/shard_map/ppermute | solution.py:380
  (5 other events, 4.3 us)

commit v2 on v1

v2 whole, which is shorter than its diff:
```python
import math

import jax
import jax.numpy as jnp
from jax import lax
from jax.experimental import pallas as pl
from jax.experimental.pallas import tpu as pltpu
from jax.sharding import PartitionSpec as P

F32 = jnp.float32
BF16 = jnp.bfloat16

LEVELS = 4
MEMBERS = 16
GROUPS = 16
SLAB = 48
SHARE = 8
LEAVES = 8
ROWS = 256
RANK = 128
DIM = 64
SLOTS = 12

VMEM = pl.BlockSpec(memory_space=pltpu.VMEM)
ANY = pl.BlockSpec(memory_space=pl.ANY)
HBM = pl.BlockSpec(memory_space=pltpu.HBM)
NN = (((1,), (0,)), ((), ()))
NT = (((1,), (1,)), ((), ()))


def mm(a, b, dims=NN):
    return lax.dot_general(a, b, dims, preferred_element_type=F32)


def split(a):
    high = a.astype(BF16)
    return high, (a - high.astype(F32)).astype(BF16)


def mm2(a, b, dims=NN):
    high, low = split(a)
    return mm(high, b, dims) + mm(low, b, dims)


def lanes(rows, width=128):
    return lax.broadcasted_iota(jnp.int32, (rows, width), 1)


def extended(pts, left, right):
    wide = pts.astype(F32)
    half = -0.5 * jnp.sum(wide * wide, axis=0, keepdims=True)
    first = half.astype(BF16).astype(F32)
    rest = half - first
    second = rest.astype(BF16).astype(F32)
    third = rest - second
    row = lax.broadcasted_iota(jnp.int32, (16, pts.shape[1]), 0)
    out = []
    for want, low, ones in ((left, 0, 3), (right, 3, 0)):
        if not want:
            continue
        value = jnp.where((row >= ones) & (row < ones + 3), 1.0, 0.0)
        for offset, term in enumerate((first, second, third)):
            value = jnp.where(row == low + offset, term, value)
        blank = jnp.zeros((128 - DIM - 16, pts.shape[1]), F32)
        out.append(jnp.concatenate([wide, value, blank], axis=0).astype(BF16))
    return out


EXPO = 4.0 / (DIM * math.log(2.0))


def kappa(left_pts, right_pts):
    (left,) = extended(left_pts, True, False)
    (right,) = extended(right_pts, False, True)
    return jnp.exp2(mm(left.T, right) * EXPO)


def call(kernel, outs, specs, scratch=(), cost=(0, 0, 0), places=None, room=60):
    return pl.pallas_call(
        kernel,
        out_shape=outs,
        in_specs=specs,
        out_specs=places or jax.tree.map(lambda _: VMEM, outs),
        scratch_shapes=list(scratch),
        compiler_params=pltpu.CompilerParams(vmem_limit_bytes=int(room * 2**20)),
        cost_estimate=pl.CostEstimate(
            flops=cost[0], bytes_accessed=cost[1], transcendentals=cost[2]
        ),
    )


def sds(shape, dtype):
    return jax.ShapeDtypeStruct(shape, dtype)


def fetch(pairs, sems):
    copies = [
        pltpu.make_async_copy(source, target, sems.at[index])
        for index, (source, target) in enumerate(pairs)
    ]
    for copy in copies:
        copy.start()
    return [copy.wait for copy in copies]


def rise_kernel(
    points,
    inputs,
    order,
    cot,
    basis,
    transfer,
    chain,
    joined,
    coeffs,
    send,
    raw_v,
    order_v,
    cot_v,
    basis_v,
    transfer_v,
    chain_v,
    joined_v,
    coeffs_v,
    source_v,
    in_sems,
    joined_sems,
    coeff_sems,
):
    waits = fetch(
        (
            (points, raw_v.at[pl.ds(DIM, DIM)]),
            (inputs, raw_v.at[pl.ds(0, DIM)]),
            (order, order_v),
            (cot, cot_v),
            (basis, basis_v),
            (transfer, transfer_v),
            (chain, chain_v),
        ),
        in_sems,
    )
    device = lax.axis_index("pts")
    base = device * (LEAVES * ROWS)
    for wait in waits[:3]:
        wait()
    for index in range(4):
        low = raw_v[:, pl.ds(index * 512, ROWS)].T
        high = raw_v[:, pl.ds(index * 512 + ROWS, ROWS)].T
        source_v[index] = jnp.concatenate([low, high], axis=1)
    lane = lanes(ROWS, ROWS).astype(F32).astype(BF16)
    one, zero = jnp.ones((), BF16), jnp.zeros((), BF16)
    joined_copies = []
    for leaf in range(LEAVES):
        pieces = [order_v[pl.ds(2 * leaf + index, 1), :] - base for index in range(2)]
        row = jnp.concatenate(pieces, axis=1)
        low = jnp.bitwise_and(row, 255).astype(F32)
        high = jnp.right_shift(row, 8).astype(F32)
        low = jnp.broadcast_to(low, (128, ROWS)).T.astype(BF16)
        high = jnp.broadcast_to(high, (128, ROWS)).T
        hit = jnp.where(jnp.concatenate([low, low], axis=1) == lane, one, zero)
        value = jnp.zeros((ROWS, 128), F32)
        for index in range(4):
            found = mm(hit, source_v[index])
            value = jnp.where(high == 2.0 * index, found[:, :128], value)
            value = jnp.where(high == 2.0 * index + 1.0, found[:, 128:], value)
        joined_v[leaf] = value.astype(BF16)
        copy = pltpu.make_async_copy(joined_v.at[leaf], joined.at[leaf], joined_sems.at[leaf])
        copy.start()
        joined_copies.append(copy)
    for wait in waits[3:]:
        wait()
    now = []
    for leaf in range(LEAVES):
        theirs = cot_v[:, pl.ds(leaf * ROWS, ROWS)]
        pair = jnp.concatenate([joined_v[leaf].T[:DIM], theirs], axis=0)
        now.append(mm(pair, basis_v[leaf]))
    offset, done, level = 0, 0, 0
    coeff_copies = []
    while len(now) > 1:
        for node, value in enumerate(now):
            coeffs_v[done + node] = value
        span = pl.ds(done, len(now))
        copy = pltpu.make_async_copy(coeffs_v.at[span], coeffs.at[span], coeff_sems.at[level])
        copy.start()
        coeff_copies.append(copy)
        done += len(now)
        level += 1
        now = [
            mm2(jnp.concatenate([now[2 * n], now[2 * n + 1]], axis=1), transfer_v[offset + n])
            for n in range(len(now) // 2)
        ]
        offset += len(now)
    value = now[0]
    parts = [value]
    for level in range(LEVELS):
        bit = jnp.bitwise_and(jnp.right_shift(device, level), 1)
        half = chain_v[0, level, pl.ds(pl.multiple_of(bit * RANK, RANK), RANK), :]
        value = mm2(value, half)
        parts.append(value)
    parts = [part.reshape(MEMBERS, SHARE, RANK) for part in parts]
    parts.append(jnp.zeros((MEMBERS, SLAB - 5 * SHARE, RANK), F32))
    send[...] = jnp.concatenate(parts, axis=1).astype(BF16)
    for copy in joined_copies + coeff_copies:
        copy.wait()


def couple_kernel(
    coeffs,
    joined,
    cot,
    leaf_skel,
    local_skel,
    chain_skel,
    top_skel,
    after,
    couplings,
    chain_k,
    both,
    top_k,
    coeffs_v,
    joined_v,
    cot_v,
    leaf_v,
    local_v,
    skel_v,
    top_v,
    couplings_v,
    chain_k_v,
    both_v,
    sems,
    out_sems,
):
    waits = fetch(
        (
            (cot, cot_v),
            (joined, joined_v),
            (chain_skel, skel_v),
            (leaf_skel, leaf_v),
            (local_skel, local_v),
            (coeffs, coeffs_v),
            (top_skel, top_v),
        ),
        sems,
    )
    device = lax.axis_index("pts")
    for wait in waits[:3]:
        wait()
    for leaf in range(LEAVES):
        theirs = cot_v[:, pl.ds(leaf * ROWS, ROWS)].T
        both_v[leaf] = jnp.concatenate([joined_v[leaf][:, :DIM], theirs], axis=1)
    done = fetch(((both_v, both),), out_sems)
    for level in range(LEVELS):
        bit = jnp.bitwise_and(jnp.right_shift(device, level), 1)
        chain_k_v[level] = kappa(skel_v[0, level, 1 - bit], skel_v[0, level, bit]).astype(BF16)
    done += fetch(((chain_k_v, chain_k),), out_sems.at[pl.ds(1, 1)])
    for wait in waits[3:6]:
        wait()
    for node in range(0, 14, 2):
        if node < 8:
            even, odd = leaf_v[node], leaf_v[node + 1]
        else:
            even, odd = local_v[node - 8], local_v[node - 7]
        high, low = split(kappa(even, odd))
        for target, other, dims in ((node, node + 1, NT), (node + 1, node, NN)):
            value = coeffs_v[other]
            couplings_v[target] = mm2(value, high, dims) + mm(value.astype(BF16), low, dims)
    done += fetch(((couplings_v, couplings),), out_sems.at[pl.ds(2, 1)])
    waits[6]()
    group = jnp.right_shift(device, LEVELS)
    mine = top_v[group]
    for other in range(GROUPS):
        value = kappa(top_v[other], mine)
        top_k[other] = jnp.where(group == other, 0.0, value).astype(BF16)
    for wait in done:
        wait()


def part(received, member, index):
    return received[member].astype(F32)[index * SHARE : (index + 1) * SHARE]


def level_sums(received, index):
    sums = [part(received, member, index) for member in range(MEMBERS)]
    for _ in range(index):
        sums = [sums[2 * n] + sums[2 * n + 1] for n in range(len(sums) // 2)]
    return sums


def total_kernel(received, send):
    total = level_sums(received, LEVELS)[0]
    total = jnp.concatenate([total, jnp.zeros_like(total)], axis=0).astype(BF16)
    for group in range(GROUPS):
        send[group] = total


def reply_kernel(received, totals, top_k, reply):
    flat = jnp.concatenate([totals[group] for group in range(GROUPS)], axis=1)
    field = mm(flat, top_k[...].reshape(GROUPS * RANK, RANK))[:SHARE]
    levels = [level_sums(received, level) for level in range(LEVELS)]
    blank = jnp.zeros((SHARE, RANK), F32)
    for member in range(MEMBERS):
        rows = [levels[level][(member >> level) ^ 1] for level in range(LEVELS)]
        reply[member] = jnp.concatenate(rows + [field, blank], axis=0).astype(BF16)


def down_kernel(
    replies,
    chain_k,
    chain,
    transfer,
    couplings,
    both,
    basis,
    near,
    give,
    output,
    keep,
    replies_v,
    chain_k_v,
    chain_v,
    transfer_v,
    couplings_v,
    both_v,
    basis_v,
    near_v,
    give_v,
    output_v,
    keep_v,
    sems,
    out_sems,
):
    waits = fetch(
        (
            (replies, replies_v),
            (chain_k, chain_k_v),
            (chain, chain_v),
            (transfer, transfer_v),
            (couplings, couplings_v),
            (both, both_v),
            (basis, basis_v),
            (near, near_v),
        ),
        sems,
    )
    device, core = lax.axis_index("pts"), lax.axis_index("rhs")
    for wait in waits[:3]:
        wait()
    table = replies_v[...].astype(F32)
    got = [
        table[:, index * SHARE : (index + 1) * SHARE].reshape(RANK, RANK)
        for index in range(LEVELS + 1)
    ]
    field = got[LEVELS]
    for level in reversed(range(LEVELS)):
        bit = jnp.bitwise_and(jnp.right_shift(device, level), 1)
        half = chain_v[0, level, pl.ds(pl.multiple_of(bit * RANK, RANK), RANK), :]
        field = mm(got[level].astype(BF16), chain_k_v[level]) + mm2(field, half, NT)
    waits[3]()
    waits[4]()
    now = [field]
    for start, count, offset in ((6, 1, 12), (4, 2, 8), (0, 4, 0)):
        below = []
        for node in range(count):
            spread = mm2(now[node], transfer_v[start + node], NT)
            for child in range(2):
                rows = spread[:, child * RANK : (child + 1) * RANK]
                below.append(couplings_v[offset + 2 * node + child] + rows)
        now = below
    for wait in waits[5:]:
        wait()
    away = pl.multiple_of((1 - core) * RANK, RANK)
    stay = pl.multiple_of(core * RANK, RANK)
    for leaf in range(LEAVES):
        swapped = jnp.concatenate([now[leaf][DIM:], now[leaf][:DIM]], axis=0)
        high, low = split(swapped)
        for target, first in ((give_v, away), (keep_v, stay)):
            rows = both_v[leaf, pl.ds(first, RANK), :]
            target[leaf] = (mm(rows, high) + mm(rows, low)).astype(target.dtype)
    done = fetch(((give_v, give), (keep_v, keep)), out_sems)
    for leaf in range(LEAVES):
        high, low = split(now[leaf])
        far = mm(basis_v[leaf], high, NT) + mm(basis_v[leaf], low, NT)
        total = (near_v[leaf] + far).astype(BF16)
        output_v[:, pl.ds(leaf * ROWS, ROWS)] = total.T[:DIM]
    done += fetch(((output_v, output),), out_sems.at[pl.ds(2, 1)])
    for wait in done:
        wait()


def near_kernel(
    ids,
    valid,
    below,
    own,
    above,
    after,
    near,
    ids_v,
    valid_v,
    below_v,
    above_v,
    own_v,
    left,
    right,
    values,
    near_v,
    sems,
    near_sems,
):
    waits = fetch(
        (
            (below, below_v),
            (own, own_v),
            (above, above_v),
            (ids, ids_v),
            (valid, valid_v),
        ),
        sems,
    )
    for index, block in enumerate((below_v, own_v, above_v)):
        waits[index]()
        for leaf in range(LEAVES):
            value = block[leaf]
            made = extended(value.T[DIM:], index == 1, True)
            right[index * LEAVES + leaf] = made[-1]
            values[index * LEAVES + leaf] = value
            if index == 1:
                left[leaf] = made[0].T
    device = lax.axis_index("pts")
    shift = (device - 1) * LEAVES

    def body(leaf, carry):
        mine = left[leaf]
        total = jnp.zeros((ROWS, 128), F32)
        for slot in range(SLOTS):
            where = ids_v[leaf, slot] - shift
            used = jnp.full((1, 128), valid_v[leaf, slot], jnp.int32).astype(F32).astype(BF16)
            tile = jnp.exp2(mm(mine, right[where]) * EXPO).astype(BF16)
            total = total + mm(tile, values[where] * used)
        near_v[leaf] = total
        pltpu.make_async_copy(near_v.at[leaf], near.at[leaf], near_sems.at[leaf]).start()
        return carry

    waits[3]()
    waits[4]()
    lax.fori_loop(0, LEAVES, body, 0)
    for leaf in range(LEAVES):
        pltpu.make_async_copy(near_v.at[leaf], near.at[leaf], near_sems.at[leaf]).wait()


def local(
    points,
    inputs,
    cotangent,
    order,
    near_ids,
    near_valid,
    leaf_basis,
    local_transfer,
    chain_transfer,
    leaf_skel,
    local_skel,
    chain_skel,
    top_skel,
):
    count = lax.axis_size("pts")
    block = (LEAVES, ROWS, 128)

    points, inputs, cot = points.T, inputs.T, cotangent.T
    leaf_skel, local_skel, chain_skel, top_skel = (
        jnp.swapaxes(skel, -1, -2) for skel in (leaf_skel, local_skel, chain_skel, top_skel)
    )
    order = order.reshape(2 * LEAVES, 128)
    joined, coeffs, send = call(
        rise_kernel,
        (
            sds(block, BF16),
            sds((14, RANK, RANK), F32),
            sds((MEMBERS, SLAB, RANK), BF16),
        ),
        [HBM] * 7,
        [
            pltpu.VMEM((2 * DIM, LEAVES * ROWS), BF16),
            pltpu.VMEM((2 * LEAVES, 128), jnp.int32),
            pltpu.VMEM((DIM, LEAVES * ROWS), BF16),
            pltpu.VMEM(block, BF16),
            pltpu.VMEM(local_transfer.shape, BF16),
            pltpu.VMEM(chain_transfer.shape, BF16),
            pltpu.VMEM(block, BF16),
            pltpu.VMEM((14, RANK, RANK), F32),
            pltpu.VMEM((4, ROWS, 256), BF16),
            pltpu.SemaphoreType.DMA((7,)),
            pltpu.SemaphoreType.DMA((LEAVES,)),
            pltpu.SemaphoreType.DMA((3,)),
        ],
        places=(HBM, HBM, VMEM),
    )(points, inputs, order, cot, leaf_basis, local_transfer, chain_transfer)

    groups = [[g * MEMBERS + i for i in range(MEMBERS)] for g in range(GROUPS)]
    across = [[g * MEMBERS + i for g in range(GROUPS)] for i in range(MEMBERS)]
    received = lax.all_to_all(send, "pts", 0, 0, axis_index_groups=groups, tiled=True)

    upward = [(i, i + 1) for i in range(count - 1)]
    below = lax.ppermute(joined, "pts", upward)
    above = lax.ppermute(joined, "pts", [(b, a) for a, b in upward])

    total = call(
        total_kernel, sds((GROUPS, 2 * SHARE, RANK), BF16), [VMEM], room=8
    )(received)
    totals = lax.all_to_all(total, "pts", 0, 0, axis_index_groups=across, tiled=True)

    tree = (14, RANK, RANK)
    square = (LEAVES, RANK, RANK)
    links = (LEVELS, RANK, RANK)
    couplings, chain_k, both, top_k = call(
        couple_kernel,
        (sds(tree, F32), sds(links, BF16), sds(block, BF16), sds((GROUPS, RANK, RANK), BF16)),
        [HBM] * 7 + [ANY],
        [
            pltpu.VMEM(tree, F32),
            pltpu.VMEM(block, BF16),
            pltpu.VMEM((DIM, LEAVES * ROWS), BF16),
            pltpu.VMEM(leaf_skel.shape, BF16),
            pltpu.VMEM(local_skel.shape, BF16),
            pltpu.VMEM(chain_skel.shape, BF16),
            pltpu.VMEM(top_skel.shape, BF16),
            pltpu.VMEM(tree, F32),
            pltpu.VMEM(links, BF16),
            pltpu.VMEM(block, BF16),
            pltpu.SemaphoreType.DMA((7,)),
            pltpu.SemaphoreType.DMA((3,)),
        ],
        cost=(2 * 10**9, 4 * 10**6, 10**6),
        places=(HBM, HBM, HBM, VMEM),
    )(coeffs, joined, cot, leaf_skel, local_skel, chain_skel, top_skel, total)

    reply = call(
        reply_kernel, sds((MEMBERS, SLAB, RANK), BF16), [VMEM] * 3, room=8
    )(received, totals, top_k)
    replies = lax.all_to_all(reply, "pts", 0, 0, axis_index_groups=groups, tiled=True)

    near = call(
        near_kernel,
        sds((LEAVES, ROWS, 128), F32),
        [HBM] * 5 + [ANY],
        [
            pltpu.SMEM((LEAVES, SLOTS), jnp.int32),
            pltpu.SMEM((LEAVES, SLOTS), jnp.int32),
            pltpu.VMEM(block, BF16),
            pltpu.VMEM(block, BF16),
            pltpu.VMEM(block, BF16),
            pltpu.VMEM(block, BF16),
            pltpu.VMEM((3 * LEAVES, 128, ROWS), BF16),
            pltpu.VMEM((3 * LEAVES, ROWS, 128), BF16),
            pltpu.VMEM((LEAVES, ROWS, 128), F32),
            pltpu.SemaphoreType.DMA((5,)),
            pltpu.SemaphoreType.DMA((LEAVES,)),
        ],
        cost=(LEAVES * 4 * 10**8, 4 * 10**6, LEAVES * 800000),
        places=HBM,
        room=60,
    )(near_ids, near_valid, below, joined, above, reply)

    give, output, keep = call(
        down_kernel,
        (sds(square, BF16), sds((DIM, LEAVES * ROWS), BF16), sds(square, F32)),
        [HBM] * 8,
        [
            pltpu.VMEM((MEMBERS, SLAB, RANK), BF16),
            pltpu.VMEM(links, BF16),
            pltpu.VMEM(chain_transfer.shape, BF16),
            pltpu.VMEM(local_transfer.shape, BF16),
            pltpu.VMEM(tree, F32),
            pltpu.VMEM(block, BF16),
            pltpu.VMEM(block, BF16),
            pltpu.VMEM(block, F32),
            pltpu.VMEM(square, BF16),
            pltpu.VMEM((DIM, LEAVES * ROWS), BF16),
            pltpu.VMEM(square, F32),
            pltpu.SemaphoreType.DMA((8,)),
            pltpu.SemaphoreType.DMA((3,)),
        ],
        places=(HBM,) * 3,
        room=60,
    )(
        replies,
        chain_k,
        chain_transfer,
        local_transfer,
        couplings,
        both,
        leaf_basis,
        near,
    )
    got = lax.ppermute(give, "rhs", [(0, 1), (1, 0)])
    basis_grad = (keep + got.astype(F32)).astype(BF16)
    return output.T, basis_grad


def solution(mesh):
    placed = (
        P("pts", None),
        P("pts", "rhs"),
        P("pts", "rhs"),
        P("pts"),
        P("pts", None),
        P("pts", None),
        P("pts", None, None),
        P("pts", None, None),
        P("pts", None, None, None),
        P("pts", None, None),
        P("pts", None, None),
        P("pts", None, None, None, None),
        P(),
    )
    return jax.shard_map(
        local,
        mesh=mesh,
        in_specs=placed,
        out_specs=(P("pts", "rhs"), P("pts", "rhs", None)),
        check_vma=False,
    )
```

time: 92.4 us -> 80 us (0.87)
  local copies, waits for them, and re-layouts: 21.2 us -> 3.25 us
  waiting for transfers between devices: 2.95 us -> 8.32 us
  Pallas kernels: 28.8 us -> 27.6 us
  starting transfers between devices: 36.8 us -> 37.8 us
    unnamed x54 -> x8, local copies, waits for them, and re-layouts: 21.2 us -> 3.25 us
    all_to_all x1, waiting for transfers between devices: 0.01 us -> 4.03 us  [local(): lax.all_to_all(total, 'pts', 0, 0, axis_index_groups=across, tiled=True)]
    ppermute x1, waiting for transfers between devices: 0.01 us -> 1.35 us  [local(): got = lax.ppermute(give, 'rhs', [(0, 1), (1, 0)])]
    pallas_call x10 -> x6, Pallas kernels: 28.8 us -> 27.6 us  [the longest x1 12.3 us: local(): call(near_kernel, sds((LEAVES, ROWS, 128), F32), [HBM] * 5 + [ANY], [pltp...]
    convert_element_type x1, other arithmetic: 0.76 us -> 1.81 us  [local(): basis_grad = (keep + got.astype(F32)).astype(BF16)]
    ppermute x1, starting transfers between devices: 4.38 us -> 5.41 us  [local(): got = lax.ppermute(give, 'rhs', [(0, 1), (1, 0)])]
  transfers between devices with their start and end apart: 6 -> 6, of which waited for: 1 -> 3; matrix products, arithmetic and copies ran while one was open for 7% -> 0% of each run, Pallas kernels for 22% -> 24%
where the time goes in v2:
time: 80 us; the launch traced here: 79.5 us
  starting transfers between devices  37.8 us (47%)
  Pallas kernels  27.6 us (34%)
  waiting for transfers between devices  8.32 us (10%)
  local copies, waits for them, and re-layouts  3.25 us (4%)
  other arithmetic  1.81 us (2%)
    all_to_all x1, starting transfers between devices, local(): lax.all_to_all(total, 'pts', 0, 0, axis_index_groups=across, tiled=True)  12.8 us
    pallas_call x1, Pallas kernels, local(): call(near_kernel, sds((LEAVES, ROWS, 128), F32), [HBM] * 5 + [ANY], [pltp...  12.3 us
    all_to_all x1, starting transfers between devices, local(): lax.all_to_all(send, 'pts', 0, 0, axis_index_groups=groups, tiled=True)  9.58 us
    all_to_all x1, starting transfers between devices, local(): lax.all_to_all(reply, 'pts', 0, 0, axis_index_groups=groups, tiled=True)  5.42 us
    ppermute x1, starting transfers between devices, local(): got = lax.ppermute(give, 'rhs', [(0, 1), (1, 0)])  5.41 us
    pallas_call x1, Pallas kernels, local(): call(couple_kernel, (sds(tree, F32), sds(links, BF16), sds(block, BF16),...  5.03 us
    pallas_call x1, Pallas kernels, local(): call(rise_kernel, (sds(block, BF16), sds((14, RANK, RANK), F32), sds((MEM...  4.65 us
    pallas_call x1, Pallas kernels, local(): call(down_kernel, (sds(square, BF16), sds((DIM, LEAVES * ROWS), BF16), sd...  4.11 us
  transfers between devices with their start and end apart: 6, of which 3 were waited for; matrix products, arithmetic and copies ran while one was open for 0% of the time, Pallas kernels for 24%

profile of v2, /device:TPU:1, one launch (start us, length us, event | category | flops | bytes accessed | tf_op | source)
XLA Modules:
  0.0 79.5 jit_solution(12503936483245912560)
XLA Ops:
  0.6 4.6 %shard_map.140 = (bf16[8,256,128]{2,1,0:T(8,128)(2,1)}, f32[14,128,128]{2,1,0:T(8,128)}, bf16[16,48,128]{2,1,0:T(8,128)(2,1)}) custom-call(bf16[64,2048]{1,0:T(8,128)(2,1)} %bitcast.9, bf16[64,2048]{1,0:T(8,128)(2,1)} %bitcast.10, s32[16,128]{1,0:T(8,128)} %bitcast.13, bf16[64,2048]{1,0:T(8,128)(2,1)} %bitcast.11, bf16[8,256,128]{2,1,0:T(8,128)(2,1)} %basis.3, ...), custom_call_target="tpu_custom_call" | custom-call | tf_op jit(solution)/shard_map/pallas_call | solution.py:474
  5.3 9.6 %all-to-all-start = ((bf16[16,48,128]{2,1,0:T(8,128)(2,1)}), bf16[16,48,128]{2,1,0:T(8,128)(2,1)S(1)}, u32[]{:S(2)}, u32[]{:S(2)}) async-start(bf16[16,48,128]{2,1,0:T(8,128)(2,1)} %get-tuple-element.12), calls=%async_computation | async-start | bytes 393216 | tf_op jit(solution)/shard_map/all_to_all | solution.py:501
  14.9 3.3 %collective-permute-start = (bf16[8,256,128]{2,1,0:T(8,128)(2,1)}, bf16[8,256,128]{2,1,0:T(8,128)(2,1)S(1)}, u32[]{:S(2)}, u32[]{:S(2)}) collective-permute-start(bf16[8,256,128]{2,1,0:T(8,128)(2,1)} %get-tuple-element.14.joined.own), channel_id=1, source_target_pairs={{0,2},{2,4},{4,6},{6,8},{8,10},{10,12},{12,14},{14,16},{16,18},{18... | collective-permute-start | bytes 1572872 | tf_op jit(solution)/shard_map/ppermute | solution.py:504
  18.2 1.3 %collective-permute-start.1 = (bf16[8,256,128]{2,1,0:T(8,128)(2,1)}, bf16[8,256,128]{2,1,0:T(8,128)(2,1)S(1)}, u32[]{:S(2)}, u32[]{:S(2)}) collective-permute-start(bf16[8,256,128]{2,1,0:T(8,128)(2,1)} %get-tuple-element.14.joined.own), channel_id=1, source_target_pairs={{2,0},{4,2},{6,4},{8,6},{10,8},{12,10},{14,12},{16,14},{18,16},{20... | collective-permute-start | bytes 1572872 | tf_op jit(solution)/shard_map/ppermute | solution.py:505
  19.5 2.9 %all-to-all-done.received = bf16[16,48,128]{2,1,0:T(8,128)(2,1)S(1)} async-done(((bf16[16,48,128]{2,1,0:T(8,128)(2,1)}), bf16[16,48,128]{2,1,0:T(8,128)(2,1)S(1)}, u32[]{:S(2)}, u32[]{:S(2)}) %all-to-all-start) | async-done | bytes 196640 | tf_op jit(solution)/shard_map/all_to_all | solution.py:501
  22.4 0.6 shard_map.141.after
  23.0 12.8 %all-to-all-start.1 = ((bf16[16,16,128]{2,1,0:T(8,128)(2,1)}), bf16[16,16,128]{2,1,0:T(8,128)(2,1)S(1)}, u32[]{:S(2)}, u32[]{:S(2)}) async-start(bf16[16,16,128]{2,1,0:T(8,128)(2,1)} %shard_map.141.after), calls=%async_computation.1 | async-start | bytes 131072 | tf_op jit(solution)/shard_map/all_to_all | solution.py:510
  35.8 5.0 %shard_map.142 = (f32[14,128,128]{2,1,0:T(8,128)}, bf16[4,128,128]{2,1,0:T(8,128)(2,1)}, bf16[8,256,128]{2,1,0:T(8,128)(2,1)}, bf16[16,128,128]{2,1,0:T(8,128)(2,1)}) custom-call(f32[14,128,128]{2,1,0:T(8,128)} %get-tuple-element.13.coeffs, bf16[8,256,128]{2,1,0:T(8,128)(2,1)} %get-tuple-element.14.joined.own, bf16[64,2048]{1,0:T(8,128)(2,1)} %bitcast.12, ...), custom_call_target="tpu_custom_call" | custom-call | flops 2000000000 | bytes 4000000 | tf_op jit(solution)/shard_map/pallas_call | solution.py:515
  40.9 4.0 %all-to-all-done.1.totals = bf16[16,16,128]{2,1,0:T(8,128)(2,1)S(1)} async-done(((bf16[16,16,128]{2,1,0:T(8,128)(2,1)}), bf16[16,16,128]{2,1,0:T(8,128)(2,1)S(1)}, u32[]{:S(2)}, u32[]{:S(2)}) %all-to-all-start.1) | async-done | bytes 65568 | tf_op jit(solution)/shard_map/all_to_all | solution.py:510
  44.9 1.0 %copy-done = bf16[16,128,128]{2,1,0:T(8,128)(2,1)S(1)} copy-done((bf16[16,128,128]{2,1,0:T(8,128)(2,1)S(1)}, bf16[16,128,128]{2,1,0:T(8,128)(2,1)}, u32[]{:S(2)}) %copy-start) | copy-done | bytes 524312
  45.9 0.9 %shard_map.143.after = bf16[16,48,128]{2,1,0:T(8,128)(2,1)} custom-call(bf16[16,48,128]{2,1,0:T(8,128)(2,1)S(1)} %all-to-all-done.received, bf16[16,16,128]{2,1,0:T(8,128)(2,1)S(1)} %all-to-all-done.1.totals, bf16[16,128,128]{2,1,0:T(8,128)(2,1)S(1)} %copy-done), custom_call_target="tpu_custom_call" | custom-call | tf_op jit(solution)/shard_map/pallas_call | solution.py:537
  46.8 5.4 %all-to-all-start.2 = ((bf16[16,48,128]{2,1,0:T(8,128)(2,1)}), bf16[16,48,128]{2,1,0:T(8,128)(2,1)S(1)}, u32[]{:S(2)}, u32[]{:S(2)}) async-start(bf16[16,48,128]{2,1,0:T(8,128)(2,1)} %shard_map.143.after), calls=%async_computation.2 | async-start | bytes 393216 | tf_op jit(solution)/shard_map/all_to_all | solution.py:540
  52.2 0.0 collective-permute-done.below
  52.2 0.0 copy-start.2
  52.2 0.0 collective-permute-done.1.above
  52.2 0.8 copy-done.2
  53.0 0.8 copy-done.3
  53.8 12.3 %shard_map.144.near = f32[8,256,128]{2,1,0:T(8,128)} custom-call(s32[8,12]{1,0:T(8,128)} %ids.1, s32[8,12]{1,0:T(8,128)} %valid.1, bf16[8,256,128]{2,1,0:T(8,128)(2,1)} %copy-done.2, bf16[8,256,128]{2,1,0:T(8,128)(2,1)} %get-tuple-element.14.joined.own, bf16[8,256,128]{2,1,0:T(8,128)(2,1)} %copy-done.3, bf16[16,48,128]{2,1,0:T(8,128)(2,1)} %shard_map.143.after), custom_call_target="tpu_custom_call" | custom-call | flops 3200000000 | bytes 4000000 | tf_op jit(solution)/shard_map/pallas_call | solution.py:542
  66.1 0.0 all-to-all-done.2.replies
  66.1 0.7 copy-done.1
  66.8 4.1 %shard_map.145 = (bf16[8,128,128]{2,1,0:T(8,128)(2,1)}, bf16[64,2048]{1,0:T(8,128)(2,1)}, f32[8,128,128]{2,1,0:T(8,128)}) custom-call(bf16[16,48,128]{2,1,0:T(8,128)(2,1)} %copy-done.1, bf16[4,128,128]{2,1,0:T(8,128)(2,1)} %get-tuple-element.16.chain_k, bf16[1,4,256,128]{3,2,1,0:T(8,128)(2,1)} %chain.3, bf16[7,256,128]{2,1,0:T(8,128)(2,1)} %transfer.3, ...), custom_call_target="tpu_custom_call" | custom-call | tf_op jit(solution)/shard_map/pallas_call | solution.py:564
  70.9 5.4 %collective-permute-start.2 = (bf16[8,128,128]{2,1,0:T(8,128)(2,1)}, bf16[8,128,128]{2,1,0:T(8,128)(2,1)S(1)}, u32[]{:S(2)}, u32[]{:S(2)}) collective-permute-start(bf16[8,128,128]{2,1,0:T(8,128)(2,1)} %get-tuple-element.21), channel_id=1, source_target_pairs={{0,1},{1,0},{2,3},{3,2},{4,5},{5,4},{6,7},{7,6},{8,9},{9,8},{10,11... | collective-permute-start | bytes 786440 | tf_op jit(solution)/shard_map/ppermute | solution.py:595
  76.3 1.4 %collective-permute-done.2 = bf16[8,128,128]{2,1,0:T(8,128)(2,1)S(1)} collective-permute-done((bf16[8,128,128]{2,1,0:T(8,128)(2,1)}, bf16[8,128,128]{2,1,0:T(8,128)(2,1)S(1)}, u32[]{:S(2)}, u32[]{:S(2)}) %collective-permute-start.2) | collective-permute-done | bytes 262176 | tf_op jit(solution)/shard_map/ppermute | solution.py:595
  77.7 1.8 %add_convert_fusion = bf16[8,128,128]{2,1,0:T(8,128)(2,1)} fusion(f32[8,128,128]{2,1,0:T(8,128)} %get-tuple-element.20, bf16[8,128,128]{2,1,0:T(8,128)(2,1)S(1)} %collective-permute-done.2), kind=kLoop, calls=%fused_computation | loop fusion | flops 393216 | bytes 1048576 | tf_op jit(solution)/shard_map/convert_element_type | solution.py:596
  (3 shorter events, 0.0 us)
Async XLA Ops:
  5.3 17.1 %all-to-all-start = ((bf16[16,48,128]{2,1,0:T(8,128)(2,1)}), bf16[16,48,128]{2,1,0:T(8,128)(2,1)S(1)}, u32[]{:S(2)}, u32[]{:S(2)}) async-start(bf16[16,48,128]{2,1,0:T(8,128)(2,1)} %get-tuple-element.12), calls=%async_computation | async-start | bytes 393216 | tf_op jit(solution)/shard_map/all_to_all | solution.py:501
  14.9 37.4 %collective-permute-start = (bf16[8,256,128]{2,1,0:T(8,128)(2,1)}, bf16[8,256,128]{2,1,0:T(8,128)(2,1)S(1)}, u32[]{:S(2)}, u32[]{:S(2)}) collective-permute-start(bf16[8,256,128]{2,1,0:T(8,128)(2,1)} %get-tuple-element.14.joined.own), channel_id=1, source_target_pairs={{0,2},{2,4},{4,6},{6,8},{8,10},{10,12},{12,14},{14,16},{16,18},{18... | collective-permute-start | bytes 1572872 | tf_op jit(solution)/shard_map/ppermute | solution.py:504
  18.2 34.1 %collective-permute-start.1 = (bf16[8,256,128]{2,1,0:T(8,128)(2,1)}, bf16[8,256,128]{2,1,0:T(8,128)(2,1)S(1)}, u32[]{:S(2)}, u32[]{:S(2)}) collective-permute-start(bf16[8,256,128]{2,1,0:T(8,128)(2,1)} %get-tuple-element.14.joined.own), channel_id=1, source_target_pairs={{2,0},{4,2},{6,4},{8,6},{10,8},{12,10},{14,12},{16,14},{18,16},{20... | collective-permute-start | bytes 1572872 | tf_op jit(solution)/shard_map/ppermute | solution.py:505
  23.0 21.8 %all-to-all-start.1 = ((bf16[16,16,128]{2,1,0:T(8,128)(2,1)}), bf16[16,16,128]{2,1,0:T(8,128)(2,1)S(1)}, u32[]{:S(2)}, u32[]{:S(2)}) async-start(bf16[16,16,128]{2,1,0:T(8,128)(2,1)} %shard_map.141.after), calls=%async_computation.1 | async-start | bytes 131072 | tf_op jit(solution)/shard_map/all_to_all | solution.py:510
  44.9 1.0 %copy-start = (bf16[16,128,128]{2,1,0:T(8,128)(2,1)S(1)}, bf16[16,128,128]{2,1,0:T(8,128)(2,1)}, u32[]{:S(2)}) copy-start(bf16[16,128,128]{2,1,0:T(8,128)(2,1)} %get-tuple-element.15.top_k) | copy-start | bytes 1572868
  46.8 19.3 %all-to-all-start.2 = ((bf16[16,48,128]{2,1,0:T(8,128)(2,1)}), bf16[16,48,128]{2,1,0:T(8,128)(2,1)S(1)}, u32[]{:S(2)}, u32[]{:S(2)}) async-start(bf16[16,48,128]{2,1,0:T(8,128)(2,1)} %shard_map.143.after), calls=%async_computation.2 | async-start | bytes 393216 | tf_op jit(solution)/shard_map/all_to_all | solution.py:540
  52.2 0.8 copy-start.2
  53.0 0.8 copy-start.3
  66.1 0.7 copy-start.1
  70.9 6.8 %collective-permute-start.2 = (bf16[8,128,128]{2,1,0:T(8,128)(2,1)}, bf16[8,128,128]{2,1,0:T(8,128)(2,1)S(1)}, u32[]{:S(2)}, u32[]{:S(2)}) collective-permute-start(bf16[8,128,128]{2,1,0:T(8,128)(2,1)} %get-tuple-element.21), channel_id=1, source_target_pairs={{0,1},{1,0},{2,3},{3,2},{4,5},{5,4},{6,7},{7,6},{8,9},{9,8},{10,11... | collective-permute-start | bytes 786440 | tf_op jit(solution)/shard_map/ppermute | solution.py:595

commit v3 on v2

--- a/solution.py
+++ b/solution.py
@@ -39,14 +39,15 @@
 
 def mm2(a, b, dims=NN):
     high, low = split(a)
-    return mm(high, b, dims) + mm(low, b, dims)
+    along = dims[0][1][0]
+    return mm(jnp.concatenate([high, low], axis=1), jnp.concatenate([b, b], axis=along), dims)
 
 
 def lanes(rows, width=128):
     return lax.broadcasted_iota(jnp.int32, (rows, width), 1)
 
 
-def extended(pts, left, right):
+def norm_rows(pts, left, right):
     wide = pts.astype(F32)
     half = -0.5 * jnp.sum(wide * wide, axis=0, keepdims=True)
     first = half.astype(BF16).astype(F32)
@@ -61,9 +62,16 @@
         value = jnp.where((row >= ones) & (row < ones + 3), 1.0, 0.0)
         for offset, term in enumerate((first, second, third)):
             value = jnp.where(row == low + offset, term, value)
-        blank = jnp.zeros((128 - DIM - 16, pts.shape[1]), F32)
-        out.append(jnp.concatenate([wide, value, blank], axis=0).astype(BF16))
+        out.append(value)
     return out
+
+
+def extended(pts, left, right):
+    blank = jnp.zeros((128 - DIM - 16, pts.shape[1]), BF16)
+    return [
+        jnp.concatenate([pts, rows.astype(BF16), blank], axis=0)
+        for rows in norm_rows(pts, left, right)
+    ]
 
 
 EXPO = 4.0 / (DIM * math.log(2.0))
@@ -195,7 +203,7 @@
     for level in range(LEVELS):
         bit = jnp.bitwise_and(jnp.right_shift(device, level), 1)
         half = chain_v[0, level, pl.ds(pl.multiple_of(bit * RANK, RANK), RANK), :]
-        value = mm2(value, half)
+        value = mm(value.astype(BF16), half)
         parts.append(value)
     parts = [part.reshape(MEMBERS, SHARE, RANK) for part in parts]
     parts.append(jnp.zeros((MEMBERS, SLAB - 5 * SHARE, RANK), F32))
@@ -211,19 +219,16 @@
     leaf_skel,
     local_skel,
     chain_skel,
-    top_skel,
     after,
     couplings,
     chain_k,
     both,
-    top_k,
     coeffs_v,
     joined_v,
     cot_v,
     leaf_v,
     local_v,
     skel_v,
-    top_v,
     couplings_v,
     chain_k_v,
     both_v,
@@ -238,7 +243,6 @@
             (leaf_skel, leaf_v),
             (local_skel, local_v),
             (coeffs, coeffs_v),
-            (top_skel, top_v),
         ),
         sems,
     )
@@ -260,17 +264,10 @@
             even, odd = leaf_v[node], leaf_v[node + 1]
         else:
             even, odd = local_v[node - 8], local_v[node - 7]
-        high, low = split(kappa(even, odd))
+        near_k = kappa(even, odd).astype(BF16)
         for target, other, dims in ((node, node + 1, NT), (node + 1, node, NN)):
-            value = coeffs_v[other]
-            couplings_v[target] = mm2(value, high, dims) + mm(value.astype(BF16), low, dims)
+            couplings_v[target] = mm2(coeffs_v[other], near_k, dims)
     done += fetch(((couplings_v, couplings),), out_sems.at[pl.ds(2, 1)])
-    waits[6]()
-    group = jnp.right_shift(device, LEVELS)
-    mine = top_v[group]
-    for other in range(GROUPS):
-        value = kappa(top_v[other], mine)
-        top_k[other] = jnp.where(group == other, 0.0, value).astype(BF16)
     for wait in done:
         wait()
 
@@ -293,9 +290,16 @@
         send[group] = total
 
 
-def reply_kernel(received, totals, top_k, reply):
+def reply_kernel(received, totals, top_skel, reply):
     flat = jnp.concatenate([totals[group] for group in range(GROUPS)], axis=1)
-    field = mm(flat, top_k[...].reshape(GROUPS * RANK, RANK))[:SHARE]
+    group = jnp.right_shift(lax.axis_index("pts"), LEVELS)
+    (mine,) = extended(top_skel[group], False, True)
+    top_k = []
+    for other in range(GROUPS):
+        (theirs,) = extended(top_skel[other], True, False)
+        value = jnp.exp2(mm(theirs.T, mine) * EXPO)
+        top_k.append(jnp.where(group == other, 0.0, value).astype(BF16))
+    field = mm(flat, jnp.concatenate(top_k, axis=0))[:SHARE]
     levels = [level_sums(received, level) for level in range(LEVELS)]
     blank = jnp.zeros((SHARE, RANK), F32)
     for member in range(MEMBERS):
@@ -354,7 +358,7 @@
     for level in reversed(range(LEVELS)):
         bit = jnp.bitwise_and(jnp.right_shift(device, level), 1)
         half = chain_v[0, level, pl.ds(pl.multiple_of(bit * RANK, RANK), RANK), :]
-        field = mm(got[level].astype(BF16), chain_k_v[level]) + mm2(field, half, NT)
+        field = mm(got[level].astype(BF16), chain_k_v[level]) + mm(field.astype(BF16), half, NT)
     waits[3]()
     waits[4]()
     now = [field]
@@ -372,16 +376,14 @@
     stay = pl.multiple_of(core * RANK, RANK)
     for leaf in range(LEAVES):
         swapped = jnp.concatenate([now[leaf][DIM:], now[leaf][:DIM]], axis=0)
-        high, low = split(swapped)
+        terms = jnp.concatenate(split(swapped), axis=0)
         for target, first in ((give_v, away), (keep_v, stay)):
             rows = both_v[leaf, pl.ds(first, RANK), :]
-            target[leaf] = (mm(rows, high) + mm(rows, low)).astype(target.dtype)
+            target[leaf] = mm(jnp.concatenate([rows, rows], axis=1), terms).astype(BF16)
     done = fetch(((give_v, give), (keep_v, keep)), out_sems)
     for leaf in range(LEAVES):
-        high, low = split(now[leaf])
-        far = mm(basis_v[leaf], high, NT) + mm(basis_v[leaf], low, NT)
-        total = (near_v[leaf] + far).astype(BF16)
-        output_v[:, pl.ds(leaf * ROWS, ROWS)] = total.T[:DIM]
+        far = mm(now[leaf][:DIM].astype(BF16), basis_v[leaf], NT)
+        output_v[:, pl.ds(leaf * ROWS, ROWS)] = (near_v[leaf] + far).astype(BF16)
     done += fetch(((output_v, output),), out_sems.at[pl.ds(2, 1)])
     for wait in done:
         wait()
@@ -397,8 +399,6 @@
     near,
     ids_v,
     valid_v,
-    below_v,
-    above_v,
     own_v,
     left,
     right,
@@ -407,42 +407,44 @@
     sems,
     near_sems,
 ):
-    waits = fetch(
-        (
-            (below, below_v),
-            (own, own_v),
-            (above, above_v),
-            (ids, ids_v),
-            (valid, valid_v),
-        ),
-        sems,
-    )
-    for index, block in enumerate((below_v, own_v, above_v)):
-        waits[index]()
+    waits = fetch(((own, own_v), (ids, ids_v), (valid, valid_v)), sems)
+    lane = lanes(ROWS)
+    for index, block in ((0, below), (2, above), (1, own_v)):
+        if index == 1:
+            waits[0]()
         for leaf in range(LEAVES):
             value = block[leaf]
-            made = extended(value.T[DIM:], index == 1, True)
-            right[index * LEAVES + leaf] = made[-1]
-            values[index * LEAVES + leaf] = value
+            turned = value.T
+            made = norm_rows(turned[DIM:], index == 1, True)
+            spare = jnp.concatenate([made[-1].T, jnp.zeros((ROWS, 112), F32)], axis=1)
+            values[index * LEAVES + leaf] = turned[:DIM]
+            right[index * LEAVES + leaf] = jnp.where(
+                lane < DIM, spare, value.astype(F32)
+            ).astype(BF16)
             if index == 1:
-                left[leaf] = made[0].T
-    device = lax.axis_index("pts")
-    shift = (device - 1) * LEAVES
+                blank = jnp.zeros((DIM - 16, ROWS), BF16)
+                left[leaf] = jnp.concatenate(
+                    [made[0].astype(BF16), blank, turned[DIM:]], axis=0
+                )
+    shift = (lax.axis_index("pts") - 1) * LEAVES
+    waits[1]()
+    waits[2]()
 
     def body(leaf, carry):
         mine = left[leaf]
-        total = jnp.zeros((ROWS, 128), F32)
-        for slot in range(SLOTS):
-            where = ids_v[leaf, slot] - shift
-            used = jnp.full((1, 128), valid_v[leaf, slot], jnp.int32).astype(F32).astype(BF16)
-            tile = jnp.exp2(mm(mine, right[where]) * EXPO).astype(BF16)
-            total = total + mm(tile, values[where] * used)
+        total = jnp.zeros((DIM, ROWS), F32)
+        for start in range(0, SLOTS, 4):
+            tiles, others = [], []
+            for slot in range(start, start + 4):
+                where = ids_v[leaf, slot] - shift
+                used = jnp.full((1, ROWS), valid_v[leaf, slot], jnp.int32).astype(F32).astype(BF16)
+                tiles.append(jnp.exp2(mm(right[where], mine) * EXPO).astype(BF16))
+                others.append(values[where] * used)
+            total = total + mm(jnp.concatenate(others, axis=1), jnp.concatenate(tiles, axis=0))
         near_v[leaf] = total
         pltpu.make_async_copy(near_v.at[leaf], near.at[leaf], near_sems.at[leaf]).start()
         return carry
 
-    waits[3]()
-    waits[4]()
     lax.fori_loop(0, LEAVES, body, 0)
     for leaf in range(LEAVES):
         pltpu.make_async_copy(near_v.at[leaf], near.at[leaf], near_sems.at[leaf]).wait()
@@ -512,10 +514,10 @@
     tree = (14, RANK, RANK)
     square = (LEAVES, RANK, RANK)
     links = (LEVELS, RANK, RANK)
-    couplings, chain_k, both, top_k = call(
+    couplings, chain_k, both = call(
         couple_kernel,
-        (sds(tree, F32), sds(links, BF16), sds(block, BF16), sds((GROUPS, RANK, RANK), BF16)),
-        [HBM] * 7 + [ANY],
+        (sds(tree, F32), sds(links, BF16), sds(block, BF16)),
+        [HBM] * 6 + [ANY],
         [
             pltpu.VMEM(tree, F32),
             pltpu.VMEM(block, BF16),
@@ -523,47 +525,44 @@
             pltpu.VMEM(leaf_skel.shape, BF16),
             pltpu.VMEM(local_skel.shape, BF16),
             pltpu.VMEM(chain_skel.shape, BF16),
-            pltpu.VMEM(top_skel.shape, BF16),
             pltpu.VMEM(tree, F32),
             pltpu.VMEM(links, BF16),
             pltpu.VMEM(block, BF16),
-            pltpu.SemaphoreType.DMA((7,)),
+            pltpu.SemaphoreType.DMA((6,)),
             pltpu.SemaphoreType.DMA((3,)),
         ],
         cost=(2 * 10**9, 4 * 10**6, 10**6),
-        places=(HBM, HBM, HBM, VMEM),
-    )(coeffs, joined, cot, leaf_skel, local_skel, chain_skel, top_skel, total)
+        places=(HBM,) * 3,
+    )(coeffs, joined, cot, leaf_skel, local_skel, chain_skel, total)
 
     reply = call(
         reply_kernel, sds((MEMBERS, SLAB, RANK), BF16), [VMEM] * 3, room=8
-    )(received, totals, top_k)
+    )(received, totals, top_skel)
     replies = lax.all_to_all(reply, "pts", 0, 0, axis_index_groups=groups, tiled=True)
 
     near = call(
         near_kernel,
-        sds((LEAVES, ROWS, 128), F32),
-        [HBM] * 5 + [ANY],
+        sds((LEAVES, DIM, ROWS), F32),
+        [HBM, HBM, VMEM, HBM, VMEM, ANY],
         [
             pltpu.SMEM((LEAVES, SLOTS), jnp.int32),
             pltpu.SMEM((LEAVES, SLOTS), jnp.int32),
             pltpu.VMEM(block, BF16),
-            pltpu.VMEM(block, BF16),
-            pltpu.VMEM(block, BF16),
-            pltpu.VMEM(block, BF16),
-            pltpu.VMEM((3 * LEAVES, 128, ROWS), BF16),
+            pltpu.VMEM((LEAVES, 128, ROWS), BF16),
             pltpu.VMEM((3 * LEAVES, ROWS, 128), BF16),
-            pltpu.VMEM((LEAVES, ROWS, 128), F32),
-            pltpu.SemaphoreType.DMA((5,)),
+            pltpu.VMEM((3 * LEAVES, DIM, ROWS), BF16),
+            pltpu.VMEM((LEAVES, DIM, ROWS), F32),
+            pltpu.SemaphoreType.DMA((3,)),
             pltpu.SemaphoreType.DMA((LEAVES,)),
         ],
-        cost=(LEAVES * 4 * 10**8, 4 * 10**6, LEAVES * 800000),
+        cost=(5 * 10**10, 4 * 10**6, LEAVES * 800000),
         places=HBM,
-        room=60,
+        room=14,
     )(near_ids, near_valid, below, joined, above, reply)
 
     give, output, keep = call(
         down_kernel,
-        (sds(square, BF16), sds((DIM, LEAVES * ROWS), BF16), sds(square, F32)),
+        (sds(square, BF16), sds((DIM, LEAVES * ROWS), BF16), sds(square, BF16)),
         [HBM] * 8,
         [
             pltpu.VMEM((MEMBERS, SLAB, RANK), BF16),
@@ -573,10 +572,10 @@
             pltpu.VMEM(tree, F32),
             pltpu.VMEM(block, BF16),
             pltpu.VMEM(block, BF16),
-            pltpu.VMEM(block, F32),
+            pltpu.VMEM((LEAVES, DIM, ROWS), F32),
             pltpu.VMEM(square, BF16),
             pltpu.VMEM((DIM, LEAVES * ROWS), BF16),
-            pltpu.VMEM(square, F32),
+            pltpu.VMEM(square, BF16),
             pltpu.SemaphoreType.DMA((8,)),
             pltpu.SemaphoreType.DMA((3,)),
         ],
@@ -593,7 +592,7 @@
         near,
     )
     got = lax.ppermute(give, "rhs", [(0, 1), (1, 0)])
-    basis_grad = (keep + got.astype(F32)).astype(BF16)
+    basis_grad = (keep.astype(F32) + got.astype(F32)).astype(BF16)
     return output.T, basis_grad
 
 

time: 80 us -> 77.6 us (0.970)
  waiting for transfers between devices: 8.32 us -> 13.1 us
  starting transfers between devices: 37.8 us -> 34.4 us
  Pallas kernels: 27.6 us -> 25.6 us
  local copies, waits for them, and re-layouts: 3.25 us -> 1.51 us
    all_to_all x1, waiting for transfers between devices: 4.03 us -> 9.49 us  [local(): lax.all_to_all(total, 'pts', 0, 0, axis_index_groups=across, tiled=True)]
    pallas_call x2, Pallas kernels: 17.3 us -> 15.5 us  [the longest x1 11.3 us: local(): call(near_kernel, sds((LEAVES, DIM, ROWS), F32), [HBM, HBM, VMEM, HBM, VM...]
    all_to_all x1, starting transfers between devices: 5.42 us -> 3.65 us  [local(): lax.all_to_all(reply, 'pts', 0, 0, axis_index_groups=groups, tiled=True)]
    unnamed x8 -> x12, local copies, waits for them, and re-layouts: 3.25 us -> 1.51 us
    ppermute x1, starting transfers between devices: 5.41 us -> 4.19 us  [local(): got = lax.ppermute(give, 'rhs', [(0, 1), (1, 0)])]
    all_to_all x1, starting transfers between devices: 12.8 us -> 11.7 us  [local(): lax.all_to_all(total, 'pts', 0, 0, axis_index_groups=across, tiled=True)]
  transfers between devices with their start and end apart: 6 -> 6, of which waited for: 3 -> 3; matrix products, arithmetic and copies ran while one was open for 0% -> 0% of each run, Pallas kernels for 24% -> 22%
where the time goes in v3:
time: 77.6 us; the launch traced here: 77.1 us
  starting transfers between devices  34.4 us (44%)
  Pallas kernels  25.6 us (33%)
  waiting for transfers between devices  13.1 us (17%)
  other arithmetic  1.72 us (2%)
  local copies, waits for them, and re-layouts  1.51 us (2%)
    all_to_all x1, starting transfers between devices, local(): lax.all_to_all(total, 'pts', 0, 0, axis_index_groups=across, tiled=True)  11.7 us
    pallas_call x1, Pallas kernels, local(): call(near_kernel, sds((LEAVES, DIM, ROWS), F32), [HBM, HBM, VMEM, HBM, VM...  11.3 us
    all_to_all x1, starting transfers between devices, local(): lax.all_to_all(send, 'pts', 0, 0, axis_index_groups=groups, tiled=True)  9.58 us
    all_to_all x1, waiting for transfers between devices, local(): lax.all_to_all(total, 'pts', 0, 0, axis_index_groups=across, tiled=True)  9.49 us
    pallas_call x1, Pallas kernels, local(): call(rise_kernel, (sds(block, BF16), sds((14, RANK, RANK), F32), sds((MEM...  4.65 us
    ppermute x1, starting transfers between devices, local(): got = lax.ppermute(give, 'rhs', [(0, 1), (1, 0)])  4.19 us
    pallas_call x1, Pallas kernels, local(): call(couple_kernel, (sds(tree, F32), sds(links, BF16), sds(block, BF16)),...  4.12 us
    ppermute x1, starting transfers between devices, local(): below = lax.ppermute(joined, 'pts', upward)  4.02 us
  transfers between devices with their start and end apart: 6, of which 3 were waited for; matrix products, arithmetic and copies ran while one was open for 0% of the time, Pallas kernels for 22%

profile of v3, /device:TPU:1, one launch (start us, length us, event | category | flops | bytes accessed | tf_op | source)
XLA Modules:
  0.0 77.1 jit_solution(15629089243705719418)
XLA Ops:
  0.6 4.7 %shard_map.140 = (bf16[8,256,128]{2,1,0:T(8,128)(2,1)}, f32[14,128,128]{2,1,0:T(8,128)}, bf16[16,48,128]{2,1,0:T(8,128)(2,1)}) custom-call(bf16[64,2048]{1,0:T(8,128)(2,1)} %bitcast.10, bf16[64,2048]{1,0:T(8,128)(2,1)} %bitcast.11, s32[16,128]{1,0:T(8,128)} %bitcast.14, bf16[64,2048]{1,0:T(8,128)(2,1)} %bitcast.12, bf16[8,256,128]{2,1,0:T(8,128)(2,1)} %basis.3, ...), custom_call_target="tpu_custom_call" | custom-call | tf_op jit(solution)/shard_map/pallas_call | solution.py:476
  5.3 9.6 %all-to-all-start = ((bf16[16,48,128]{2,1,0:T(8,128)(2,1)}), bf16[16,48,128]{2,1,0:T(8,128)(2,1)S(1)}, u32[]{:S(2)}, u32[]{:S(2)}) async-start(bf16[16,48,128]{2,1,0:T(8,128)(2,1)} %get-tuple-element.11), calls=%async_computation | async-start | bytes 393216 | tf_op jit(solution)/shard_map/all_to_all | solution.py:503
  14.9 1.3 %collective-permute-start.1 = (bf16[8,256,128]{2,1,0:T(8,128)(2,1)}, bf16[8,256,128]{2,1,0:T(8,128)(2,1)S(1)}, u32[]{:S(2)}, u32[]{:S(2)}) collective-permute-start(bf16[8,256,128]{2,1,0:T(8,128)(2,1)} %get-tuple-element.13.joined.own), channel_id=1, source_target_pairs={{2,0},{4,2},{6,4},{8,6},{10,8},{12,10},{14,12},{16,14},{18,16},{20... | collective-permute-start | bytes 1572872 | tf_op jit(solution)/shard_map/ppermute | solution.py:507
  16.2 4.0 %collective-permute-start = (bf16[8,256,128]{2,1,0:T(8,128)(2,1)}, bf16[8,256,128]{2,1,0:T(8,128)(2,1)S(1)}, u32[]{:S(2)}, u32[]{:S(2)}) collective-permute-start(bf16[8,256,128]{2,1,0:T(8,128)(2,1)} %get-tuple-element.13.joined.own), channel_id=1, source_target_pairs={{0,2},{2,4},{4,6},{6,8},{8,10},{10,12},{12,14},{14,16},{16,18},{18... | collective-permute-start | bytes 1572872 | tf_op jit(solution)/shard_map/ppermute | solution.py:506
  20.2 2.2 %all-to-all-done.received = bf16[16,48,128]{2,1,0:T(8,128)(2,1)S(1)} async-done(((bf16[16,48,128]{2,1,0:T(8,128)(2,1)}), bf16[16,48,128]{2,1,0:T(8,128)(2,1)S(1)}, u32[]{:S(2)}, u32[]{:S(2)}) %all-to-all-start) | async-done | bytes 196640 | tf_op jit(solution)/shard_map/all_to_all | solution.py:503
  22.4 0.6 shard_map.141.after
  23.1 11.7 %all-to-all-start.1 = ((bf16[16,16,128]{2,1,0:T(8,128)(2,1)}), bf16[16,16,128]{2,1,0:T(8,128)(2,1)S(1)}, u32[]{:S(2)}, u32[]{:S(2)}) async-start(bf16[16,16,128]{2,1,0:T(8,128)(2,1)} %shard_map.141.after), calls=%async_computation.1 | async-start | bytes 131072 | tf_op jit(solution)/shard_map/all_to_all | solution.py:512
  34.8 0.0 copy-start.1
  34.8 4.1 %shard_map.143 = (f32[14,128,128]{2,1,0:T(8,128)}, bf16[4,128,128]{2,1,0:T(8,128)(2,1)}, bf16[8,256,128]{2,1,0:T(8,128)(2,1)}) custom-call(f32[14,128,128]{2,1,0:T(8,128)} %get-tuple-element.12.coeffs, bf16[8,256,128]{2,1,0:T(8,128)(2,1)} %get-tuple-element.13.joined.own, bf16[64,2048]{1,0:T(8,128)(2,1)} %bitcast.13, bf16[8,64,128]{2,1,0:T(8,128)(2,1)} %bitcast.16, ...), custom_call_target="tpu_custom_call" | custom-call | flops 2000000000 | bytes 4000000 | tf_op jit(solution)/shard_map/pallas_call | solution.py:517
  38.9 9.5 %all-to-all-done.1.totals = bf16[16,16,128]{2,1,0:T(8,128)(2,1)S(1)} async-done(((bf16[16,16,128]{2,1,0:T(8,128)(2,1)}), bf16[16,16,128]{2,1,0:T(8,128)(2,1)S(1)}, u32[]{:S(2)}, u32[]{:S(2)}) %all-to-all-start.1) | async-done | bytes 65568 | tf_op jit(solution)/shard_map/all_to_all | solution.py:512
  48.4 0.0 copy-done.1
  48.4 1.2 %shard_map.142.after = bf16[16,48,128]{2,1,0:T(8,128)(2,1)} custom-call(bf16[16,48,128]{2,1,0:T(8,128)(2,1)S(1)} %all-to-all-done.received, bf16[16,16,128]{2,1,0:T(8,128)(2,1)S(1)} %all-to-all-done.1.totals, bf16[16,64,128]{2,1,0:T(8,128)(2,1)S(1)} %bitcast.9), custom_call_target="tpu_custom_call" | custom-call | tf_op jit(solution)/shard_map/pallas_call | solution.py:538
  49.6 3.7 %all-to-all-start.2 = ((bf16[16,48,128]{2,1,0:T(8,128)(2,1)}), bf16[16,48,128]{2,1,0:T(8,128)(2,1)S(1)}, u32[]{:S(2)}, u32[]{:S(2)}) async-start(bf16[16,48,128]{2,1,0:T(8,128)(2,1)} %shard_map.142.after), calls=%async_computation.2 | async-start | bytes 393216 | tf_op jit(solution)/shard_map/all_to_all | solution.py:541
  53.2 0.0 collective-permute-done.1.above
  53.2 0.0 collective-permute-done.below
  53.3 0.0 copy-done.2
  53.3 11.3 %shard_map.144.near = f32[8,64,256]{2,1,0:T(8,128)S(1)} custom-call(s32[8,12]{1,0:T(8,128)S(1)} %copy-done.3, s32[8,12]{1,0:T(8,128)S(1)} %copy-done.4, bf16[8,256,128]{2,1,0:T(8,128)(2,1)S(1)} %collective-permute-done.below, bf16[8,256,128]{2,1,0:T(8,128)(2,1)S(1)} %copy-done.2, bf16[8,256,128]{2,1,0:T(8,128)(2,1)S(1)} %collective-permute-done.1.above, ...), custom_call_target="tpu_custom_call" | custom-call | flops 49999998976 | bytes 4000000 | tf_op jit(solution)/shard_map/pallas_call | solution.py:543
  64.6 0.8 %copy-done = f32[8,64,256]{2,1,0:T(8,128)} copy-done((f32[8,64,256]{2,1,0:T(8,128)}, f32[8,64,256]{2,1,0:T(8,128)S(1)}, u32[]{:S(2)}) %copy-start) | copy-done | bytes 524312
  65.5 0.0 all-to-all-done.2.replies
  65.5 0.7 copy-done.5
  66.1 3.7 %shard_map.145 = (bf16[8,128,128]{2,1,0:T(8,128)(2,1)}, bf16[64,2048]{1,0:T(8,128)(2,1)}, bf16[8,128,128]{2,1,0:T(8,128)(2,1)}) custom-call(bf16[16,48,128]{2,1,0:T(8,128)(2,1)} %copy-done.5, bf16[4,128,128]{2,1,0:T(8,128)(2,1)} %get-tuple-element.14.chain_k, bf16[1,4,256,128]{3,2,1,0:T(8,128)(2,1)} %chain.3, bf16[7,256,128]{2,1,0:T(8,128)(2,1)} %transfer.3, ...), custom_call_target="tpu_custom_call" | custom-call | tf_op jit(solution)/shard_map/pallas_call | solution.py:563
  69.8 4.2 %collective-permute-start.2 = (bf16[8,128,128]{2,1,0:T(8,128)(2,1)}, bf16[8,128,128]{2,1,0:T(8,128)(2,1)S(1)}, u32[]{:S(2)}, u32[]{:S(2)}) collective-permute-start(bf16[8,128,128]{2,1,0:T(8,128)(2,1)} %get-tuple-element.19), channel_id=1, source_target_pairs={{0,1},{1,0},{2,3},{3,2},{4,5},{5,4},{6,7},{7,6},{8,9},{9,8},{10,11... | collective-permute-start | bytes 786440 | tf_op jit(solution)/shard_map/ppermute | solution.py:594
  74.0 1.4 %collective-permute-done.2 = bf16[8,128,128]{2,1,0:T(8,128)(2,1)S(1)} collective-permute-done((bf16[8,128,128]{2,1,0:T(8,128)(2,1)}, bf16[8,128,128]{2,1,0:T(8,128)(2,1)S(1)}, u32[]{:S(2)}, u32[]{:S(2)}) %collective-permute-start.2) | collective-permute-done | bytes 262176 | tf_op jit(solution)/shard_map/ppermute | solution.py:594
  75.4 1.7 %add_convert_fusion = bf16[8,128,128]{2,1,0:T(8,128)(2,1)} fusion(bf16[8,128,128]{2,1,0:T(8,128)(2,1)S(1)} %collective-permute-done.2, bf16[8,128,128]{2,1,0:T(8,128)(2,1)} %get-tuple-element.18), kind=kLoop, calls=%fused_computation | loop fusion | flops 524288 | bytes 786432 | tf_op jit(solution)/shard_map/convert_element_type | solution.py:595
  (7 shorter events, 0.0 us)
Async XLA Ops:
  5.3 17.1 %all-to-all-start = ((bf16[16,48,128]{2,1,0:T(8,128)(2,1)}), bf16[16,48,128]{2,1,0:T(8,128)(2,1)S(1)}, u32[]{:S(2)}, u32[]{:S(2)}) async-start(bf16[16,48,128]{2,1,0:T(8,128)(2,1)} %get-tuple-element.11), calls=%async_computation | async-start | bytes 393216 | tf_op jit(solution)/shard_map/all_to_all | solution.py:503
  14.9 38.4 %collective-permute-start.1 = (bf16[8,256,128]{2,1,0:T(8,128)(2,1)}, bf16[8,256,128]{2,1,0:T(8,128)(2,1)S(1)}, u32[]{:S(2)}, u32[]{:S(2)}) collective-permute-start(bf16[8,256,128]{2,1,0:T(8,128)(2,1)} %get-tuple-element.13.joined.own), channel_id=1, source_target_pairs={{2,0},{4,2},{6,4},{8,6},{10,8},{12,10},{14,12},{16,14},{18,16},{20... | collective-permute-start | bytes 1572872 | tf_op jit(solution)/shard_map/ppermute | solution.py:507
  16.2 37.1 %collective-permute-start = (bf16[8,256,128]{2,1,0:T(8,128)(2,1)}, bf16[8,256,128]{2,1,0:T(8,128)(2,1)S(1)}, u32[]{:S(2)}, u32[]{:S(2)}) collective-permute-start(bf16[8,256,128]{2,1,0:T(8,128)(2,1)} %get-tuple-element.13.joined.own), channel_id=1, source_target_pairs={{0,2},{2,4},{4,6},{6,8},{8,10},{10,12},{12,14},{14,16},{16,18},{18... | collective-permute-start | bytes 1572872 | tf_op jit(solution)/shard_map/ppermute | solution.py:506
  23.1 25.3 %all-to-all-start.1 = ((bf16[16,16,128]{2,1,0:T(8,128)(2,1)}), bf16[16,16,128]{2,1,0:T(8,128)(2,1)S(1)}, u32[]{:S(2)}, u32[]{:S(2)}) async-start(bf16[16,16,128]{2,1,0:T(8,128)(2,1)} %shard_map.141.after), calls=%async_computation.1 | async-start | bytes 131072 | tf_op jit(solution)/shard_map/all_to_all | solution.py:512
  34.8 13.6 %copy-start.1 = (bf16[16,128,64]{1,2,0:T(8,128)(2,1)S(1)}, bf16[16,128,64]{1,2,0:T(8,128)(2,1)}, u32[]{:S(2)}) copy-start(bf16[16,128,64]{1,2,0:T(8,128)(2,1)} %param.25) | copy-start | bytes 786436
  48.4 4.9 %copy-start.2 = (bf16[8,256,128]{2,1,0:T(8,128)(2,1)S(1)}, bf16[8,256,128]{2,1,0:T(8,128)(2,1)}, u32[]{:S(2)}) copy-start(bf16[8,256,128]{2,1,0:T(8,128)(2,1)} %get-tuple-element.13.joined.own) | copy-start | bytes 1572868
  49.6 3.7 %copy-start.3 = (s32[8,12]{1,0:T(8,128)S(1)}, s32[8,12]{1,0:T(8,128)}, u32[]{:S(2)}) copy-start(s32[8,12]{1,0:T(8,128)} %ids.1) | copy-start | bytes 1156
  49.6 3.7 %copy-start.4 = (s32[8,12]{1,0:T(8,128)S(1)}, s32[8,12]{1,0:T(8,128)}, u32[]{:S(2)}) copy-start(s32[8,12]{1,0:T(8,128)} %valid.1) | copy-start | bytes 1156
  49.6 15.9 %all-to-all-start.2 = ((bf16[16,48,128]{2,1,0:T(8,128)(2,1)}), bf16[16,48,128]{2,1,0:T(8,128)(2,1)S(1)}, u32[]{:S(2)}, u32[]{:S(2)}) async-start(bf16[16,48,128]{2,1,0:T(8,128)(2,1)} %shard_map.142.after), calls=%async_computation.2 | async-start | bytes 393216 | tf_op jit(solution)/shard_map/all_to_all | solution.py:541
  64.6 0.8 %copy-start = (f32[8,64,256]{2,1,0:T(8,128)}, f32[8,64,256]{2,1,0:T(8,128)S(1)}, u32[]{:S(2)}) copy-start(f32[8,64,256]{2,1,0:T(8,128)S(1)} %shard_map.144.near) | copy-start | bytes 1572868
  65.5 0.7 copy-start.5
  69.8 5.5 %collective-permute-start.2 = (bf16[8,128,128]{2,1,0:T(8,128)(2,1)}, bf16[8,128,128]{2,1,0:T(8,128)(2,1)S(1)}, u32[]{:S(2)}, u32[]{:S(2)}) collective-permute-start(bf16[8,128,128]{2,1,0:T(8,128)(2,1)} %get-tuple-element.19), channel_id=1, source_target_pairs={{0,1},{1,0},{2,3},{3,2},{4,5},{5,4},{6,7},{7,6},{8,9},{9,8},{10,11... | collective-permute-start | bytes 786440 | tf_op jit(solution)/shard_map/ppermute | solution.py:594

commit v4 on v3

--- a/solution.py
+++ b/solution.py
@@ -308,48 +308,10 @@
 
 
 def down_kernel(
-    replies,
-    chain_k,
-    chain,
-    transfer,
-    couplings,
-    both,
-    basis,
-    near,
-    give,
-    output,
-    keep,
-    replies_v,
-    chain_k_v,
-    chain_v,
-    transfer_v,
-    couplings_v,
-    both_v,
-    basis_v,
-    near_v,
-    give_v,
-    output_v,
-    keep_v,
-    sems,
-    out_sems,
+    replies, chain_k, chain, transfer, couplings, both, basis, near, give, output, keep
 ):
-    waits = fetch(
-        (
-            (replies, replies_v),
-            (chain_k, chain_k_v),
-            (chain, chain_v),
-            (transfer, transfer_v),
-            (couplings, couplings_v),
-            (both, both_v),
-            (basis, basis_v),
-            (near, near_v),
-        ),
-        sems,
-    )
     device, core = lax.axis_index("pts"), lax.axis_index("rhs")
-    for wait in waits[:3]:
-        wait()
-    table = replies_v[...].astype(F32)
+    table = replies[...].astype(F32)
     got = [
         table[:, index * SHARE : (index + 1) * SHARE].reshape(RANK, RANK)
         for index in range(LEVELS + 1)
@@ -357,44 +319,36 @@
     field = got[LEVELS]
     for level in reversed(range(LEVELS)):
         bit = jnp.bitwise_and(jnp.right_shift(device, level), 1)
-        half = chain_v[0, level, pl.ds(pl.multiple_of(bit * RANK, RANK), RANK), :]
-        field = mm(got[level].astype(BF16), chain_k_v[level]) + mm(field.astype(BF16), half, NT)
-    waits[3]()
-    waits[4]()
+        half = chain[0, level, pl.ds(pl.multiple_of(bit * RANK, RANK), RANK), :]
+        field = mm(got[level].astype(BF16), chain_k[level]) + mm(field.astype(BF16), half, NT)
     now = [field]
     for start, count, offset in ((6, 1, 12), (4, 2, 8), (0, 4, 0)):
         below = []
         for node in range(count):
-            spread = mm2(now[node], transfer_v[start + node], NT)
+            spread = mm2(now[node], transfer[start + node], NT)
             for child in range(2):
                 rows = spread[:, child * RANK : (child + 1) * RANK]
-                below.append(couplings_v[offset + 2 * node + child] + rows)
+                below.append(couplings[offset + 2 * node + child] + rows)
         now = below
-    for wait in waits[5:]:
-        wait()
     away = pl.multiple_of((1 - core) * RANK, RANK)
     stay = pl.multiple_of(core * RANK, RANK)
     for leaf in range(LEAVES):
         swapped = jnp.concatenate([now[leaf][DIM:], now[leaf][:DIM]], axis=0)
         terms = jnp.concatenate(split(swapped), axis=0)
-        for target, first in ((give_v, away), (keep_v, stay)):
-            rows = both_v[leaf, pl.ds(first, RANK), :]
-            target[leaf] = mm(jnp.concatenate([rows, rows], axis=1), terms).astype(BF16)
-    done = fetch(((give_v, give), (keep_v, keep)), out_sems)
+        for target, first in ((give, away), (keep, stay)):
+            rows = both[leaf, pl.ds(first, RANK), :]
+            target[leaf] = mm(jnp.concatenate([rows, rows], axis=1), terms).astype(target.dtype)
     for leaf in range(LEAVES):
-        far = mm(now[leaf][:DIM].astype(BF16), basis_v[leaf], NT)
-        output_v[:, pl.ds(leaf * ROWS, ROWS)] = (near_v[leaf] + far).astype(BF16)
-    done += fetch(((output_v, output),), out_sems.at[pl.ds(2, 1)])
-    for wait in done:
-        wait()
+        far = mm(now[leaf][:DIM].astype(BF16), basis[leaf], NT)
+        output[:, pl.ds(leaf * ROWS, ROWS)] = (near[leaf] + far).astype(BF16)
 
 
 def near_kernel(
     ids,
     valid,
-    below,
+    swap_a,
     own,
-    above,
+    swap_b,
     after,
     near,
     ids_v,
@@ -409,7 +363,10 @@
 ):
     waits = fetch(((own, own_v), (ids, ids_v), (valid, valid_v)), sems)
     lane = lanes(ROWS)
-    for index, block in ((0, below), (2, above), (1, own_v)):
+    device = lax.axis_index("pts")
+    odd = jnp.bitwise_and(device, 1)
+    places = ((2 - 2 * odd) * LEAVES, LEAVES, 2 * odd * LEAVES)
+    for index, block in ((0, swap_a), (2, swap_b), (1, own_v)):
         if index == 1:
             waits[0]()
         for leaf in range(LEAVES):
@@ -417,8 +374,8 @@
             turned = value.T
             made = norm_rows(turned[DIM:], index == 1, True)
             spare = jnp.concatenate([made[-1].T, jnp.zeros((ROWS, 112), F32)], axis=1)
-            values[index * LEAVES + leaf] = turned[:DIM]
-            right[index * LEAVES + leaf] = jnp.where(
+            values[places[index] + leaf] = turned[:DIM]
+            right[places[index] + leaf] = jnp.where(
                 lane < DIM, spare, value.astype(F32)
             ).astype(BF16)
             if index == 1:
@@ -426,7 +383,7 @@
                 left[leaf] = jnp.concatenate(
                     [made[0].astype(BF16), blank, turned[DIM:]], axis=0
                 )
-    shift = (lax.axis_index("pts") - 1) * LEAVES
+    shift = (device - 1) * LEAVES
     waits[1]()
     waits[2]()
 
@@ -502,9 +459,10 @@
     across = [[g * MEMBERS + i for g in range(GROUPS)] for i in range(MEMBERS)]
     received = lax.all_to_all(send, "pts", 0, 0, axis_index_groups=groups, tiled=True)
 
-    upward = [(i, i + 1) for i in range(count - 1)]
-    below = lax.ppermute(joined, "pts", upward)
-    above = lax.ppermute(joined, "pts", [(b, a) for a, b in upward])
+    swaps = []
+    for first in (0, 1):
+        pairs = [(i, i + 1) for i in range(first, count - 1, 2)]
+        swaps.append(lax.ppermute(joined, "pts", pairs + [(b, a) for a, b in pairs]))
 
     total = call(
         total_kernel, sds((GROUPS, 2 * SHARE, RANK), BF16), [VMEM], room=8
@@ -558,29 +516,13 @@
         cost=(5 * 10**10, 4 * 10**6, LEAVES * 800000),
         places=HBM,
         room=14,
-    )(near_ids, near_valid, below, joined, above, reply)
+    )(near_ids, near_valid, swaps[0], joined, swaps[1], reply)
 
     give, output, keep = call(
         down_kernel,
-        (sds(square, BF16), sds((DIM, LEAVES * ROWS), BF16), sds(square, BF16)),
-        [HBM] * 8,
-        [
-            pltpu.VMEM((MEMBERS, SLAB, RANK), BF16),
-            pltpu.VMEM(links, BF16),
-            pltpu.VMEM(chain_transfer.shape, BF16),
-            pltpu.VMEM(local_transfer.shape, BF16),
-            pltpu.VMEM(tree, F32),
-            pltpu.VMEM(block, BF16),
-            pltpu.VMEM(block, BF16),
-            pltpu.VMEM((LEAVES, DIM, ROWS), F32),
-            pltpu.VMEM(square, BF16),
-            pltpu.VMEM((DIM, LEAVES * ROWS), BF16),
-            pltpu.VMEM(square, BF16),
-            pltpu.SemaphoreType.DMA((8,)),
-            pltpu.SemaphoreType.DMA((3,)),
-        ],
-        places=(HBM,) * 3,
-        room=60,
+        (sds(square, BF16), sds((DIM, LEAVES * ROWS), BF16), sds(square, F32)),
+        [VMEM] * 8,
+        room=14,
     )(
         replies,
         chain_k,
@@ -592,7 +534,7 @@
         near,
     )
     got = lax.ppermute(give, "rhs", [(0, 1), (1, 0)])
-    basis_grad = (keep.astype(F32) + got.astype(F32)).astype(BF16)
+    basis_grad = (keep + got.astype(F32)).astype(BF16)
     return output.T, basis_grad
 
 

time: 77.6 us -> 75.9 us (0.978)
  waiting for transfers between devices: 13.1 us -> 8.17 us
  starting transfers between devices: 34.4 us -> 37.2 us
  local copies, waits for them, and re-layouts: 1.51 us -> 3.06 us
  other arithmetic: 1.72 us -> 0.77 us
    all_to_all x1, waiting for transfers between devices: 9.49 us -> 5.86 us  [local(): lax.all_to_all(total, 'pts', 0, 0, axis_index_groups=across, tiled=True)]
    unnamed x12 -> x24, local copies, waits for them, and re-layouts: 1.51 us -> 3.06 us
    pallas_call x1, Pallas kernels: 3.66 us -> 2.31 us  [local(): call(down_kernel, (sds(square, BF16), sds((DIM, LEAVES * ROWS), BF16), sd...]
    all_to_all x1, waiting for transfers between devices: 2.22 us -> 1.16 us  [local(): lax.all_to_all(send, 'pts', 0, 0, axis_index_groups=groups, tiled=True)]
    ppermute x2, starting transfers between devices: 5.31 us -> 6.35 us  [local(): lax.ppermute(joined, 'pts', pairs + [(b, a) for a, b in pairs])]
    pallas_call x1, Pallas kernels: 11.3 us -> 12.4 us  [local(): call(near_kernel, sds((LEAVES, DIM, ROWS), F32), [HBM, HBM, VMEM, HBM, VM...]
    ppermute x1, starting transfers between devices: 4.19 us -> 5.21 us  [local(): got = lax.ppermute(give, 'rhs', [(0, 1), (1, 0)])]
    convert_element_type x1, other arithmetic: 1.72 us -> 0.77 us  [local(): basis_grad = (keep + got.astype(F32)).astype(BF16)]
  transfers between devices with their start and end apart: 6 -> 6, of which waited for: 3 -> 3; matrix products, arithmetic and copies ran while one was open for 0% -> 0% of each run, Pallas kernels for 22% -> 24%
where the time goes in v4:
time: 75.9 us; the launch traced here: 75.3 us
  starting transfers between devices  37.2 us (49%)
  Pallas kernels  25.3 us (33%)
  waiting for transfers between devices  8.17 us (11%)
  local copies, waits for them, and re-layouts  3.06 us (4%)
  between operations  0.85 us (1%)
  other arithmetic  0.77 us (1%)
    pallas_call x1, Pallas kernels, local(): call(near_kernel, sds((LEAVES, DIM, ROWS), F32), [HBM, HBM, VMEM, HBM, VM...  12.4 us
    all_to_all x1, starting transfers between devices, local(): lax.all_to_all(total, 'pts', 0, 0, axis_index_groups=across, tiled=True)  11.7 us
    all_to_all x1, starting transfers between devices, local(): lax.all_to_all(send, 'pts', 0, 0, axis_index_groups=groups, tiled=True)  9.58 us
    ppermute x2, starting transfers between devices, local(): lax.ppermute(joined, 'pts', pairs + [(b, a) for a, b in pairs])  6.35 us
    all_to_all x1, waiting for transfers between devices, local(): lax.all_to_all(total, 'pts', 0, 0, axis_index_groups=across, tiled=True)  5.86 us
    ppermute x1, starting transfers between devices, local(): got = lax.ppermute(give, 'rhs', [(0, 1), (1, 0)])  5.21 us
    pallas_call x1, Pallas kernels, local(): call(rise_kernel, (sds(block, BF16), sds((14, RANK, RANK), F32), sds((MEM...  4.64 us
    all_to_all x1, starting transfers between devices, local(): lax.all_to_all(reply, 'pts', 0, 0, axis_index_groups=groups, tiled=True)  4.33 us
  transfers between devices with their start and end apart: 6, of which 3 were waited for; matrix products, arithmetic and copies ran while one was open for 0% of the time, Pallas kernels for 24%

profile of v4, /device:TPU:1, one launch (start us, length us, event | category | flops | bytes accessed | tf_op | source)
XLA Modules:
  0.0 75.3 jit_solution(17163047508279219459)
XLA Ops:
  0.6 4.6 %shard_map.140 = (bf16[8,256,128]{2,1,0:T(8,128)(2,1)}, f32[14,128,128]{2,1,0:T(8,128)}, bf16[16,48,128]{2,1,0:T(8,128)(2,1)}) custom-call(bf16[64,2048]{1,0:T(8,128)(2,1)} %bitcast.10, bf16[64,2048]{1,0:T(8,128)(2,1)} %bitcast.11, s32[16,128]{1,0:T(8,128)} %bitcast.14, bf16[64,2048]{1,0:T(8,128)(2,1)} %bitcast.12, bf16[8,256,128]{2,1,0:T(8,128)(2,1)} %basis.3, ...), custom_call_target="tpu_custom_call" | custom-call | tf_op jit(solution)/shard_map/pallas_call | solution.py:433
  5.3 9.6 %all-to-all-start = ((bf16[16,48,128]{2,1,0:T(8,128)(2,1)}), bf16[16,48,128]{2,1,0:T(8,128)(2,1)S(1)}, u32[]{:S(2)}, u32[]{:S(2)}) async-start(bf16[16,48,128]{2,1,0:T(8,128)(2,1)} %get-tuple-element.11), calls=%async_computation | async-start | bytes 393216 | tf_op jit(solution)/shard_map/all_to_all | solution.py:460
  14.9 0.7 collective-permute-start.1
  15.6 5.7 %collective-permute-start = (bf16[8,256,128]{2,1,0:T(8,128)(2,1)}, bf16[8,256,128]{2,1,0:T(8,128)(2,1)}, u32[]{:S(2)}, u32[]{:S(2)}) collective-permute-start(bf16[8,256,128]{2,1,0:T(8,128)(2,1)} %get-tuple-element.13.joined.own), channel_id=1, source_target_pairs={{0,2},{4,6},{8,10},{12,14},{16,18},{20,22},{24,26},{28,30},{32,34}... | collective-permute-start | bytes 1572872 | tf_op jit(solution)/shard_map/ppermute | solution.py:465
  21.2 1.2 %all-to-all-done.received = bf16[16,48,128]{2,1,0:T(8,128)(2,1)S(1)} async-done(((bf16[16,48,128]{2,1,0:T(8,128)(2,1)}), bf16[16,48,128]{2,1,0:T(8,128)(2,1)S(1)}, u32[]{:S(2)}, u32[]{:S(2)}) %all-to-all-start) | async-done | bytes 196640 | tf_op jit(solution)/shard_map/all_to_all | solution.py:460
  22.4 0.6 shard_map.141.after
  23.0 11.7 %all-to-all-start.1 = ((bf16[16,16,128]{2,1,0:T(8,128)(2,1)}), bf16[16,16,128]{2,1,0:T(8,128)(2,1)S(1)}, u32[]{:S(2)}, u32[]{:S(2)}) async-start(bf16[16,16,128]{2,1,0:T(8,128)(2,1)} %shard_map.141.after), calls=%async_computation.1 | async-start | bytes 131072 | tf_op jit(solution)/shard_map/all_to_all | solution.py:470
  34.7 0.0 copy-start.5
  34.7 4.2 %shard_map.143 = (f32[14,128,128]{2,1,0:T(8,128)}, bf16[4,128,128]{2,1,0:T(8,128)(2,1)}, bf16[8,256,128]{2,1,0:T(8,128)(2,1)}) custom-call(f32[14,128,128]{2,1,0:T(8,128)} %get-tuple-element.12.coeffs, bf16[8,256,128]{2,1,0:T(8,128)(2,1)} %get-tuple-element.13.joined.own, bf16[64,2048]{1,0:T(8,128)(2,1)} %bitcast.13, bf16[8,64,128]{2,1,0:T(8,128)(2,1)} %bitcast.16, ...), custom_call_target="tpu_custom_call" | custom-call | flops 2000000000 | bytes 4000000 | tf_op jit(solution)/shard_map/pallas_call | solution.py:475
  38.9 5.9 %all-to-all-done.1.totals = bf16[16,16,128]{2,1,0:T(8,128)(2,1)S(1)} async-done(((bf16[16,16,128]{2,1,0:T(8,128)(2,1)}), bf16[16,16,128]{2,1,0:T(8,128)(2,1)S(1)}, u32[]{:S(2)}, u32[]{:S(2)}) %all-to-all-start.1) | async-done | bytes 65568 | tf_op jit(solution)/shard_map/all_to_all | solution.py:470
  44.8 1.2 %shard_map.142.after = bf16[16,48,128]{2,1,0:T(8,128)(2,1)} custom-call(bf16[16,48,128]{2,1,0:T(8,128)(2,1)S(1)} %all-to-all-done.received, bf16[16,16,128]{2,1,0:T(8,128)(2,1)S(1)} %all-to-all-done.1.totals, bf16[16,64,128]{2,1,0:T(8,128)(2,1)S(1)} %bitcast.9), custom_call_target="tpu_custom_call" | custom-call | tf_op jit(solution)/shard_map/pallas_call | solution.py:496
  45.9 4.3 %all-to-all-start.2 = ((bf16[16,48,128]{2,1,0:T(8,128)(2,1)}), bf16[16,48,128]{2,1,0:T(8,128)(2,1)S(1)}, u32[]{:S(2)}, u32[]{:S(2)}) async-start(bf16[16,48,128]{2,1,0:T(8,128)(2,1)} %shard_map.142.after), calls=%async_computation.2 | async-start | bytes 393216 | tf_op jit(solution)/shard_map/all_to_all | solution.py:499
  50.3 0.0 copy-start
  50.3 0.0 copy-start.1
  50.3 0.0 copy-start.2
  50.3 0.0 copy-start.6
  50.4 0.8 %copy-done.8 = bf16[8,256,128]{2,1,0:T(8,128)(2,1)} copy-done((bf16[8,256,128]{2,1,0:T(8,128)(2,1)}, bf16[8,256,128]{2,1,0:T(8,128)(2,1)S(1)}, u32[]{:S(2)}) %copy-start.8) | copy-done | bytes 524312
  51.2 1.1 %copy-done.7 = bf16[8,256,128]{2,1,0:T(8,128)(2,1)S(1)} copy-done((bf16[8,256,128]{2,1,0:T(8,128)(2,1)S(1)}, bf16[8,256,128]{2,1,0:T(8,128)(2,1)}, u32[]{:S(2)}) %copy-start.7) | copy-done | bytes 524312
  52.4 1.0 %copy-done.9 = bf16[8,256,128]{2,1,0:T(8,128)(2,1)S(1)} copy-done((bf16[8,256,128]{2,1,0:T(8,128)(2,1)S(1)}, bf16[8,256,128]{2,1,0:T(8,128)(2,1)}, u32[]{:S(2)}) %copy-start.9) | copy-done | bytes 524312
  53.4 12.4 %shard_map.144.near = f32[8,64,256]{2,1,0:T(8,128)S(1)} custom-call(s32[8,12]{1,0:T(8,128)S(1)} %copy-done.10, s32[8,12]{1,0:T(8,128)S(1)} %copy-done.11, bf16[8,256,128]{2,1,0:T(8,128)(2,1)} %collective-permute-done.swap_a, bf16[8,256,128]{2,1,0:T(8,128)(2,1)S(1)} %copy-done.7, bf16[8,256,128]{2,1,0:T(8,128)(2,1)S(1)} %copy-done.9, ...), custom_call_target="tpu_custom_call" | custom-call | flops 49999998976 | bytes 4000000 | tf_op jit(solution)/shard_map/pallas_call | solution.py:501
  65.8 2.3 %shard_map.145 = (bf16[8,128,128]{2,1,0:T(8,128)(2,1)S(1)}, bf16[64,2048]{1,0:T(8,128)(2,1)}, f32[8,128,128]{2,1,0:T(8,128)S(1)}) custom-call(bf16[16,48,128]{2,1,0:T(8,128)(2,1)S(1)} %all-to-all-done.2.replies, bf16[4,128,128]{2,1,0:T(8,128)(2,1)S(1)} %copy-done.6, bf16[1,4,256,128]{3,2,1,0:T(8,128)(2,1)S(1)} %copy-done.2, ...), custom_call_target="tpu_custom_call" | custom-call | tf_op jit(solution)/shard_map/pallas_call | solution.py:521
  68.2 5.2 %collective-permute-start.2 = (bf16[8,128,128]{2,1,0:T(8,128)(2,1)S(1)}, bf16[8,128,128]{2,1,0:T(8,128)(2,1)S(1)}, u32[]{:S(2)}, u32[]{:S(2)}) collective-permute-start(bf16[8,128,128]{2,1,0:T(8,128)(2,1)S(1)} %get-tuple-element.19), channel_id=1, source_target_pairs={{0,1},{1,0},{2,3},{3,2},{4,5},{5,4},{6,7},{7,6},{8,9},{9,8},{10,11... | collective-permute-start | bytes 786440 | tf_op jit(solution)/shard_map/ppermute | solution.py:536
  73.4 1.1 %collective-permute-done.2 = bf16[8,128,128]{2,1,0:T(8,128)(2,1)S(1)} collective-permute-done((bf16[8,128,128]{2,1,0:T(8,128)(2,1)S(1)}, bf16[8,128,128]{2,1,0:T(8,128)(2,1)S(1)}, u32[]{:S(2)}, u32[]{:S(2)}) %collective-permute-start.2) | collective-permute-done | bytes 262176 | tf_op jit(solution)/shard_map/ppermute | solution.py:536
  74.5 0.8 %add_convert_fusion = bf16[8,128,128]{2,1,0:T(8,128)(2,1)} fusion(f32[8,128,128]{2,1,0:T(8,128)S(1)} %get-tuple-element.18, bf16[8,128,128]{2,1,0:T(8,128)(2,1)S(1)} %collective-permute-done.2), kind=kLoop, calls=%fused_computation | loop fusion | flops 393216 | bytes 1048576 | tf_op jit(solution)/shard_map/convert_element_type | solution.py:537
  (19 shorter events, 0.0 us)
Async XLA Ops:
  5.3 17.1 %all-to-all-start = ((bf16[16,48,128]{2,1,0:T(8,128)(2,1)}), bf16[16,48,128]{2,1,0:T(8,128)(2,1)S(1)}, u32[]{:S(2)}, u32[]{:S(2)}) async-start(bf16[16,48,128]{2,1,0:T(8,128)(2,1)} %get-tuple-element.11), calls=%async_computation | async-start | bytes 393216 | tf_op jit(solution)/shard_map/all_to_all | solution.py:460
  14.9 35.5 %collective-permute-start.1 = (bf16[8,256,128]{2,1,0:T(8,128)(2,1)}, bf16[8,256,128]{2,1,0:T(8,128)(2,1)S(1)}, u32[]{:S(2)}, u32[]{:S(2)}) collective-permute-start(bf16[8,256,128]{2,1,0:T(8,128)(2,1)} %get-tuple-element.13.joined.own), channel_id=1, source_target_pairs={{2,4},{6,8},{10,12},{14,16},{18,20},{22,24},{26,28},{30,32},{34,36... | collective-permute-start | bytes 1572872 | tf_op jit(solution)/shard_map/ppermute | solution.py:465
  15.6 35.6 %collective-permute-start = (bf16[8,256,128]{2,1,0:T(8,128)(2,1)}, bf16[8,256,128]{2,1,0:T(8,128)(2,1)}, u32[]{:S(2)}, u32[]{:S(2)}) collective-permute-start(bf16[8,256,128]{2,1,0:T(8,128)(2,1)} %get-tuple-element.13.joined.own), channel_id=1, source_target_pairs={{0,2},{4,6},{8,10},{12,14},{16,18},{20,22},{24,26},{28,30},{32,34}... | collective-permute-start | bytes 1572872 | tf_op jit(solution)/shard_map/ppermute | solution.py:465
  23.0 21.7 %all-to-all-start.1 = ((bf16[16,16,128]{2,1,0:T(8,128)(2,1)}), bf16[16,16,128]{2,1,0:T(8,128)(2,1)S(1)}, u32[]{:S(2)}, u32[]{:S(2)}) async-start(bf16[16,16,128]{2,1,0:T(8,128)(2,1)} %shard_map.141.after), calls=%async_computation.1 | async-start | bytes 131072 | tf_op jit(solution)/shard_map/all_to_all | solution.py:470
  34.7 10.0 %copy-start.5 = (bf16[16,128,64]{1,2,0:T(8,128)(2,1)S(1)}, bf16[16,128,64]{1,2,0:T(8,128)(2,1)}, u32[]{:S(2)}) copy-start(bf16[16,128,64]{1,2,0:T(8,128)(2,1)} %param.25) | copy-start | bytes 786436
  45.9 5.3 %copy-start.10 = (s32[8,12]{1,0:T(8,128)S(1)}, s32[8,12]{1,0:T(8,128)}, u32[]{:S(2)}) copy-start(s32[8,12]{1,0:T(8,128)} %ids.1) | copy-start | bytes 1156
  45.9 5.3 %copy-start.11 = (s32[8,12]{1,0:T(8,128)S(1)}, s32[8,12]{1,0:T(8,128)}, u32[]{:S(2)}) copy-start(s32[8,12]{1,0:T(8,128)} %valid.1) | copy-start | bytes 1156
  45.9 19.8 %all-to-all-start.2 = ((bf16[16,48,128]{2,1,0:T(8,128)(2,1)}), bf16[16,48,128]{2,1,0:T(8,128)(2,1)S(1)}, u32[]{:S(2)}, u32[]{:S(2)}) async-start(bf16[16,48,128]{2,1,0:T(8,128)(2,1)} %shard_map.142.after), calls=%async_computation.2 | async-start | bytes 393216 | tf_op jit(solution)/shard_map/all_to_all | solution.py:499
  50.3 15.5 %copy-start = (bf16[8,256,128]{2,1,0:T(8,128)(2,1)S(1)}, bf16[8,256,128]{2,1,0:T(8,128)(2,1)}, u32[]{:S(2)}) copy-start(bf16[8,256,128]{2,1,0:T(8,128)(2,1)} %basis.3) | copy-start | bytes 1572868
  50.3 15.5 %copy-start.1 = (bf16[7,256,128]{2,1,0:T(8,128)(2,1)S(1)}, bf16[7,256,128]{2,1,0:T(8,128)(2,1)}, u32[]{:S(2)}) copy-start(bf16[7,256,128]{2,1,0:T(8,128)(2,1)} %transfer.3) | copy-start | bytes 1376260
  50.3 15.5 %copy-start.2 = (bf16[1,4,256,128]{3,2,1,0:T(8,128)(2,1)S(1)}, bf16[1,4,256,128]{3,2,1,0:T(8,128)(2,1)}, u32[]{:S(2)}) copy-start(bf16[1,4,256,128]{3,2,1,0:T(8,128)(2,1)} %chain.3) | copy-start | bytes 786436
  50.3 15.5 %copy-start.3 = (f32[14,128,128]{2,1,0:T(8,128)S(1)}, f32[14,128,128]{2,1,0:T(8,128)}, u32[]{:S(2)}) copy-start(f32[14,128,128]{2,1,0:T(8,128)} %get-tuple-element.15.couplings) | copy-start | bytes 2752516
  50.3 15.5 %copy-start.4 = (bf16[8,256,128]{2,1,0:T(8,128)(2,1)S(1)}, bf16[8,256,128]{2,1,0:T(8,128)(2,1)}, u32[]{:S(2)}) copy-start(bf16[8,256,128]{2,1,0:T(8,128)(2,1)} %get-tuple-element.16.both) | copy-start | bytes 1572868
  50.3 15.5 %copy-start.6 = (bf16[4,128,128]{2,1,0:T(8,128)(2,1)S(1)}, bf16[4,128,128]{2,1,0:T(8,128)(2,1)}, u32[]{:S(2)}) copy-start(bf16[4,128,128]{2,1,0:T(8,128)(2,1)} %get-tuple-element.14.chain_k) | copy-start | bytes 393220
  50.4 0.8 %copy-start.8 = (bf16[8,256,128]{2,1,0:T(8,128)(2,1)}, bf16[8,256,128]{2,1,0:T(8,128)(2,1)S(1)}, u32[]{:S(2)}) copy-start(bf16[8,256,128]{2,1,0:T(8,128)(2,1)S(1)} %collective-permute-done.1.swap_b) | copy-start | bytes 1572868
  51.2 1.2 %copy-start.7 = (bf16[8,256,128]{2,1,0:T(8,128)(2,1)S(1)}, bf16[8,256,128]{2,1,0:T(8,128)(2,1)}, u32[]{:S(2)}) copy-start(bf16[8,256,128]{2,1,0:T(8,128)(2,1)} %get-tuple-element.13.joined.own) | copy-start | bytes 1572868
  52.4 1.0 %copy-start.9 = (bf16[8,256,128]{2,1,0:T(8,128)(2,1)S(1)}, bf16[8,256,128]{2,1,0:T(8,128)(2,1)}, u32[]{:S(2)}) copy-start(bf16[8,256,128]{2,1,0:T(8,128)(2,1)} %copy-done.8) | copy-start | bytes 1572868
  68.2 6.4 %collective-permute-start.2 = (bf16[8,128,128]{2,1,0:T(8,128)(2,1)S(1)}, bf16[8,128,128]{2,1,0:T(8,128)(2,1)S(1)}, u32[]{:S(2)}, u32[]{:S(2)}) collective-permute-start(bf16[8,128,128]{2,1,0:T(8,128)(2,1)S(1)} %get-tuple-element.19), channel_id=1, source_target_pairs={{0,1},{1,0},{2,3},{3,2},{4,5},{5,4},{6,7},{7,6},{8,9},{9,8},{10,11... | collective-permute-start | bytes 786440 | tf_op jit(solution)/shard_map/ppermute | solution.py:536

commit v5 on v4

--- a/solution.py
+++ b/solution.py
@@ -109,6 +109,16 @@
     for copy in copies:
         copy.start()
     return [copy.wait for copy in copies]
+
+
+def chain_products(chain, device):
+    product, products = None, []
+    for level in range(LEVELS):
+        bit = jnp.bitwise_and(jnp.right_shift(device, level), 1)
+        half = chain[0, level, pl.ds(pl.multiple_of(bit * RANK, RANK), RANK), :]
+        product = half if product is None else mm(product, half).astype(BF16)
+        products.append(product)
+    return products
 
 
 def rise_kernel(
@@ -140,17 +150,18 @@
             (points, raw_v.at[pl.ds(DIM, DIM)]),
             (inputs, raw_v.at[pl.ds(0, DIM)]),
             (order, order_v),
+            (chain, chain_v),
             (cot, cot_v),
             (basis, basis_v),
             (transfer, transfer_v),
-            (chain, chain_v),
         ),
         in_sems,
     )
     device = lax.axis_index("pts")
     base = device * (LEAVES * ROWS)
-    for wait in waits[:3]:
+    for wait in waits[:4]:
         wait()
+    products = chain_products(chain_v, device)
     for index in range(4):
         low = raw_v[:, pl.ds(index * 512, ROWS)].T
         high = raw_v[:, pl.ds(index * 512 + ROWS, ROWS)].T
@@ -175,7 +186,7 @@
         copy = pltpu.make_async_copy(joined_v.at[leaf], joined.at[leaf], joined_sems.at[leaf])
         copy.start()
         joined_copies.append(copy)
-    for wait in waits[3:]:
+    for wait in waits[4:]:
         wait()
     now = []
     for leaf in range(LEAVES):
@@ -198,13 +209,9 @@
             for n in range(len(now) // 2)
         ]
         offset += len(now)
-    value = now[0]
-    parts = [value]
-    for level in range(LEVELS):
-        bit = jnp.bitwise_and(jnp.right_shift(device, level), 1)
-        half = chain_v[0, level, pl.ds(pl.multiple_of(bit * RANK, RANK), RANK), :]
-        value = mm(value.astype(BF16), half)
-        parts.append(value)
+    above = mm(now[0].astype(BF16), jnp.concatenate(products, axis=1))
+    parts = [now[0]]
+    parts += [above[:, level * RANK : (level + 1) * RANK] for level in range(LEVELS)]
     parts = [part.reshape(MEMBERS, SHARE, RANK) for part in parts]
     parts.append(jnp.zeros((MEMBERS, SLAB - 5 * SHARE, RANK), F32))
     send[...] = jnp.concatenate(parts, axis=1).astype(BF16)
@@ -219,6 +226,7 @@
     leaf_skel,
     local_skel,
     chain_skel,
+    chain,
     after,
     couplings,
     chain_k,
@@ -229,6 +237,7 @@
     leaf_v,
     local_v,
     skel_v,
+    chain_v,
     couplings_v,
     chain_k_v,
     both_v,
@@ -240,6 +249,7 @@
             (cot, cot_v),
             (joined, joined_v),
             (chain_skel, skel_v),
+            (chain, chain_v),
             (leaf_skel, leaf_v),
             (local_skel, local_v),
             (coeffs, coeffs_v),
@@ -247,17 +257,22 @@
         sems,
     )
     device = lax.axis_index("pts")
-    for wait in waits[:3]:
+    for wait in waits[:4]:
         wait()
     for leaf in range(LEAVES):
         theirs = cot_v[:, pl.ds(leaf * ROWS, ROWS)].T
         both_v[leaf] = jnp.concatenate([joined_v[leaf][:, :DIM], theirs], axis=1)
     done = fetch(((both_v, both),), out_sems)
+    products = chain_products(chain_v, device)
     for level in range(LEVELS):
         bit = jnp.bitwise_and(jnp.right_shift(device, level), 1)
-        chain_k_v[level] = kappa(skel_v[0, level, 1 - bit], skel_v[0, level, bit]).astype(BF16)
+        value = kappa(skel_v[0, level, 1 - bit], skel_v[0, level, bit]).astype(BF16)
+        if level > 0:
+            value = mm(value, products[level - 1], NT).astype(BF16)
+        chain_k_v[level] = value
+    chain_k_v[LEVELS] = products[LEVELS - 1].T
     done += fetch(((chain_k_v, chain_k),), out_sems.at[pl.ds(1, 1)])
-    for wait in waits[3:6]:
+    for wait in waits[4:]:
         wait()
     for node in range(0, 14, 2):
         if node < 8:
@@ -308,19 +323,16 @@
 
 
 def down_kernel(
-    replies, chain_k, chain, transfer, couplings, both, basis, near, give, output, keep
+    replies, chain_k, transfer, couplings, both, basis, near, give, output, keep
 ):
-    device, core = lax.axis_index("pts"), lax.axis_index("rhs")
+    core = lax.axis_index("rhs")
     table = replies[...].astype(F32)
     got = [
         table[:, index * SHARE : (index + 1) * SHARE].reshape(RANK, RANK)
         for index in range(LEVELS + 1)
     ]
-    field = got[LEVELS]
-    for level in reversed(range(LEVELS)):
-        bit = jnp.bitwise_and(jnp.right_shift(device, level), 1)
-        half = chain[0, level, pl.ds(pl.multiple_of(bit * RANK, RANK), RANK), :]
-        field = mm(got[level].astype(BF16), chain_k[level]) + mm(field.astype(BF16), half, NT)
+    rows = jnp.concatenate([part.astype(BF16) for part in got], axis=1)
+    field = mm(rows, chain_k[...].reshape((LEVELS + 1) * RANK, RANK))
     now = [field]
     for start, count, offset in ((6, 1, 12), (4, 2, 8), (0, 4, 0)):
         below = []
@@ -353,7 +365,9 @@
     near,
     ids_v,
     valid_v,
+    swap_a_v,
     own_v,
+    swap_b_v,
     left,
     right,
     values,
@@ -361,14 +375,16 @@
     sems,
     near_sems,
 ):
-    waits = fetch(((own, own_v), (ids, ids_v), (valid, valid_v)), sems)
+    waits = fetch(
+        ((own, own_v), (swap_a, swap_a_v), (swap_b, swap_b_v), (ids, ids_v), (valid, valid_v)),
+        sems,
+    )
     lane = lanes(ROWS)
     device = lax.axis_index("pts")
     odd = jnp.bitwise_and(device, 1)
     places = ((2 - 2 * odd) * LEAVES, LEAVES, 2 * odd * LEAVES)
-    for index, block in ((0, swap_a), (2, swap_b), (1, own_v)):
-        if index == 1:
-            waits[0]()
+    for wait, index, block in ((0, 1, own_v), (1, 0, swap_a_v), (2, 2, swap_b_v)):
+        waits[wait]()
         for leaf in range(LEAVES):
             value = block[leaf]
             turned = value.T
@@ -384,8 +400,8 @@
                     [made[0].astype(BF16), blank, turned[DIM:]], axis=0
                 )
     shift = (device - 1) * LEAVES
-    waits[1]()
-    waits[2]()
+    waits[3]()
+    waits[4]()
 
     def body(leaf, carry):
         mine = left[leaf]
@@ -471,11 +487,11 @@
 
     tree = (14, RANK, RANK)
     square = (LEAVES, RANK, RANK)
-    links = (LEVELS, RANK, RANK)
+    links = (LEVELS + 1, RANK, RANK)
     couplings, chain_k, both = call(
         couple_kernel,
         (sds(tree, F32), sds(links, BF16), sds(block, BF16)),
-        [HBM] * 6 + [ANY],
+        [HBM] * 7 + [ANY],
         [
             pltpu.VMEM(tree, F32),
             pltpu.VMEM(block, BF16),
@@ -483,15 +499,16 @@
             pltpu.VMEM(leaf_skel.shape, BF16),
             pltpu.VMEM(local_skel.shape, BF16),
             pltpu.VMEM(chain_skel.shape, BF16),
+            pltpu.VMEM(chain_transfer.shape, BF16),
             pltpu.VMEM(tree, F32),
             pltpu.VMEM(links, BF16),
             pltpu.VMEM(block, BF16),
-            pltpu.SemaphoreType.DMA((6,)),
+            pltpu.SemaphoreType.DMA((7,)),
             pltpu.SemaphoreType.DMA((3,)),
         ],
         cost=(2 * 10**9, 4 * 10**6, 10**6),
         places=(HBM,) * 3,
-    )(coeffs, joined, cot, leaf_skel, local_skel, chain_skel, total)
+    )(coeffs, joined, cot, leaf_skel, local_skel, chain_skel, chain_transfer, total)
 
     reply = call(
         reply_kernel, sds((MEMBERS, SLAB, RANK), BF16), [VMEM] * 3, room=8
@@ -501,32 +518,33 @@
     near = call(
         near_kernel,
         sds((LEAVES, DIM, ROWS), F32),
-        [HBM, HBM, VMEM, HBM, VMEM, ANY],
+        [HBM] * 5 + [ANY],
         [
             pltpu.SMEM((LEAVES, SLOTS), jnp.int32),
             pltpu.SMEM((LEAVES, SLOTS), jnp.int32),
+            pltpu.VMEM(block, BF16),
+            pltpu.VMEM(block, BF16),
             pltpu.VMEM(block, BF16),
             pltpu.VMEM((LEAVES, 128, ROWS), BF16),
             pltpu.VMEM((3 * LEAVES, ROWS, 128), BF16),
             pltpu.VMEM((3 * LEAVES, DIM, ROWS), BF16),
             pltpu.VMEM((LEAVES, DIM, ROWS), F32),
-            pltpu.SemaphoreType.DMA((3,)),
+            pltpu.SemaphoreType.DMA((5,)),
             pltpu.SemaphoreType.DMA((LEAVES,)),
         ],
         cost=(5 * 10**10, 4 * 10**6, LEAVES * 800000),
         places=HBM,
-        room=14,
+        room=60,
     )(near_ids, near_valid, swaps[0], joined, swaps[1], reply)
 
     give, output, keep = call(
         down_kernel,
         (sds(square, BF16), sds((DIM, LEAVES * ROWS), BF16), sds(square, F32)),
-        [VMEM] * 8,
+        [VMEM] * 7,
         room=14,
     )(
         replies,
         chain_k,
-        chain_transfer,
         local_transfer,
         couplings,
         both,

time: 75.9 us -> 74 us (0.975)
  local copies, waits for them, and re-layouts: 3.06 us -> 1.87 us
    unnamed x24 -> x16, local copies, waits for them, and re-layouts: 3.06 us -> 1.87 us
  transfers between devices with their start and end apart: 6 -> 6, of which waited for: 3 -> 3; matrix products, arithmetic and copies ran while one was open for 0% -> 0% of each run, Pallas kernels for 24% -> 25%
where the time goes in v5:
time: 74 us; the launch traced here: 73.5 us
  starting transfers between devices  37 us (50%)
  Pallas kernels  25.2 us (34%)
  waiting for transfers between devices  7.79 us (11%)
  local copies, waits for them, and re-layouts  1.87 us (3%)
  between operations  0.83 us (1%)
  other arithmetic  0.77 us (1%)
    pallas_call x1, Pallas kernels, local(): call(near_kernel, sds((LEAVES, DIM, ROWS), F32), [HBM] * 5 + [ANY], [pltp...  12.2 us
    all_to_all x1, starting transfers between devices, local(): lax.all_to_all(total, 'pts', 0, 0, axis_index_groups=across, tiled=True)  11.7 us
    all_to_all x1, starting transfers between devices, local(): lax.all_to_all(send, 'pts', 0, 0, axis_index_groups=groups, tiled=True)  9.58 us
    ppermute x2, starting transfers between devices, local(): lax.ppermute(joined, 'pts', pairs + [(b, a) for a, b in pairs])  6.35 us
    all_to_all x1, waiting for transfers between devices, local(): lax.all_to_all(total, 'pts', 0, 0, axis_index_groups=across, tiled=True)  5.48 us
    ppermute x1, starting transfers between devices, local(): got = lax.ppermute(give, 'rhs', [(0, 1), (1, 0)])  5.21 us
    pallas_call x1, Pallas kernels, local(): call(rise_kernel, (sds(block, BF16), sds((14, RANK, RANK), F32), sds((MEM...  4.78 us
    pallas_call x1, Pallas kernels, local(): call(couple_kernel, (sds(tree, F32), sds(links, BF16), sds(block, BF16)),...  4.52 us
  transfers between devices with their start and end apart: 6, of which 3 were waited for; matrix products, arithmetic and copies ran while one was open for 0% of the time, Pallas kernels for 25%

profile of v5, /device:TPU:1, one launch (start us, length us, event | category | flops | bytes accessed | tf_op | source)
XLA Modules:
  0.0 73.5 jit_solution(13391312399054863424)
XLA Ops:
  0.6 4.8 %shard_map.140 = (bf16[8,256,128]{2,1,0:T(8,128)(2,1)}, f32[14,128,128]{2,1,0:T(8,128)}, bf16[16,48,128]{2,1,0:T(8,128)(2,1)}) custom-call(bf16[64,2048]{1,0:T(8,128)(2,1)} %bitcast.10, bf16[64,2048]{1,0:T(8,128)(2,1)} %bitcast.11, s32[16,128]{1,0:T(8,128)} %bitcast.14, bf16[64,2048]{1,0:T(8,128)(2,1)} %bitcast.12, bf16[8,256,128]{2,1,0:T(8,128)(2,1)} %basis.3, ...), custom_call_target="tpu_custom_call" | custom-call | tf_op jit(solution)/shard_map/pallas_call | solution.py:449
  5.4 9.6 %all-to-all-start = ((bf16[16,48,128]{2,1,0:T(8,128)(2,1)}), bf16[16,48,128]{2,1,0:T(8,128)(2,1)S(1)}, u32[]{:S(2)}, u32[]{:S(2)}) async-start(bf16[16,48,128]{2,1,0:T(8,128)(2,1)} %get-tuple-element.11), calls=%async_computation | async-start | bytes 393216 | tf_op jit(solution)/shard_map/all_to_all | solution.py:476
  15.0 0.7 collective-permute-start.1
  15.7 5.7 %collective-permute-start = (bf16[8,256,128]{2,1,0:T(8,128)(2,1)}, bf16[8,256,128]{2,1,0:T(8,128)(2,1)}, u32[]{:S(2)}, u32[]{:S(2)}) collective-permute-start(bf16[8,256,128]{2,1,0:T(8,128)(2,1)} %get-tuple-element.13.joined.own), channel_id=1, source_target_pairs={{0,2},{4,6},{8,10},{12,14},{16,18},{20,22},{24,26},{28,30},{32,34}... | collective-permute-start | bytes 1572872 | tf_op jit(solution)/shard_map/ppermute | solution.py:481
  21.4 1.2 %all-to-all-done.received = bf16[16,48,128]{2,1,0:T(8,128)(2,1)S(1)} async-done(((bf16[16,48,128]{2,1,0:T(8,128)(2,1)}), bf16[16,48,128]{2,1,0:T(8,128)(2,1)S(1)}, u32[]{:S(2)}, u32[]{:S(2)}) %all-to-all-start) | async-done | bytes 196640 | tf_op jit(solution)/shard_map/all_to_all | solution.py:476
  22.5 0.6 shard_map.141.after
  23.2 11.7 %all-to-all-start.1 = ((bf16[16,16,128]{2,1,0:T(8,128)(2,1)}), bf16[16,16,128]{2,1,0:T(8,128)(2,1)S(1)}, u32[]{:S(2)}, u32[]{:S(2)}) async-start(bf16[16,16,128]{2,1,0:T(8,128)(2,1)} %shard_map.141.after), calls=%async_computation.1 | async-start | bytes 131072 | tf_op jit(solution)/shard_map/all_to_all | solution.py:486
  34.9 0.0 copy-start.5
  34.9 4.5 %shard_map.143 = (f32[14,128,128]{2,1,0:T(8,128)}, bf16[5,128,128]{2,1,0:T(8,128)(2,1)}, bf16[8,256,128]{2,1,0:T(8,128)(2,1)}) custom-call(f32[14,128,128]{2,1,0:T(8,128)} %get-tuple-element.12.coeffs, bf16[8,256,128]{2,1,0:T(8,128)(2,1)} %get-tuple-element.13.joined.own, bf16[64,2048]{1,0:T(8,128)(2,1)} %bitcast.13, bf16[8,64,128]{2,1,0:T(8,128)(2,1)} %bitcast.16, ...), custom_call_target="tpu_custom_call" | custom-call | flops 2000000000 | bytes 4000000 | tf_op jit(solution)/shard_map/pallas_call | solution.py:491
  39.4 5.5 %all-to-all-done.1.totals = bf16[16,16,128]{2,1,0:T(8,128)(2,1)S(1)} async-done(((bf16[16,16,128]{2,1,0:T(8,128)(2,1)}), bf16[16,16,128]{2,1,0:T(8,128)(2,1)S(1)}, u32[]{:S(2)}, u32[]{:S(2)}) %all-to-all-start.1) | async-done | bytes 65568 | tf_op jit(solution)/shard_map/all_to_all | solution.py:486
  44.9 1.2 %shard_map.142.after = bf16[16,48,128]{2,1,0:T(8,128)(2,1)} custom-call(bf16[16,48,128]{2,1,0:T(8,128)(2,1)S(1)} %all-to-all-done.received, bf16[16,16,128]{2,1,0:T(8,128)(2,1)S(1)} %all-to-all-done.1.totals, bf16[16,64,128]{2,1,0:T(8,128)(2,1)S(1)} %bitcast.9), custom_call_target="tpu_custom_call" | custom-call | tf_op jit(solution)/shard_map/pallas_call | solution.py:513
  46.1 4.2 %all-to-all-start.2 = ((bf16[16,48,128]{2,1,0:T(8,128)(2,1)}), bf16[16,48,128]{2,1,0:T(8,128)(2,1)S(1)}, u32[]{:S(2)}, u32[]{:S(2)}) async-start(bf16[16,48,128]{2,1,0:T(8,128)(2,1)} %shard_map.142.after), calls=%async_computation.2 | async-start | bytes 393216 | tf_op jit(solution)/shard_map/all_to_all | solution.py:516
  50.3 0.0 copy-start
  50.3 0.0 copy-start.1
  50.3 0.0 copy-start.6
  50.4 0.0 collective-permute-done.swap_a
  50.4 0.8 %copy-done.7 = bf16[8,256,128]{2,1,0:T(8,128)(2,1)} copy-done((bf16[8,256,128]{2,1,0:T(8,128)(2,1)}, bf16[8,256,128]{2,1,0:T(8,128)(2,1)S(1)}, u32[]{:S(2)}) %copy-start.7) | copy-done | bytes 524312
  51.2 12.2 %shard_map.144.near = f32[8,64,256]{2,1,0:T(8,128)} custom-call(s32[8,12]{1,0:T(8,128)} %ids.1, s32[8,12]{1,0:T(8,128)} %valid.1, bf16[8,256,128]{2,1,0:T(8,128)(2,1)} %collective-permute-done.swap_a, bf16[8,256,128]{2,1,0:T(8,128)(2,1)} %get-tuple-element.13.joined.own, bf16[8,256,128]{2,1,0:T(8,128)(2,1)} %copy-done.7, bf16[16,48,128]{2,1,0:T(8,128)(2,1)} %shard_map.142.after), custom_call_target="tpu_custom_call" | custom-call | flops 49999998976 | bytes 4000000 | tf_op jit(solution)/shard_map/pallas_call | solution.py:518
  63.4 0.0 all-to-all-done.2.replies
  63.5 1.0 %copy-done.4 = f32[8,64,256]{2,1,0:T(8,128)S(1)} copy-done((f32[8,64,256]{2,1,0:T(8,128)S(1)}, f32[8,64,256]{2,1,0:T(8,128)}, u32[]{:S(2)}) %copy-start.4) | copy-done | bytes 524312
  64.5 1.9 %shard_map.145 = (bf16[8,128,128]{2,1,0:T(8,128)(2,1)S(1)}, bf16[64,2048]{1,0:T(8,128)(2,1)}, f32[8,128,128]{2,1,0:T(8,128)S(1)}) custom-call(bf16[16,48,128]{2,1,0:T(8,128)(2,1)S(1)} %all-to-all-done.2.replies, bf16[5,128,128]{2,1,0:T(8,128)(2,1)S(1)} %copy-done.6, bf16[7,256,128]{2,1,0:T(8,128)(2,1)S(1)} %copy-done.1, f32[14,128,128]{2,1,0:T(8,128)S(1)} %copy-done.2, ...), custom_call_target="tpu_custom_call" | custom-call | tf_op jit(solution)/shard_map/pallas_call | solution.py:540
  66.4 5.2 %collective-permute-start.2 = (bf16[8,128,128]{2,1,0:T(8,128)(2,1)S(1)}, bf16[8,128,128]{2,1,0:T(8,128)(2,1)S(1)}, u32[]{:S(2)}, u32[]{:S(2)}) collective-permute-start(bf16[8,128,128]{2,1,0:T(8,128)(2,1)S(1)} %get-tuple-element.19), channel_id=1, source_target_pairs={{0,1},{1,0},{2,3},{3,2},{4,5},{5,4},{6,7},{7,6},{8,9},{9,8},{10,11... | collective-permute-start | bytes 786440 | tf_op jit(solution)/shard_map/ppermute | solution.py:554
  71.6 1.1 %collective-permute-done.2 = bf16[8,128,128]{2,1,0:T(8,128)(2,1)S(1)} collective-permute-done((bf16[8,128,128]{2,1,0:T(8,128)(2,1)S(1)}, bf16[8,128,128]{2,1,0:T(8,128)(2,1)S(1)}, u32[]{:S(2)}, u32[]{:S(2)}) %collective-permute-start.2) | collective-permute-done | bytes 262176 | tf_op jit(solution)/shard_map/ppermute | solution.py:554
  72.7 0.8 %add_convert_fusion = bf16[8,128,128]{2,1,0:T(8,128)(2,1)} fusion(f32[8,128,128]{2,1,0:T(8,128)S(1)} %get-tuple-element.18, bf16[8,128,128]{2,1,0:T(8,128)(2,1)S(1)} %collective-permute-done.2), kind=kLoop, calls=%fused_computation | loop fusion | flops 393216 | bytes 1048576 | tf_op jit(solution)/shard_map/convert_element_type | solution.py:555
  (11 shorter events, 0.0 us)
Async XLA Ops:
  5.4 17.1 %all-to-all-start = ((bf16[16,48,128]{2,1,0:T(8,128)(2,1)}), bf16[16,48,128]{2,1,0:T(8,128)(2,1)S(1)}, u32[]{:S(2)}, u32[]{:S(2)}) async-start(bf16[16,48,128]{2,1,0:T(8,128)(2,1)} %get-tuple-element.11), calls=%async_computation | async-start | bytes 393216 | tf_op jit(solution)/shard_map/all_to_all | solution.py:476
  15.0 35.3 %collective-permute-start.1 = (bf16[8,256,128]{2,1,0:T(8,128)(2,1)}, bf16[8,256,128]{2,1,0:T(8,128)(2,1)S(1)}, u32[]{:S(2)}, u32[]{:S(2)}) collective-permute-start(bf16[8,256,128]{2,1,0:T(8,128)(2,1)} %get-tuple-element.13.joined.own), channel_id=1, source_target_pairs={{2,4},{6,8},{10,12},{14,16},{18,20},{22,24},{26,28},{30,32},{34,36... | collective-permute-start | bytes 1572872 | tf_op jit(solution)/shard_map/ppermute | solution.py:481
  15.7 34.6 %collective-permute-start = (bf16[8,256,128]{2,1,0:T(8,128)(2,1)}, bf16[8,256,128]{2,1,0:T(8,128)(2,1)}, u32[]{:S(2)}, u32[]{:S(2)}) collective-permute-start(bf16[8,256,128]{2,1,0:T(8,128)(2,1)} %get-tuple-element.13.joined.own), channel_id=1, source_target_pairs={{0,2},{4,6},{8,10},{12,14},{16,18},{20,22},{24,26},{28,30},{32,34}... | collective-permute-start | bytes 1572872 | tf_op jit(solution)/shard_map/ppermute | solution.py:481
  23.2 21.7 %all-to-all-start.1 = ((bf16[16,16,128]{2,1,0:T(8,128)(2,1)}), bf16[16,16,128]{2,1,0:T(8,128)(2,1)S(1)}, u32[]{:S(2)}, u32[]{:S(2)}) async-start(bf16[16,16,128]{2,1,0:T(8,128)(2,1)} %shard_map.141.after), calls=%async_computation.1 | async-start | bytes 131072 | tf_op jit(solution)/shard_map/all_to_all | solution.py:486
  34.9 10.0 %copy-start.5 = (bf16[16,128,64]{1,2,0:T(8,128)(2,1)S(1)}, bf16[16,128,64]{1,2,0:T(8,128)(2,1)}, u32[]{:S(2)}) copy-start(bf16[16,128,64]{1,2,0:T(8,128)(2,1)} %param.25) | copy-start | bytes 786436
  46.1 17.3 %all-to-all-start.2 = ((bf16[16,48,128]{2,1,0:T(8,128)(2,1)}), bf16[16,48,128]{2,1,0:T(8,128)(2,1)S(1)}, u32[]{:S(2)}, u32[]{:S(2)}) async-start(bf16[16,48,128]{2,1,0:T(8,128)(2,1)} %shard_map.142.after), calls=%async_computation.2 | async-start | bytes 393216 | tf_op jit(solution)/shard_map/all_to_all | solution.py:516
  50.3 13.1 %copy-start = (bf16[8,256,128]{2,1,0:T(8,128)(2,1)S(1)}, bf16[8,256,128]{2,1,0:T(8,128)(2,1)}, u32[]{:S(2)}) copy-start(bf16[8,256,128]{2,1,0:T(8,128)(2,1)} %basis.3) | copy-start | bytes 1572868
  50.3 13.1 %copy-start.1 = (bf16[7,256,128]{2,1,0:T(8,128)(2,1)S(1)}, bf16[7,256,128]{2,1,0:T(8,128)(2,1)}, u32[]{:S(2)}) copy-start(bf16[7,256,128]{2,1,0:T(8,128)(2,1)} %transfer.3) | copy-start | bytes 1376260
  50.3 13.1 %copy-start.2 = (f32[14,128,128]{2,1,0:T(8,128)S(1)}, f32[14,128,128]{2,1,0:T(8,128)}, u32[]{:S(2)}) copy-start(f32[14,128,128]{2,1,0:T(8,128)} %get-tuple-element.15.couplings) | copy-start | bytes 2752516
  50.3 13.1 %copy-start.3 = (bf16[8,256,128]{2,1,0:T(8,128)(2,1)S(1)}, bf16[8,256,128]{2,1,0:T(8,128)(2,1)}, u32[]{:S(2)}) copy-start(bf16[8,256,128]{2,1,0:T(8,128)(2,1)} %get-tuple-element.16.both) | copy-start | bytes 1572868
  50.3 13.1 %copy-start.6 = (bf16[5,128,128]{2,1,0:T(8,128)(2,1)S(1)}, bf16[5,128,128]{2,1,0:T(8,128)(2,1)}, u32[]{:S(2)}) copy-start(bf16[5,128,128]{2,1,0:T(8,128)(2,1)} %get-tuple-element.14.chain_k) | copy-start | bytes 491524
  50.3 0.8 %copy-start.7 = (bf16[8,256,128]{2,1,0:T(8,128)(2,1)}, bf16[8,256,128]{2,1,0:T(8,128)(2,1)S(1)}, u32[]{:S(2)}) copy-start(bf16[8,256,128]{2,1,0:T(8,128)(2,1)S(1)} %collective-permute-done.1.swap_b) | copy-start | bytes 1572868
  63.5 1.0 %copy-start.4 = (f32[8,64,256]{2,1,0:T(8,128)S(1)}, f32[8,64,256]{2,1,0:T(8,128)}, u32[]{:S(2)}) copy-start(f32[8,64,256]{2,1,0:T(8,128)} %shard_map.144.near) | copy-start | bytes 1572868
  66.4 6.4 %collective-permute-start.2 = (bf16[8,128,128]{2,1,0:T(8,128)(2,1)S(1)}, bf16[8,128,128]{2,1,0:T(8,128)(2,1)S(1)}, u32[]{:S(2)}, u32[]{:S(2)}) collective-permute-start(bf16[8,128,128]{2,1,0:T(8,128)(2,1)S(1)} %get-tuple-element.19), channel_id=1, source_target_pairs={{0,1},{1,0},{2,3},{3,2},{4,5},{5,4},{6,7},{7,6},{8,9},{9,8},{10,11... | collective-permute-start | bytes 786440 | tf_op jit(solution)/shard_map/ppermute | solution.py:554

commit v6 on v5

--- a/solution.py
+++ b/solution.py
@@ -323,7 +323,7 @@
 
 
 def down_kernel(
-    replies, chain_k, transfer, couplings, both, basis, near, give, output, keep
+    replies, chain_k, transfer, couplings, both, fields, give, keep
 ):
     core = lax.axis_index("rhs")
     table = replies[...].astype(F32)
@@ -351,7 +351,12 @@
             rows = both[leaf, pl.ds(first, RANK), :]
             target[leaf] = mm(jnp.concatenate([rows, rows], axis=1), terms).astype(target.dtype)
     for leaf in range(LEAVES):
-        far = mm(now[leaf][:DIM].astype(BF16), basis[leaf], NT)
+        fields[leaf] = now[leaf][:DIM].astype(BF16)
+
+
+def finish_kernel(fields, basis, near, output):
+    for leaf in range(LEAVES):
+        far = mm(fields[leaf], basis[leaf], NT)
         output[:, pl.ds(leaf * ROWS, ROWS)] = (near[leaf] + far).astype(BF16)
 
 
@@ -534,24 +539,23 @@
         ],
         cost=(5 * 10**10, 4 * 10**6, LEAVES * 800000),
         places=HBM,
-        room=60,
+        room=14,
     )(near_ids, near_valid, swaps[0], joined, swaps[1], reply)
 
-    give, output, keep = call(
+    fields, give, keep = call(
         down_kernel,
-        (sds(square, BF16), sds((DIM, LEAVES * ROWS), BF16), sds(square, F32)),
-        [VMEM] * 7,
+        (sds((LEAVES, DIM, RANK), BF16), sds(square, BF16), sds(square, F32)),
+        [VMEM] * 5,
         room=14,
-    )(
-        replies,
-        chain_k,
-        local_transfer,
-        couplings,
-        both,
-        leaf_basis,
-        near,
-    )
+    )(replies, chain_k, local_transfer, couplings, both)
     got = lax.ppermute(give, "rhs", [(0, 1), (1, 0)])
+    output = call(
+        finish_kernel,
+        sds((DIM, LEAVES * ROWS), BF16),
+        [VMEM] * 3,
+        cost=(3 * 10**9, 2 * 10**6, 0),
+        room=14,
+    )(fields, leaf_basis, near)
     basis_grad = (keep + got.astype(F32)).astype(BF16)
     return output.T, basis_grad
 

time: 74 us -> 71.8 us (0.970)
  starting transfers between devices: 37 us -> 34.2 us
  waiting for transfers between devices: 7.79 us -> 10.2 us
  local copies, waits for them, and re-layouts: 1.87 us -> 0.88 us
  Pallas kernels: 25.2 us -> 24.4 us
    all_to_all x1, waiting for transfers between devices: 5.48 us -> 7.24 us  [local(): lax.all_to_all(total, 'pts', 0, 0, axis_index_groups=across, tiled=True)]
    all_to_all x1, waiting for transfers between devices: 1.16 us -> 2.8 us  [local(): lax.all_to_all(send, 'pts', 0, 0, axis_index_groups=groups, tiled=True)]
    ppermute x2, starting transfers between devices: 6.35 us -> 4.72 us  [local(): lax.ppermute(joined, 'pts', pairs + [(b, a) for a, b in pairs])]
    ppermute x1, waiting for transfers between devices: 1.14 us -> 0.12 us  [local(): got = lax.ppermute(give, 'rhs', [(0, 1), (1, 0)])]
    unnamed x16 -> x22, local copies, waits for them, and re-layouts: 1.87 us -> 0.88 us
    pallas_call x1, Pallas kernels: 12.2 us -> 11.2 us  [local(): call(near_kernel, sds((LEAVES, DIM, ROWS), F32), [HBM] * 5 + [ANY], [pltp...]
    pallas_call x1 -> x2, Pallas kernels: 1.88 us -> 2.03 us  [the longest x1 1.03 us: local(): call(down_kernel, (sds((LEAVES, DIM, RANK), BF16), sds(square, BF16), sds...]
  transfers between devices with their start and end apart: 6 -> 6, of which waited for: 3 -> 3; matrix products, arithmetic and copies ran while one was open for 0% -> 0% of each run, Pallas kernels for 25% -> 26%
where the time goes in v6:
time: 71.8 us; the launch traced here: 71.3 us
  starting transfers between devices  34.2 us (48%)
  Pallas kernels  24.4 us (34%)
  waiting for transfers between devices  10.2 us (14%)
  local copies, waits for them, and re-layouts  0.88 us (1%)
  between operations  0.84 us (1%)
  other arithmetic  0.76 us (1%)
    all_to_all x1, starting transfers between devices, local(): lax.all_to_all(total, 'pts', 0, 0, axis_index_groups=across, tiled=True)  11.8 us
    pallas_call x1, Pallas kernels, local(): call(near_kernel, sds((LEAVES, DIM, ROWS), F32), [HBM] * 5 + [ANY], [pltp...  11.2 us
    all_to_all x1, starting transfers between devices, local(): lax.all_to_all(send, 'pts', 0, 0, axis_index_groups=groups, tiled=True)  9.58 us
    all_to_all x1, waiting for transfers between devices, local(): lax.all_to_all(total, 'pts', 0, 0, axis_index_groups=across, tiled=True)  7.24 us
    pallas_call x1, Pallas kernels, local(): call(rise_kernel, (sds(block, BF16), sds((14, RANK, RANK), F32), sds((MEM...  4.82 us
    ppermute x2, starting transfers between devices, local(): lax.ppermute(joined, 'pts', pairs + [(b, a) for a, b in pairs])  4.72 us
    pallas_call x1, Pallas kernels, local(): call(couple_kernel, (sds(tree, F32), sds(links, BF16), sds(block, BF16)),...  4.53 us
    ppermute x1, starting transfers between devices, local(): got = lax.ppermute(give, 'rhs', [(0, 1), (1, 0)])  4.49 us
  transfers between devices with their start and end apart: 6, of which 3 were waited for; matrix products, arithmetic and copies ran while one was open for 0% of the time, Pallas kernels for 26%

profile of v6, /device:TPU:1, one launch (start us, length us, event | category | flops | bytes accessed | tf_op | source)
XLA Modules:
  0.0 71.3 jit_solution(14593171778218158314)
XLA Ops:
  0.6 4.8 %shard_map.140 = (bf16[8,256,128]{2,1,0:T(8,128)(2,1)}, f32[14,128,128]{2,1,0:T(8,128)}, bf16[16,48,128]{2,1,0:T(8,128)(2,1)}) custom-call(bf16[64,2048]{1,0:T(8,128)(2,1)} %bitcast.10, bf16[64,2048]{1,0:T(8,128)(2,1)} %bitcast.11, s32[16,128]{1,0:T(8,128)} %bitcast.14, bf16[64,2048]{1,0:T(8,128)(2,1)} %bitcast.12, bf16[8,256,128]{2,1,0:T(8,128)(2,1)} %basis.3, ...), custom_call_target="tpu_custom_call" | custom-call | tf_op jit(solution)/shard_map/pallas_call | solution.py:454
  5.5 9.6 %all-to-all-start = ((bf16[16,48,128]{2,1,0:T(8,128)(2,1)}), bf16[16,48,128]{2,1,0:T(8,128)(2,1)S(1)}, u32[]{:S(2)}, u32[]{:S(2)}) async-start(bf16[16,48,128]{2,1,0:T(8,128)(2,1)} %get-tuple-element.11), calls=%async_computation | async-start | bytes 393216 | tf_op jit(solution)/shard_map/all_to_all | solution.py:481
  15.0 3.3 %collective-permute-start = (bf16[8,256,128]{2,1,0:T(8,128)(2,1)}, bf16[8,256,128]{2,1,0:T(8,128)(2,1)S(1)}, u32[]{:S(2)}, u32[]{:S(2)}) collective-permute-start(bf16[8,256,128]{2,1,0:T(8,128)(2,1)} %get-tuple-element.13.joined.own), channel_id=1, source_target_pairs={{0,2},{4,6},{8,10},{12,14},{16,18},{20,22},{24,26},{28,30},{32,34}... | collective-permute-start | bytes 1572872 | tf_op jit(solution)/shard_map/ppermute | solution.py:486
  18.3 1.5 %collective-permute-start.1 = (bf16[8,256,128]{2,1,0:T(8,128)(2,1)}, bf16[8,256,128]{2,1,0:T(8,128)(2,1)}, u32[]{:S(2)}, u32[]{:S(2)}) collective-permute-start(bf16[8,256,128]{2,1,0:T(8,128)(2,1)} %get-tuple-element.13.joined.own), channel_id=1, source_target_pairs={{2,4},{6,8},{10,12},{14,16},{18,20},{22,24},{26,28},{30,32},{34,36... | collective-permute-start | bytes 1572872 | tf_op jit(solution)/shard_map/ppermute | solution.py:486
  19.8 2.8 %all-to-all-done.received = bf16[16,48,128]{2,1,0:T(8,128)(2,1)S(1)} async-done(((bf16[16,48,128]{2,1,0:T(8,128)(2,1)}), bf16[16,48,128]{2,1,0:T(8,128)(2,1)S(1)}, u32[]{:S(2)}, u32[]{:S(2)}) %all-to-all-start) | async-done | bytes 196640 | tf_op jit(solution)/shard_map/all_to_all | solution.py:481
  22.6 0.6 shard_map.141.after
  23.2 11.8 %all-to-all-start.1 = ((bf16[16,16,128]{2,1,0:T(8,128)(2,1)}), bf16[16,16,128]{2,1,0:T(8,128)(2,1)S(1)}, u32[]{:S(2)}, u32[]{:S(2)}) async-start(bf16[16,16,128]{2,1,0:T(8,128)(2,1)} %shard_map.141.after), calls=%async_computation.1 | async-start | bytes 131072 | tf_op jit(solution)/shard_map/all_to_all | solution.py:491
  35.0 0.0 copy-start.4
  35.0 4.5 %shard_map.143 = (f32[14,128,128]{2,1,0:T(8,128)}, bf16[5,128,128]{2,1,0:T(8,128)(2,1)}, bf16[8,256,128]{2,1,0:T(8,128)(2,1)}) custom-call(f32[14,128,128]{2,1,0:T(8,128)} %get-tuple-element.12.coeffs, bf16[8,256,128]{2,1,0:T(8,128)(2,1)} %get-tuple-element.13.joined.own, bf16[64,2048]{1,0:T(8,128)(2,1)} %bitcast.13, bf16[8,64,128]{2,1,0:T(8,128)(2,1)} %bitcast.15, ...), custom_call_target="tpu_custom_call" | custom-call | flops 2000000000 | bytes 4000000 | tf_op jit(solution)/shard_map/pallas_call | solution.py:496
  39.5 7.2 %all-to-all-done.1.totals = bf16[16,16,128]{2,1,0:T(8,128)(2,1)S(1)} async-done(((bf16[16,16,128]{2,1,0:T(8,128)(2,1)}), bf16[16,16,128]{2,1,0:T(8,128)(2,1)S(1)}, u32[]{:S(2)}, u32[]{:S(2)}) %all-to-all-start.1) | async-done | bytes 65568 | tf_op jit(solution)/shard_map/all_to_all | solution.py:491
  46.8 1.2 %shard_map.142.after = bf16[16,48,128]{2,1,0:T(8,128)(2,1)} custom-call(bf16[16,48,128]{2,1,0:T(8,128)(2,1)S(1)} %all-to-all-done.received, bf16[16,16,128]{2,1,0:T(8,128)(2,1)S(1)} %all-to-all-done.1.totals, bf16[16,64,128]{2,1,0:T(8,128)(2,1)S(1)} %bitcast.9), custom_call_target="tpu_custom_call" | custom-call | tf_op jit(solution)/shard_map/pallas_call | solution.py:518
  47.9 3.7 %all-to-all-start.2 = ((bf16[16,48,128]{2,1,0:T(8,128)(2,1)}), bf16[16,48,128]{2,1,0:T(8,128)(2,1)S(1)}, u32[]{:S(2)}, u32[]{:S(2)}) async-start(bf16[16,48,128]{2,1,0:T(8,128)(2,1)} %shard_map.142.after), calls=%async_computation.2 | async-start | bytes 393216 | tf_op jit(solution)/shard_map/all_to_all | solution.py:521
  51.6 0.0 copy-start
  51.7 0.0 copy-start.5
  51.7 0.0 collective-permute-done.swap_a
  51.7 0.0 collective-permute-done.1.swap_b
  51.7 11.2 %shard_map.145.near = f32[8,64,256]{2,1,0:T(8,128)S(1)} custom-call(s32[8,12]{1,0:T(8,128)S(1)} %copy-done.7, s32[8,12]{1,0:T(8,128)S(1)} %copy-done.8, bf16[8,256,128]{2,1,0:T(8,128)(2,1)S(1)} %collective-permute-done.swap_a, bf16[8,256,128]{2,1,0:T(8,128)(2,1)S(1)} %copy-done.6, bf16[8,256,128]{2,1,0:T(8,128)(2,1)} %collective-permute-done.1.swap_b, ...), custom_call_target="tpu_custom_call" | custom-call | flops 49999998976 | bytes 4000000 | tf_op jit(solution)/shard_map/pallas_call | solution.py:523
  63.0 0.8 %copy-done.9 = f32[8,64,256]{2,1,0:T(8,128)} copy-done((f32[8,64,256]{2,1,0:T(8,128)}, f32[8,64,256]{2,1,0:T(8,128)S(1)}, u32[]{:S(2)}) %copy-start.9) | copy-done | bytes 524312
  63.8 0.0 copy-start.3
  63.9 1.0 %shard_map.144 = (bf16[8,64,128]{2,1,0:T(8,128)(2,1)S(1)}, bf16[8,128,128]{2,1,0:T(8,128)(2,1)S(1)}, f32[8,128,128]{2,1,0:T(8,128)S(1)}) custom-call(bf16[16,48,128]{2,1,0:T(8,128)(2,1)S(1)} %all-to-all-done.2.replies, bf16[5,128,128]{2,1,0:T(8,128)(2,1)S(1)} %copy-done.5, bf16[7,256,128]{2,1,0:T(8,128)(2,1)S(1)} %copy-done, f32[14,128,128]{2,1,0:T(8,128)S(1)} %copy-done.1, ...), custom_call_target="tpu_custom_call" | custom-call | tf_op jit(solution)/shard_map/pallas_call | solution.py:545
  64.9 4.5 %collective-permute-start.2 = (bf16[8,128,128]{2,1,0:T(8,128)(2,1)S(1)}, bf16[8,128,128]{2,1,0:T(8,128)(2,1)S(1)}, u32[]{:S(2)}, u32[]{:S(2)}) collective-permute-start(bf16[8,128,128]{2,1,0:T(8,128)(2,1)S(1)} %get-tuple-element.19), channel_id=1, source_target_pairs={{0,1},{1,0},{2,3},{3,2},{4,5},{5,4},{6,7},{7,6},{8,9},{9,8},{10,11... | collective-permute-start | bytes 786440 | tf_op jit(solution)/shard_map/ppermute | solution.py:551
  69.4 1.0 %shard_map.146 = bf16[64,2048]{1,0:T(8,128)(2,1)} custom-call(bf16[8,64,128]{2,1,0:T(8,128)(2,1)S(1)} %get-tuple-element.17.fields, bf16[8,256,128]{2,1,0:T(8,128)(2,1)S(1)} %copy-done.3, f32[8,64,256]{2,1,0:T(8,128)S(1)} %copy-done.10), custom_call_target="tpu_custom_call" | custom-call | flops 3000000000 | bytes 2000000 | tf_op jit(solution)/shard_map/pallas_call | solution.py:552
  70.4 0.1 collective-permute-done.2
  70.5 0.8 %add_convert_fusion = bf16[8,128,128]{2,1,0:T(8,128)(2,1)} fusion(f32[8,128,128]{2,1,0:T(8,128)S(1)} %get-tuple-element.18, bf16[8,128,128]{2,1,0:T(8,128)(2,1)S(1)} %collective-permute-done.2), kind=kLoop, calls=%fused_computation | loop fusion | flops 393216 | bytes 1048576 | tf_op jit(solution)/shard_map/convert_element_type | solution.py:559
  (18 shorter events, 0.0 us)
Async XLA Ops:
  5.5 17.1 %all-to-all-start = ((bf16[16,48,128]{2,1,0:T(8,128)(2,1)}), bf16[16,48,128]{2,1,0:T(8,128)(2,1)S(1)}, u32[]{:S(2)}, u32[]{:S(2)}) async-start(bf16[16,48,128]{2,1,0:T(8,128)(2,1)} %get-tuple-element.11), calls=%async_computation | async-start | bytes 393216 | tf_op jit(solution)/shard_map/all_to_all | solution.py:481
  15.0 36.7 %collective-permute-start = (bf16[8,256,128]{2,1,0:T(8,128)(2,1)}, bf16[8,256,128]{2,1,0:T(8,128)(2,1)S(1)}, u32[]{:S(2)}, u32[]{:S(2)}) collective-permute-start(bf16[8,256,128]{2,1,0:T(8,128)(2,1)} %get-tuple-element.13.joined.own), channel_id=1, source_target_pairs={{0,2},{4,6},{8,10},{12,14},{16,18},{20,22},{24,26},{28,30},{32,34}... | collective-permute-start | bytes 1572872 | tf_op jit(solution)/shard_map/ppermute | solution.py:486
  18.3 33.4 %collective-permute-start.1 = (bf16[8,256,128]{2,1,0:T(8,128)(2,1)}, bf16[8,256,128]{2,1,0:T(8,128)(2,1)}, u32[]{:S(2)}, u32[]{:S(2)}) collective-permute-start(bf16[8,256,128]{2,1,0:T(8,128)(2,1)} %get-tuple-element.13.joined.own), channel_id=1, source_target_pairs={{2,4},{6,8},{10,12},{14,16},{18,20},{22,24},{26,28},{30,32},{34,36... | collective-permute-start | bytes 1572872 | tf_op jit(solution)/shard_map/ppermute | solution.py:486
  23.2 23.6 %all-to-all-start.1 = ((bf16[16,16,128]{2,1,0:T(8,128)(2,1)}), bf16[16,16,128]{2,1,0:T(8,128)(2,1)S(1)}, u32[]{:S(2)}, u32[]{:S(2)}) async-start(bf16[16,16,128]{2,1,0:T(8,128)(2,1)} %shard_map.141.after), calls=%async_computation.1 | async-start | bytes 131072 | tf_op jit(solution)/shard_map/all_to_all | solution.py:491
  35.0 11.8 %copy-start.4 = (bf16[16,128,64]{1,2,0:T(8,128)(2,1)S(1)}, bf16[16,128,64]{1,2,0:T(8,128)(2,1)}, u32[]{:S(2)}) copy-start(bf16[16,128,64]{1,2,0:T(8,128)(2,1)} %param.25) | copy-start | bytes 786436
  46.8 4.9 %copy-start.6 = (bf16[8,256,128]{2,1,0:T(8,128)(2,1)S(1)}, bf16[8,256,128]{2,1,0:T(8,128)(2,1)}, u32[]{:S(2)}) copy-start(bf16[8,256,128]{2,1,0:T(8,128)(2,1)} %get-tuple-element.13.joined.own) | copy-start | bytes 1572868
  47.9 3.8 %copy-start.7 = (s32[8,12]{1,0:T(8,128)S(1)}, s32[8,12]{1,0:T(8,128)}, u32[]{:S(2)}) copy-start(s32[8,12]{1,0:T(8,128)} %ids.1) | copy-start | bytes 1156
  47.9 3.8 %copy-start.8 = (s32[8,12]{1,0:T(8,128)S(1)}, s32[8,12]{1,0:T(8,128)}, u32[]{:S(2)}) copy-start(s32[8,12]{1,0:T(8,128)} %valid.1) | copy-start | bytes 1156
  47.9 15.9 %all-to-all-start.2 = ((bf16[16,48,128]{2,1,0:T(8,128)(2,1)}), bf16[16,48,128]{2,1,0:T(8,128)(2,1)S(1)}, u32[]{:S(2)}, u32[]{:S(2)}) async-start(bf16[16,48,128]{2,1,0:T(8,128)(2,1)} %shard_map.142.after), calls=%async_computation.2 | async-start | bytes 393216 | tf_op jit(solution)/shard_map/all_to_all | solution.py:521
  51.6 12.2 %copy-start = (bf16[7,256,128]{2,1,0:T(8,128)(2,1)S(1)}, bf16[7,256,128]{2,1,0:T(8,128)(2,1)}, u32[]{:S(2)}) copy-start(bf16[7,256,128]{2,1,0:T(8,128)(2,1)} %transfer.3) | copy-start | bytes 1376260
  51.7 12.2 %copy-start.1 = (f32[14,128,128]{2,1,0:T(8,128)S(1)}, f32[14,128,128]{2,1,0:T(8,128)}, u32[]{:S(2)}) copy-start(f32[14,128,128]{2,1,0:T(8,128)} %get-tuple-element.15.couplings) | copy-start | bytes 2752516
  51.7 12.2 %copy-start.2 = (bf16[8,256,128]{2,1,0:T(8,128)(2,1)S(1)}, bf16[8,256,128]{2,1,0:T(8,128)(2,1)}, u32[]{:S(2)}) copy-start(bf16[8,256,128]{2,1,0:T(8,128)(2,1)} %get-tuple-element.16.both) | copy-start | bytes 1572868
  51.7 12.2 %copy-start.5 = (bf16[5,128,128]{2,1,0:T(8,128)(2,1)S(1)}, bf16[5,128,128]{2,1,0:T(8,128)(2,1)}, u32[]{:S(2)}) copy-start(bf16[5,128,128]{2,1,0:T(8,128)(2,1)} %get-tuple-element.14.chain_k) | copy-start | bytes 491524
  63.0 0.8 %copy-start.9 = (f32[8,64,256]{2,1,0:T(8,128)}, f32[8,64,256]{2,1,0:T(8,128)S(1)}, u32[]{:S(2)}) copy-start(f32[8,64,256]{2,1,0:T(8,128)S(1)} %shard_map.145.near) | copy-start | bytes 1572868
  63.8 5.6 %copy-start.3 = (bf16[8,256,128]{2,1,0:T(8,128)(2,1)S(1)}, bf16[8,256,128]{2,1,0:T(8,128)(2,1)}, u32[]{:S(2)}) copy-start(bf16[8,256,128]{2,1,0:T(8,128)(2,1)} %basis.3) | copy-start | bytes 1572868
  63.8 5.6 %copy-start.10 = (f32[8,64,256]{2,1,0:T(8,128)S(1)}, f32[8,64,256]{2,1,0:T(8,128)}, u32[]{:S(2)}) copy-start(f32[8,64,256]{2,1,0:T(8,128)} %copy-done.9) | copy-start | bytes 1572868
  64.9 5.6 %collective-permute-start.2 = (bf16[8,128,128]{2,1,0:T(8,128)(2,1)S(1)}, bf16[8,128,128]{2,1,0:T(8,128)(2,1)S(1)}, u32[]{:S(2)}, u32[]{:S(2)}) collective-permute-start(bf16[8,128,128]{2,1,0:T(8,128)(2,1)S(1)} %get-tuple-element.19), channel_id=1, source_target_pairs={{0,1},{1,0},{2,3},{3,2},{4,5},{5,4},{6,7},{7,6},{8,9},{9,8},{10,11... | collective-permute-start | bytes 786440 | tf_op jit(solution)/shard_map/ppermute | solution.py:551

commit v7 on v6

--- a/solution.py
+++ b/solution.py
@@ -308,13 +308,14 @@
 def reply_kernel(received, totals, top_skel, reply):
     flat = jnp.concatenate([totals[group] for group in range(GROUPS)], axis=1)
     group = jnp.right_shift(lax.axis_index("pts"), LEVELS)
-    (mine,) = extended(top_skel[group], False, True)
+    (mine,) = extended(top_skel[group], True, False)
+    mine = mine.T
     top_k = []
     for other in range(GROUPS):
-        (theirs,) = extended(top_skel[other], True, False)
-        value = jnp.exp2(mm(theirs.T, mine) * EXPO)
+        (theirs,) = extended(top_skel[other], False, True)
+        value = jnp.exp2(mm(mine, theirs) * EXPO)
         top_k.append(jnp.where(group == other, 0.0, value).astype(BF16))
-    field = mm(flat, jnp.concatenate(top_k, axis=0))[:SHARE]
+    field = mm(flat, jnp.concatenate(top_k, axis=1), NT)[:SHARE]
     levels = [level_sums(received, level) for level in range(LEVELS)]
     blank = jnp.zeros((SHARE, RANK), F32)
     for member in range(MEMBERS):
@@ -384,7 +385,8 @@
         ((own, own_v), (swap_a, swap_a_v), (swap_b, swap_b_v), (ids, ids_v), (valid, valid_v)),
         sems,
     )
-    lane = lanes(ROWS)
+    lane = lanes(ROWS).astype(F32).astype(BF16)
+    edge = jnp.full((), DIM, BF16)
     device = lax.axis_index("pts")
     odd = jnp.bitwise_and(device, 1)
     places = ((2 - 2 * odd) * LEAVES, LEAVES, 2 * odd * LEAVES)
@@ -394,11 +396,10 @@
             value = block[leaf]
             turned = value.T
             made = norm_rows(turned[DIM:], index == 1, True)
-            spare = jnp.concatenate([made[-1].T, jnp.zeros((ROWS, 112), F32)], axis=1)
+            spare = made[-1].astype(BF16).T
+            spare = jnp.concatenate([spare, jnp.zeros((ROWS, 112), BF16)], axis=1)
             values[places[index] + leaf] = turned[:DIM]
-            right[places[index] + leaf] = jnp.where(
-                lane < DIM, spare, value.astype(F32)
-            ).astype(BF16)
+            right[places[index] + leaf] = jnp.where(lane < edge, spare, value)
             if index == 1:
                 blank = jnp.zeros((DIM - 16, ROWS), BF16)
                 left[leaf] = jnp.concatenate(

time: 71.8 us -> 70.8 us (0.986)
  Pallas kernels: 24.4 us -> 23.4 us
    pallas_call x1, Pallas kernels: 11.2 us -> 10.2 us  [local(): call(near_kernel, sds((LEAVES, DIM, ROWS), F32), [HBM] * 5 + [ANY], [pltp...]
  transfers between devices with their start and end apart: 6 -> 6, of which waited for: 3 -> 3; matrix products, arithmetic and copies ran while one was open for 0% -> 0% of each run, Pallas kernels for 26% -> 25%
where the time goes in v7:
time: 70.8 us; the launch traced here: 70.3 us
  starting transfers between devices  34.2 us (48%)
  Pallas kernels  23.4 us (33%)
  waiting for transfers between devices  10.2 us (14%)
  local copies, waits for them, and re-layouts  0.88 us (1%)
  between operations  0.84 us (1%)
  other arithmetic  0.76 us (1%)
    all_to_all x1, starting transfers between devices, local(): lax.all_to_all(total, 'pts', 0, 0, axis_index_groups=across, tiled=True)  11.8 us
    pallas_call x1, Pallas kernels, local(): call(near_kernel, sds((LEAVES, DIM, ROWS), F32), [HBM] * 5 + [ANY], [pltp...  10.2 us
    all_to_all x1, starting transfers between devices, local(): lax.all_to_all(send, 'pts', 0, 0, axis_index_groups=groups, tiled=True)  9.58 us
    all_to_all x1, waiting for transfers between devices, local(): lax.all_to_all(total, 'pts', 0, 0, axis_index_groups=across, tiled=True)  7.24 us
    pallas_call x1, Pallas kernels, local(): call(rise_kernel, (sds(block, BF16), sds((14, RANK, RANK), F32), sds((MEM...  4.82 us
    ppermute x2, starting transfers between devices, local(): lax.ppermute(joined, 'pts', pairs + [(b, a) for a, b in pairs])  4.72 us
    pallas_call x1, Pallas kernels, local(): call(couple_kernel, (sds(tree, F32), sds(links, BF16), sds(block, BF16)),...  4.53 us
    ppermute x1, starting transfers between devices, local(): got = lax.ppermute(give, 'rhs', [(0, 1), (1, 0)])  4.49 us
  transfers between devices with their start and end apart: 6, of which 3 were waited for; matrix products, arithmetic and copies ran while one was open for 0% of the time, Pallas kernels for 25%

profile of v7, /device:TPU:1, one launch (start us, length us, event | category | flops | bytes accessed | tf_op | source)
XLA Modules:
  0.0 70.3 jit_solution(14788315142338832199)
XLA Ops:
  0.6 4.8 %shard_map.140 = (bf16[8,256,128]{2,1,0:T(8,128)(2,1)}, f32[14,128,128]{2,1,0:T(8,128)}, bf16[16,48,128]{2,1,0:T(8,128)(2,1)}) custom-call(bf16[64,2048]{1,0:T(8,128)(2,1)} %bitcast.10, bf16[64,2048]{1,0:T(8,128)(2,1)} %bitcast.11, s32[16,128]{1,0:T(8,128)} %bitcast.14, bf16[64,2048]{1,0:T(8,128)(2,1)} %bitcast.12, bf16[8,256,128]{2,1,0:T(8,128)(2,1)} %basis.3, ...), custom_call_target="tpu_custom_call" | custom-call | tf_op jit(solution)/shard_map/pallas_call | solution.py:455
  5.5 9.6 %all-to-all-start = ((bf16[16,48,128]{2,1,0:T(8,128)(2,1)}), bf16[16,48,128]{2,1,0:T(8,128)(2,1)S(1)}, u32[]{:S(2)}, u32[]{:S(2)}) async-start(bf16[16,48,128]{2,1,0:T(8,128)(2,1)} %get-tuple-element.11), calls=%async_computation | async-start | bytes 393216 | tf_op jit(solution)/shard_map/all_to_all | solution.py:482
  15.0 3.3 %collective-permute-start = (bf16[8,256,128]{2,1,0:T(8,128)(2,1)}, bf16[8,256,128]{2,1,0:T(8,128)(2,1)S(1)}, u32[]{:S(2)}, u32[]{:S(2)}) collective-permute-start(bf16[8,256,128]{2,1,0:T(8,128)(2,1)} %get-tuple-element.13.joined.own), channel_id=1, source_target_pairs={{0,2},{4,6},{8,10},{12,14},{16,18},{20,22},{24,26},{28,30},{32,34}... | collective-permute-start | bytes 1572872 | tf_op jit(solution)/shard_map/ppermute | solution.py:487
  18.3 1.5 %collective-permute-start.1 = (bf16[8,256,128]{2,1,0:T(8,128)(2,1)}, bf16[8,256,128]{2,1,0:T(8,128)(2,1)}, u32[]{:S(2)}, u32[]{:S(2)}) collective-permute-start(bf16[8,256,128]{2,1,0:T(8,128)(2,1)} %get-tuple-element.13.joined.own), channel_id=1, source_target_pairs={{2,4},{6,8},{10,12},{14,16},{18,20},{22,24},{26,28},{30,32},{34,36... | collective-permute-start | bytes 1572872 | tf_op jit(solution)/shard_map/ppermute | solution.py:487
  19.8 2.8 %all-to-all-done.received = bf16[16,48,128]{2,1,0:T(8,128)(2,1)S(1)} async-done(((bf16[16,48,128]{2,1,0:T(8,128)(2,1)}), bf16[16,48,128]{2,1,0:T(8,128)(2,1)S(1)}, u32[]{:S(2)}, u32[]{:S(2)}) %all-to-all-start) | async-done | bytes 196640 | tf_op jit(solution)/shard_map/all_to_all | solution.py:482
  22.6 0.6 shard_map.141.after
  23.2 11.8 %all-to-all-start.1 = ((bf16[16,16,128]{2,1,0:T(8,128)(2,1)}), bf16[16,16,128]{2,1,0:T(8,128)(2,1)S(1)}, u32[]{:S(2)}, u32[]{:S(2)}) async-start(bf16[16,16,128]{2,1,0:T(8,128)(2,1)} %shard_map.141.after), calls=%async_computation.1 | async-start | bytes 131072 | tf_op jit(solution)/shard_map/all_to_all | solution.py:492
  35.0 0.0 copy-start.4
  35.0 4.5 %shard_map.143 = (f32[14,128,128]{2,1,0:T(8,128)}, bf16[5,128,128]{2,1,0:T(8,128)(2,1)}, bf16[8,256,128]{2,1,0:T(8,128)(2,1)}) custom-call(f32[14,128,128]{2,1,0:T(8,128)} %get-tuple-element.12.coeffs, bf16[8,256,128]{2,1,0:T(8,128)(2,1)} %get-tuple-element.13.joined.own, bf16[64,2048]{1,0:T(8,128)(2,1)} %bitcast.13, bf16[8,64,128]{2,1,0:T(8,128)(2,1)} %bitcast.15, ...), custom_call_target="tpu_custom_call" | custom-call | flops 2000000000 | bytes 4000000 | tf_op jit(solution)/shard_map/pallas_call | solution.py:497
  39.5 7.2 %all-to-all-done.1.totals = bf16[16,16,128]{2,1,0:T(8,128)(2,1)S(1)} async-done(((bf16[16,16,128]{2,1,0:T(8,128)(2,1)}), bf16[16,16,128]{2,1,0:T(8,128)(2,1)S(1)}, u32[]{:S(2)}, u32[]{:S(2)}) %all-to-all-start.1) | async-done | bytes 65568 | tf_op jit(solution)/shard_map/all_to_all | solution.py:492
  46.8 1.2 %shard_map.142.after = bf16[16,48,128]{2,1,0:T(8,128)(2,1)} custom-call(bf16[16,48,128]{2,1,0:T(8,128)(2,1)S(1)} %all-to-all-done.received, bf16[16,16,128]{2,1,0:T(8,128)(2,1)S(1)} %all-to-all-done.1.totals, bf16[16,64,128]{2,1,0:T(8,128)(2,1)S(1)} %bitcast.9), custom_call_target="tpu_custom_call" | custom-call | tf_op jit(solution)/shard_map/pallas_call | solution.py:519
  48.0 3.7 %all-to-all-start.2 = ((bf16[16,48,128]{2,1,0:T(8,128)(2,1)}), bf16[16,48,128]{2,1,0:T(8,128)(2,1)S(1)}, u32[]{:S(2)}, u32[]{:S(2)}) async-start(bf16[16,48,128]{2,1,0:T(8,128)(2,1)} %shard_map.142.after), calls=%async_computation.2 | async-start | bytes 393216 | tf_op jit(solution)/shard_map/all_to_all | solution.py:522
  51.7 0.0 copy-start
  51.7 0.0 copy-start.5
  51.8 0.0 collective-permute-done.swap_a
  51.8 10.2 %shard_map.145.near = f32[8,64,256]{2,1,0:T(8,128)S(1)} custom-call(s32[8,12]{1,0:T(8,128)S(1)} %copy-done.7, s32[8,12]{1,0:T(8,128)S(1)} %copy-done.8, bf16[8,256,128]{2,1,0:T(8,128)(2,1)S(1)} %collective-permute-done.swap_a, bf16[8,256,128]{2,1,0:T(8,128)(2,1)S(1)} %copy-done.6, bf16[8,256,128]{2,1,0:T(8,128)(2,1)} %collective-permute-done.1.swap_b, ...), custom_call_target="tpu_custom_call" | custom-call | flops 49999998976 | bytes 4000000 | tf_op jit(solution)/shard_map/pallas_call | solution.py:524
  62.0 0.8 %copy-done.9 = f32[8,64,256]{2,1,0:T(8,128)} copy-done((f32[8,64,256]{2,1,0:T(8,128)}, f32[8,64,256]{2,1,0:T(8,128)S(1)}, u32[]{:S(2)}) %copy-start.9) | copy-done | bytes 524312
  62.8 0.0 all-to-all-done.2.replies
  62.9 0.0 copy-start.3
  62.9 1.0 %shard_map.144 = (bf16[8,64,128]{2,1,0:T(8,128)(2,1)S(1)}, bf16[8,128,128]{2,1,0:T(8,128)(2,1)S(1)}, f32[8,128,128]{2,1,0:T(8,128)S(1)}) custom-call(bf16[16,48,128]{2,1,0:T(8,128)(2,1)S(1)} %all-to-all-done.2.replies, bf16[5,128,128]{2,1,0:T(8,128)(2,1)S(1)} %copy-done.5, bf16[7,256,128]{2,1,0:T(8,128)(2,1)S(1)} %copy-done, f32[14,128,128]{2,1,0:T(8,128)S(1)} %copy-done.1, ...), custom_call_target="tpu_custom_call" | custom-call | tf_op jit(solution)/shard_map/pallas_call | solution.py:546
  63.9 4.5 %collective-permute-start.2 = (bf16[8,128,128]{2,1,0:T(8,128)(2,1)S(1)}, bf16[8,128,128]{2,1,0:T(8,128)(2,1)S(1)}, u32[]{:S(2)}, u32[]{:S(2)}) collective-permute-start(bf16[8,128,128]{2,1,0:T(8,128)(2,1)S(1)} %get-tuple-element.19), channel_id=1, source_target_pairs={{0,1},{1,0},{2,3},{3,2},{4,5},{5,4},{6,7},{7,6},{8,9},{9,8},{10,11... | collective-permute-start | bytes 786440 | tf_op jit(solution)/shard_map/ppermute | solution.py:552
  68.4 1.0 %shard_map.146 = bf16[64,2048]{1,0:T(8,128)(2,1)} custom-call(bf16[8,64,128]{2,1,0:T(8,128)(2,1)S(1)} %get-tuple-element.17.fields, bf16[8,256,128]{2,1,0:T(8,128)(2,1)S(1)} %copy-done.3, f32[8,64,256]{2,1,0:T(8,128)S(1)} %copy-done.10), custom_call_target="tpu_custom_call" | custom-call | flops 3000000000 | bytes 2000000 | tf_op jit(solution)/shard_map/pallas_call | solution.py:553
  69.4 0.1 collective-permute-done.2
  69.6 0.8 %add_convert_fusion = bf16[8,128,128]{2,1,0:T(8,128)(2,1)} fusion(f32[8,128,128]{2,1,0:T(8,128)S(1)} %get-tuple-element.18, bf16[8,128,128]{2,1,0:T(8,128)(2,1)S(1)} %collective-permute-done.2), kind=kLoop, calls=%fused_computation | loop fusion | flops 393216 | bytes 1048576 | tf_op jit(solution)/shard_map/convert_element_type | solution.py:560
  (18 shorter events, 0.0 us)
Async XLA Ops:
  5.5 17.1 %all-to-all-start = ((bf16[16,48,128]{2,1,0:T(8,128)(2,1)}), bf16[16,48,128]{2,1,0:T(8,128)(2,1)S(1)}, u32[]{:S(2)}, u32[]{:S(2)}) async-start(bf16[16,48,128]{2,1,0:T(8,128)(2,1)} %get-tuple-element.11), calls=%async_computation | async-start | bytes 393216 | tf_op jit(solution)/shard_map/all_to_all | solution.py:482
  15.0 36.7 %collective-permute-start = (bf16[8,256,128]{2,1,0:T(8,128)(2,1)}, bf16[8,256,128]{2,1,0:T(8,128)(2,1)S(1)}, u32[]{:S(2)}, u32[]{:S(2)}) collective-permute-start(bf16[8,256,128]{2,1,0:T(8,128)(2,1)} %get-tuple-element.13.joined.own), channel_id=1, source_target_pairs={{0,2},{4,6},{8,10},{12,14},{16,18},{20,22},{24,26},{28,30},{32,34}... | collective-permute-start | bytes 1572872 | tf_op jit(solution)/shard_map/ppermute | solution.py:487
  18.3 33.5 %collective-permute-start.1 = (bf16[8,256,128]{2,1,0:T(8,128)(2,1)}, bf16[8,256,128]{2,1,0:T(8,128)(2,1)}, u32[]{:S(2)}, u32[]{:S(2)}) collective-permute-start(bf16[8,256,128]{2,1,0:T(8,128)(2,1)} %get-tuple-element.13.joined.own), channel_id=1, source_target_pairs={{2,4},{6,8},{10,12},{14,16},{18,20},{22,24},{26,28},{30,32},{34,36... | collective-permute-start | bytes 1572872 | tf_op jit(solution)/shard_map/ppermute | solution.py:487
  23.2 23.6 %all-to-all-start.1 = ((bf16[16,16,128]{2,1,0:T(8,128)(2,1)}), bf16[16,16,128]{2,1,0:T(8,128)(2,1)S(1)}, u32[]{:S(2)}, u32[]{:S(2)}) async-start(bf16[16,16,128]{2,1,0:T(8,128)(2,1)} %shard_map.141.after), calls=%async_computation.1 | async-start | bytes 131072 | tf_op jit(solution)/shard_map/all_to_all | solution.py:492
  35.0 11.8 %copy-start.4 = (bf16[16,128,64]{1,2,0:T(8,128)(2,1)S(1)}, bf16[16,128,64]{1,2,0:T(8,128)(2,1)}, u32[]{:S(2)}) copy-start(bf16[16,128,64]{1,2,0:T(8,128)(2,1)} %param.25) | copy-start | bytes 786436
  46.8 5.0 %copy-start.6 = (bf16[8,256,128]{2,1,0:T(8,128)(2,1)S(1)}, bf16[8,256,128]{2,1,0:T(8,128)(2,1)}, u32[]{:S(2)}) copy-start(bf16[8,256,128]{2,1,0:T(8,128)(2,1)} %get-tuple-element.13.joined.own) | copy-start | bytes 1572868
  48.0 3.8 %copy-start.7 = (s32[8,12]{1,0:T(8,128)S(1)}, s32[8,12]{1,0:T(8,128)}, u32[]{:S(2)}) copy-start(s32[8,12]{1,0:T(8,128)} %ids.1) | copy-start | bytes 1156
  48.0 3.8 %copy-start.8 = (s32[8,12]{1,0:T(8,128)S(1)}, s32[8,12]{1,0:T(8,128)}, u32[]{:S(2)}) copy-start(s32[8,12]{1,0:T(8,128)} %valid.1) | copy-start | bytes 1156
  48.0 14.8 %all-to-all-start.2 = ((bf16[16,48,128]{2,1,0:T(8,128)(2,1)}), bf16[16,48,128]{2,1,0:T(8,128)(2,1)S(1)}, u32[]{:S(2)}, u32[]{:S(2)}) async-start(bf16[16,48,128]{2,1,0:T(8,128)(2,1)} %shard_map.142.after), calls=%async_computation.2 | async-start | bytes 393216 | tf_op jit(solution)/shard_map/all_to_all | solution.py:522
  51.7 11.1 %copy-start = (bf16[7,256,128]{2,1,0:T(8,128)(2,1)S(1)}, bf16[7,256,128]{2,1,0:T(8,128)(2,1)}, u32[]{:S(2)}) copy-start(bf16[7,256,128]{2,1,0:T(8,128)(2,1)} %transfer.3) | copy-start | bytes 1376260
  51.7 11.1 %copy-start.1 = (f32[14,128,128]{2,1,0:T(8,128)S(1)}, f32[14,128,128]{2,1,0:T(8,128)}, u32[]{:S(2)}) copy-start(f32[14,128,128]{2,1,0:T(8,128)} %get-tuple-element.15.couplings) | copy-start | bytes 2752516
  51.7 11.1 %copy-start.2 = (bf16[8,256,128]{2,1,0:T(8,128)(2,1)S(1)}, bf16[8,256,128]{2,1,0:T(8,128)(2,1)}, u32[]{:S(2)}) copy-start(bf16[8,256,128]{2,1,0:T(8,128)(2,1)} %get-tuple-element.16.both) | copy-start | bytes 1572868
  51.7 11.1 %copy-start.5 = (bf16[5,128,128]{2,1,0:T(8,128)(2,1)S(1)}, bf16[5,128,128]{2,1,0:T(8,128)(2,1)}, u32[]{:S(2)}) copy-start(bf16[5,128,128]{2,1,0:T(8,128)(2,1)} %get-tuple-element.14.chain_k) | copy-start | bytes 491524
  62.0 0.8 %copy-start.9 = (f32[8,64,256]{2,1,0:T(8,128)}, f32[8,64,256]{2,1,0:T(8,128)S(1)}, u32[]{:S(2)}) copy-start(f32[8,64,256]{2,1,0:T(8,128)S(1)} %shard_map.145.near) | copy-start | bytes 1572868
  62.9 5.6 %copy-start.3 = (bf16[8,256,128]{2,1,0:T(8,128)(2,1)S(1)}, bf16[8,256,128]{2,1,0:T(8,128)(2,1)}, u32[]{:S(2)}) copy-start(bf16[8,256,128]{2,1,0:T(8,128)(2,1)} %basis.3) | copy-start | bytes 1572868
  62.9 5.6 %copy-start.10 = (f32[8,64,256]{2,1,0:T(8,128)S(1)}, f32[8,64,256]{2,1,0:T(8,128)}, u32[]{:S(2)}) copy-start(f32[8,64,256]{2,1,0:T(8,128)} %copy-done.9) | copy-start | bytes 1572868
  63.9 5.6 %collective-permute-start.2 = (bf16[8,128,128]{2,1,0:T(8,128)(2,1)S(1)}, bf16[8,128,128]{2,1,0:T(8,128)(2,1)S(1)}, u32[]{:S(2)}, u32[]{:S(2)}) collective-permute-start(bf16[8,128,128]{2,1,0:T(8,128)(2,1)S(1)} %get-tuple-element.19), channel_id=1, source_target_pairs={{0,1},{1,0},{2,3},{3,2},{4,5},{5,4},{6,7},{7,6},{8,9},{9,8},{10,11... | collective-permute-start | bytes 786440 | tf_op jit(solution)/shard_map/ppermute | solution.py:552

commit v8 on v7

--- a/solution.py
+++ b/solution.py
@@ -246,23 +246,19 @@
 ):
     waits = fetch(
         (
-            (cot, cot_v),
-            (joined, joined_v),
             (chain_skel, skel_v),
             (chain, chain_v),
             (leaf_skel, leaf_v),
             (local_skel, local_v),
             (coeffs, coeffs_v),
+            (cot, cot_v),
+            (joined, joined_v),
         ),
         sems,
     )
     device = lax.axis_index("pts")
-    for wait in waits[:4]:
+    for wait in waits[:2]:
         wait()
-    for leaf in range(LEAVES):
-        theirs = cot_v[:, pl.ds(leaf * ROWS, ROWS)].T
-        both_v[leaf] = jnp.concatenate([joined_v[leaf][:, :DIM], theirs], axis=1)
-    done = fetch(((both_v, both),), out_sems)
     products = chain_products(chain_v, device)
     for level in range(LEVELS):
         bit = jnp.bitwise_and(jnp.right_shift(device, level), 1)
@@ -271,8 +267,8 @@
             value = mm(value, products[level - 1], NT).astype(BF16)
         chain_k_v[level] = value
     chain_k_v[LEVELS] = products[LEVELS - 1].T
-    done += fetch(((chain_k_v, chain_k),), out_sems.at[pl.ds(1, 1)])
-    for wait in waits[4:]:
+    done = fetch(((chain_k_v, chain_k),), out_sems)
+    for wait in waits[2:5]:
         wait()
     for node in range(0, 14, 2):
         if node < 8:
@@ -282,7 +278,13 @@
         near_k = kappa(even, odd).astype(BF16)
         for target, other, dims in ((node, node + 1, NT), (node + 1, node, NN)):
             couplings_v[target] = mm2(coeffs_v[other], near_k, dims)
-    done += fetch(((couplings_v, couplings),), out_sems.at[pl.ds(2, 1)])
+    done += fetch(((couplings_v, couplings),), out_sems.at[pl.ds(1, 1)])
+    for wait in waits[5:]:
+        wait()
+    for leaf in range(LEAVES):
+        theirs = cot_v[:, pl.ds(leaf * ROWS, ROWS)].T
+        both_v[leaf] = jnp.concatenate([joined_v[leaf][:, :DIM], theirs], axis=1)
+    done += fetch(((both_v, both),), out_sems.at[pl.ds(2, 1)])
     for wait in done:
         wait()
 

time: 70.8 us -> 70.8 us (level)
  no operation moved by 1% of the time
where the time goes in v8:
time: 70.8 us; the launch traced here: 70.3 us
  starting transfers between devices  34.2 us (48%)
  Pallas kernels  23.4 us (33%)
  waiting for transfers between devices  10.2 us (14%)
  local copies, waits for them, and re-layouts  0.88 us (1%)
  between operations  0.84 us (1%)
  other arithmetic  0.76 us (1%)
    all_to_all x1, starting transfers between devices, local(): lax.all_to_all(total, 'pts', 0, 0, axis_index_groups=across, tiled=True)  11.8 us
    pallas_call x1, Pallas kernels, local(): call(near_kernel, sds((LEAVES, DIM, ROWS), F32), [HBM] * 5 + [ANY], [pltp...  10.2 us
    all_to_all x1, starting transfers between devices, local(): lax.all_to_all(send, 'pts', 0, 0, axis_index_groups=groups, tiled=True)  9.58 us
    all_to_all x1, waiting for transfers between devices, local(): lax.all_to_all(total, 'pts', 0, 0, axis_index_groups=across, tiled=True)  7.26 us
    pallas_call x1, Pallas kernels, local(): call(rise_kernel, (sds(block, BF16), sds((14, RANK, RANK), F32), sds((MEM...  4.82 us
    ppermute x2, starting transfers between devices, local(): lax.ppermute(joined, 'pts', pairs + [(b, a) for a, b in pairs])  4.72 us
    pallas_call x1, Pallas kernels, local(): call(couple_kernel, (sds(tree, F32), sds(links, BF16), sds(block, BF16)),...  4.52 us
    ppermute x1, starting transfers between devices, local(): got = lax.ppermute(give, 'rhs', [(0, 1), (1, 0)])  4.49 us
  transfers between devices with their start and end apart: 6, of which 3 were waited for; matrix products, arithmetic and copies ran while one was open for 0% of the time, Pallas kernels for 25%

profile of v8, /device:TPU:1, one launch (start us, length us, event | category | flops | bytes accessed | tf_op | source)
XLA Modules:
  0.0 70.3 jit_solution(7564269444259913453)
XLA Ops:
  0.6 4.8 %shard_map.140 = (bf16[8,256,128]{2,1,0:T(8,128)(2,1)}, f32[14,128,128]{2,1,0:T(8,128)}, bf16[16,48,128]{2,1,0:T(8,128)(2,1)}) custom-call(bf16[64,2048]{1,0:T(8,128)(2,1)} %bitcast.10, bf16[64,2048]{1,0:T(8,128)(2,1)} %bitcast.11, s32[16,128]{1,0:T(8,128)} %bitcast.14, bf16[64,2048]{1,0:T(8,128)(2,1)} %bitcast.12, bf16[8,256,128]{2,1,0:T(8,128)(2,1)} %basis.3, ...), custom_call_target="tpu_custom_call" | custom-call | tf_op jit(solution)/shard_map/pallas_call | solution.py:457
  5.5 9.6 %all-to-all-start = ((bf16[16,48,128]{2,1,0:T(8,128)(2,1)}), bf16[16,48,128]{2,1,0:T(8,128)(2,1)S(1)}, u32[]{:S(2)}, u32[]{:S(2)}) async-start(bf16[16,48,128]{2,1,0:T(8,128)(2,1)} %get-tuple-element.11), calls=%async_computation | async-start | bytes 393216 | tf_op jit(solution)/shard_map/all_to_all | solution.py:484
  15.0 3.3 %collective-permute-start = (bf16[8,256,128]{2,1,0:T(8,128)(2,1)}, bf16[8,256,128]{2,1,0:T(8,128)(2,1)S(1)}, u32[]{:S(2)}, u32[]{:S(2)}) collective-permute-start(bf16[8,256,128]{2,1,0:T(8,128)(2,1)} %get-tuple-element.13.joined.own), channel_id=1, source_target_pairs={{0,2},{4,6},{8,10},{12,14},{16,18},{20,22},{24,26},{28,30},{32,34}... | collective-permute-start | bytes 1572872 | tf_op jit(solution)/shard_map/ppermute | solution.py:489
  18.3 1.5 %collective-permute-start.1 = (bf16[8,256,128]{2,1,0:T(8,128)(2,1)}, bf16[8,256,128]{2,1,0:T(8,128)(2,1)}, u32[]{:S(2)}, u32[]{:S(2)}) collective-permute-start(bf16[8,256,128]{2,1,0:T(8,128)(2,1)} %get-tuple-element.13.joined.own), channel_id=1, source_target_pairs={{2,4},{6,8},{10,12},{14,16},{18,20},{22,24},{26,28},{30,32},{34,36... | collective-permute-start | bytes 1572872 | tf_op jit(solution)/shard_map/ppermute | solution.py:489
  19.8 2.8 %all-to-all-done.received = bf16[16,48,128]{2,1,0:T(8,128)(2,1)S(1)} async-done(((bf16[16,48,128]{2,1,0:T(8,128)(2,1)}), bf16[16,48,128]{2,1,0:T(8,128)(2,1)S(1)}, u32[]{:S(2)}, u32[]{:S(2)}) %all-to-all-start) | async-done | bytes 196640 | tf_op jit(solution)/shard_map/all_to_all | solution.py:484
  22.6 0.6 shard_map.141.after
  23.2 11.8 %all-to-all-start.1 = ((bf16[16,16,128]{2,1,0:T(8,128)(2,1)}), bf16[16,16,128]{2,1,0:T(8,128)(2,1)S(1)}, u32[]{:S(2)}, u32[]{:S(2)}) async-start(bf16[16,16,128]{2,1,0:T(8,128)(2,1)} %shard_map.141.after), calls=%async_computation.1 | async-start | bytes 131072 | tf_op jit(solution)/shard_map/all_to_all | solution.py:494
  35.0 0.0 copy-start.4
  35.0 4.5 %shard_map.143 = (f32[14,128,128]{2,1,0:T(8,128)}, bf16[5,128,128]{2,1,0:T(8,128)(2,1)}, bf16[8,256,128]{2,1,0:T(8,128)(2,1)}) custom-call(f32[14,128,128]{2,1,0:T(8,128)} %get-tuple-element.12.coeffs, bf16[8,256,128]{2,1,0:T(8,128)(2,1)} %get-tuple-element.13.joined.own, bf16[64,2048]{1,0:T(8,128)(2,1)} %bitcast.13, bf16[8,64,128]{2,1,0:T(8,128)(2,1)} %bitcast.15, ...), custom_call_target="tpu_custom_call" | custom-call | flops 2000000000 | bytes 4000000 | tf_op jit(solution)/shard_map/pallas_call | solution.py:499
  39.5 7.3 %all-to-all-done.1.totals = bf16[16,16,128]{2,1,0:T(8,128)(2,1)S(1)} async-done(((bf16[16,16,128]{2,1,0:T(8,128)(2,1)}), bf16[16,16,128]{2,1,0:T(8,128)(2,1)S(1)}, u32[]{:S(2)}, u32[]{:S(2)}) %all-to-all-start.1) | async-done | bytes 65568 | tf_op jit(solution)/shard_map/all_to_all | solution.py:494
  46.8 1.2 %shard_map.142.after = bf16[16,48,128]{2,1,0:T(8,128)(2,1)} custom-call(bf16[16,48,128]{2,1,0:T(8,128)(2,1)S(1)} %all-to-all-done.received, bf16[16,16,128]{2,1,0:T(8,128)(2,1)S(1)} %all-to-all-done.1.totals, bf16[16,64,128]{2,1,0:T(8,128)(2,1)S(1)} %bitcast.9), custom_call_target="tpu_custom_call" | custom-call | tf_op jit(solution)/shard_map/pallas_call | solution.py:521
  48.0 3.7 %all-to-all-start.2 = ((bf16[16,48,128]{2,1,0:T(8,128)(2,1)}), bf16[16,48,128]{2,1,0:T(8,128)(2,1)S(1)}, u32[]{:S(2)}, u32[]{:S(2)}) async-start(bf16[16,48,128]{2,1,0:T(8,128)(2,1)} %shard_map.142.after), calls=%async_computation.2 | async-start | bytes 393216 | tf_op jit(solution)/shard_map/all_to_all | solution.py:524
  51.7 0.0 copy-start
  51.7 0.0 copy-start.5
  51.8 0.0 collective-permute-done.swap_a
  51.8 10.2 %shard_map.145.near = f32[8,64,256]{2,1,0:T(8,128)S(1)} custom-call(s32[8,12]{1,0:T(8,128)S(1)} %copy-done.7, s32[8,12]{1,0:T(8,128)S(1)} %copy-done.8, bf16[8,256,128]{2,1,0:T(8,128)(2,1)S(1)} %collective-permute-done.swap_a, bf16[8,256,128]{2,1,0:T(8,128)(2,1)S(1)} %copy-done.6, bf16[8,256,128]{2,1,0:T(8,128)(2,1)} %collective-permute-done.1.swap_b, ...), custom_call_target="tpu_custom_call" | custom-call | flops 49999998976 | bytes 4000000 | tf_op jit(solution)/shard_map/pallas_call | solution.py:526
  62.0 0.8 %copy-done.9 = f32[8,64,256]{2,1,0:T(8,128)} copy-done((f32[8,64,256]{2,1,0:T(8,128)}, f32[8,64,256]{2,1,0:T(8,128)S(1)}, u32[]{:S(2)}) %copy-start.9) | copy-done | bytes 524312
  62.8 0.0 all-to-all-done.2.replies
  62.9 0.0 copy-start.3
  62.9 1.0 %shard_map.144 = (bf16[8,64,128]{2,1,0:T(8,128)(2,1)S(1)}, bf16[8,128,128]{2,1,0:T(8,128)(2,1)S(1)}, f32[8,128,128]{2,1,0:T(8,128)S(1)}) custom-call(bf16[16,48,128]{2,1,0:T(8,128)(2,1)S(1)} %all-to-all-done.2.replies, bf16[5,128,128]{2,1,0:T(8,128)(2,1)S(1)} %copy-done.5, bf16[7,256,128]{2,1,0:T(8,128)(2,1)S(1)} %copy-done, f32[14,128,128]{2,1,0:T(8,128)S(1)} %copy-done.1, ...), custom_call_target="tpu_custom_call" | custom-call | tf_op jit(solution)/shard_map/pallas_call | solution.py:548
  63.9 4.5 %collective-permute-start.2 = (bf16[8,128,128]{2,1,0:T(8,128)(2,1)S(1)}, bf16[8,128,128]{2,1,0:T(8,128)(2,1)S(1)}, u32[]{:S(2)}, u32[]{:S(2)}) collective-permute-start(bf16[8,128,128]{2,1,0:T(8,128)(2,1)S(1)} %get-tuple-element.19), channel_id=1, source_target_pairs={{0,1},{1,0},{2,3},{3,2},{4,5},{5,4},{6,7},{7,6},{8,9},{9,8},{10,11... | collective-permute-start | bytes 786440 | tf_op jit(solution)/shard_map/ppermute | solution.py:554
  68.4 1.0 %shard_map.146 = bf16[64,2048]{1,0:T(8,128)(2,1)} custom-call(bf16[8,64,128]{2,1,0:T(8,128)(2,1)S(1)} %get-tuple-element.17.fields, bf16[8,256,128]{2,1,0:T(8,128)(2,1)S(1)} %copy-done.3, f32[8,64,256]{2,1,0:T(8,128)S(1)} %copy-done.10), custom_call_target="tpu_custom_call" | custom-call | flops 3000000000 | bytes 2000000 | tf_op jit(solution)/shard_map/pallas_call | solution.py:555
  69.4 0.1 collective-permute-done.2
  69.6 0.8 %add_convert_fusion = bf16[8,128,128]{2,1,0:T(8,128)(2,1)} fusion(f32[8,128,128]{2,1,0:T(8,128)S(1)} %get-tuple-element.18, bf16[8,128,128]{2,1,0:T(8,128)(2,1)S(1)} %collective-permute-done.2), kind=kLoop, calls=%fused_computation | loop fusion | flops 393216 | bytes 1048576 | tf_op jit(solution)/shard_map/convert_element_type | solution.py:562
  (18 shorter events, 0.0 us)
Async XLA Ops:
  5.5 17.1 %all-to-all-start = ((bf16[16,48,128]{2,1,0:T(8,128)(2,1)}), bf16[16,48,128]{2,1,0:T(8,128)(2,1)S(1)}, u32[]{:S(2)}, u32[]{:S(2)}) async-start(bf16[16,48,128]{2,1,0:T(8,128)(2,1)} %get-tuple-element.11), calls=%async_computation | async-start | bytes 393216 | tf_op jit(solution)/shard_map/all_to_all | solution.py:484
  15.0 36.7 %collective-permute-start = (bf16[8,256,128]{2,1,0:T(8,128)(2,1)}, bf16[8,256,128]{2,1,0:T(8,128)(2,1)S(1)}, u32[]{:S(2)}, u32[]{:S(2)}) collective-permute-start(bf16[8,256,128]{2,1,0:T(8,128)(2,1)} %get-tuple-element.13.joined.own), channel_id=1, source_target_pairs={{0,2},{4,6},{8,10},{12,14},{16,18},{20,22},{24,26},{28,30},{32,34}... | collective-permute-start | bytes 1572872 | tf_op jit(solution)/shard_map/ppermute | solution.py:489
  18.3 33.5 %collective-permute-start.1 = (bf16[8,256,128]{2,1,0:T(8,128)(2,1)}, bf16[8,256,128]{2,1,0:T(8,128)(2,1)}, u32[]{:S(2)}, u32[]{:S(2)}) collective-permute-start(bf16[8,256,128]{2,1,0:T(8,128)(2,1)} %get-tuple-element.13.joined.own), channel_id=1, source_target_pairs={{2,4},{6,8},{10,12},{14,16},{18,20},{22,24},{26,28},{30,32},{34,36... | collective-permute-start | bytes 1572872 | tf_op jit(solution)/shard_map/ppermute | solution.py:489
  23.2 23.6 %all-to-all-start.1 = ((bf16[16,16,128]{2,1,0:T(8,128)(2,1)}), bf16[16,16,128]{2,1,0:T(8,128)(2,1)S(1)}, u32[]{:S(2)}, u32[]{:S(2)}) async-start(bf16[16,16,128]{2,1,0:T(8,128)(2,1)} %shard_map.141.after), calls=%async_computation.1 | async-start | bytes 131072 | tf_op jit(solution)/shard_map/all_to_all | solution.py:494
  35.0 11.8 %copy-start.4 = (bf16[16,128,64]{1,2,0:T(8,128)(2,1)S(1)}, bf16[16,128,64]{1,2,0:T(8,128)(2,1)}, u32[]{:S(2)}) copy-start(bf16[16,128,64]{1,2,0:T(8,128)(2,1)} %param.25) | copy-start | bytes 786436
  46.8 5.0 %copy-start.6 = (bf16[8,256,128]{2,1,0:T(8,128)(2,1)S(1)}, bf16[8,256,128]{2,1,0:T(8,128)(2,1)}, u32[]{:S(2)}) copy-start(bf16[8,256,128]{2,1,0:T(8,128)(2,1)} %get-tuple-element.13.joined.own) | copy-start | bytes 1572868
  48.0 3.8 %copy-start.7 = (s32[8,12]{1,0:T(8,128)S(1)}, s32[8,12]{1,0:T(8,128)}, u32[]{:S(2)}) copy-start(s32[8,12]{1,0:T(8,128)} %ids.1) | copy-start | bytes 1156
  48.0 3.8 %copy-start.8 = (s32[8,12]{1,0:T(8,128)S(1)}, s32[8,12]{1,0:T(8,128)}, u32[]{:S(2)}) copy-start(s32[8,12]{1,0:T(8,128)} %valid.1) | copy-start | bytes 1156
  48.0 14.8 %all-to-all-start.2 = ((bf16[16,48,128]{2,1,0:T(8,128)(2,1)}), bf16[16,48,128]{2,1,0:T(8,128)(2,1)S(1)}, u32[]{:S(2)}, u32[]{:S(2)}) async-start(bf16[16,48,128]{2,1,0:T(8,128)(2,1)} %shard_map.142.after), calls=%async_computation.2 | async-start | bytes 393216 | tf_op jit(solution)/shard_map/all_to_all | solution.py:524
  51.7 11.1 %copy-start = (bf16[7,256,128]{2,1,0:T(8,128)(2,1)S(1)}, bf16[7,256,128]{2,1,0:T(8,128)(2,1)}, u32[]{:S(2)}) copy-start(bf16[7,256,128]{2,1,0:T(8,128)(2,1)} %transfer.3) | copy-start | bytes 1376260
  51.7 11.1 %copy-start.1 = (f32[14,128,128]{2,1,0:T(8,128)S(1)}, f32[14,128,128]{2,1,0:T(8,128)}, u32[]{:S(2)}) copy-start(f32[14,128,128]{2,1,0:T(8,128)} %get-tuple-element.15.couplings) | copy-start | bytes 2752516
  51.7 11.1 %copy-start.2 = (bf16[8,256,128]{2,1,0:T(8,128)(2,1)S(1)}, bf16[8,256,128]{2,1,0:T(8,128)(2,1)}, u32[]{:S(2)}) copy-start(bf16[8,256,128]{2,1,0:T(8,128)(2,1)} %get-tuple-element.16.both) | copy-start | bytes 1572868
  51.7 11.1 %copy-start.5 = (bf16[5,128,128]{2,1,0:T(8,128)(2,1)S(1)}, bf16[5,128,128]{2,1,0:T(8,128)(2,1)}, u32[]{:S(2)}) copy-start(bf16[5,128,128]{2,1,0:T(8,128)(2,1)} %get-tuple-element.14.chain_k) | copy-start | bytes 491524
  62.0 0.8 %copy-start.9 = (f32[8,64,256]{2,1,0:T(8,128)}, f32[8,64,256]{2,1,0:T(8,128)S(1)}, u32[]{:S(2)}) copy-start(f32[8,64,256]{2,1,0:T(8,128)S(1)} %shard_map.145.near) | copy-start | bytes 1572868
  62.9 5.6 %copy-start.3 = (bf16[8,256,128]{2,1,0:T(8,128)(2,1)S(1)}, bf16[8,256,128]{2,1,0:T(8,128)(2,1)}, u32[]{:S(2)}) copy-start(bf16[8,256,128]{2,1,0:T(8,128)(2,1)} %basis.3) | copy-start | bytes 1572868
  62.9 5.6 %copy-start.10 = (f32[8,64,256]{2,1,0:T(8,128)S(1)}, f32[8,64,256]{2,1,0:T(8,128)}, u32[]{:S(2)}) copy-start(f32[8,64,256]{2,1,0:T(8,128)} %copy-done.9) | copy-start | bytes 1572868
  63.9 5.6 %collective-permute-start.2 = (bf16[8,128,128]{2,1,0:T(8,128)(2,1)S(1)}, bf16[8,128,128]{2,1,0:T(8,128)(2,1)S(1)}, u32[]{:S(2)}, u32[]{:S(2)}) collective-permute-start(bf16[8,128,128]{2,1,0:T(8,128)(2,1)S(1)} %get-tuple-element.19), channel_id=1, source_target_pairs={{0,1},{1,0},{2,3},{3,2},{4,5},{5,4},{6,7},{7,6},{8,9},{9,8},{10,11... | collective-permute-start | bytes 786440 | tf_op jit(solution)/shard_map/ppermute | solution.py:554
